TPU v7x, 32 devices: a whole 2x2x4 slice. The times are simulated.
32 devices in a mesh: mode: 16 (over z, y, x), col: 2 (over core).
Axes of the slice: x: 2, y: 2, z: 4, core: 2. Of those that a mesh axis runs over, the one named last changes fastest.
Arguments:
- tensor: float32 [512, 4, 4096], P('mode', 'col'), may hold values from -12 to 12, as said below
- initial: float32 [512, 128], replicated, may hold values from -6 to 6
Outputs:
- core_tensor: float32 [128, 4, 4096], P(None, 'col', 'mode')
- basis: float32 [512, 128], replicated
- triangle: float32 [512, 512], replicated
Inputs may be any that keep to these rules, and one draw needn't show every extreme that they name: `tensor`: a float field of order one.
All inputs are finite; a program needn't handle non-finite values.
Results may differ from a plain program's by a relative error of at most 0.0003.
Values sent between devices are 32-bit elements; how exact they have to be, the bound alone decides.
No kernel may reach another device: no remote copies, remote signals or barrier semaphores. Data moves between devices by JAX's collectives and lax.ppermute only.
A program may use at most 128 MiB of HBM per device.

v0:
```python
import jax
import jax.numpy as jnp
from jax import lax
from jax.sharding import PartitionSpec as P

ITERS = 3


precise = lax.Precision.HIGHEST


def swapped(value, axis, bit):
    mask = 2**bit
    pairs = [(source, source ^ mask) for source in range(lax.axis_size(axis))]
    return lax.ppermute(value, axis, pairs)


def gram_of(left_side, right_side):
    return jnp.dot(left_side.T, right_side, precision=precise, preferred_element_type=jnp.float32)


def local(tensor, initial):
    regrouped = lax.all_to_all(tensor, "mode", split_axis=2, concat_axis=0, tiled=True)
    row_count, slab_count, cell_count = regrouped.shape
    unfold = regrouped.reshape(row_count, slab_count * cell_count)
    column_total = slab_count * cell_count * lax.axis_size("mode") * lax.axis_size("col")
    local_gram = (
        jnp.dot(unfold, unfold.T, precision=precise, preferred_element_type=jnp.float32)
        / column_total
    )
    gram_sum = local_gram
    mode_levels = lax.axis_size("mode").bit_length() - 1
    col_levels = lax.axis_size("col").bit_length() - 1
    for level in range(mode_levels):
        partner = swapped(gram_sum, "mode", level)
        gram_sum = gram_sum + partner
    for level in range(col_levels):
        partner = swapped(gram_sum, "col", level)
        gram_sum = gram_sum + partner
    triangle = jnp.linalg.cholesky(gram_sum).T
    current = initial
    for sweep in range(ITERS):
        product = jnp.dot(gram_sum, current, precision=precise, preferred_element_type=jnp.float32)
        inner = gram_of(product, product)
        lower_factor = jnp.linalg.cholesky(inner)
        current = lax.linalg.triangular_solve(
            lower_factor, product, left_side=False, lower=True, transpose_a=True
        )
    core_flat = jnp.dot(current.T, unfold, precision=precise, preferred_element_type=jnp.float32)
    core_tensor = core_flat.reshape(current.shape[1], slab_count, cell_count)
    return (core_tensor, current, triangle)


def solution(mesh):
    return jax.shard_map(
        local,
        mesh=mesh,
        in_specs=(P("mode", "col", None), P()),
        out_specs=(P(None, "col", "mode"), P(), P()),
        check_vma=False,
    )
```

profile of v0, /device:TPU:0, one launch (start us, length us, event | category | flops | bytes accessed | tf_op | source)
XLA Modules:
  0.0 359.2 jit_solution(18378753689138286458)
XLA Ops:
  0.6 6.5 %copy.35 = f32[32,2,4096]{0,1,2:T(2,128)} copy(f32[32,2,4096]{2,1,0:T(2,128)} %param.5) | data formatting | bytes 2097152 | tf_op args[0]
  7.2 5.8 %reshape.62 = f32[16,1,16384]{2,1,0:T(1,128)S(1)} reshape(f32[4096,2,32]{2,1,0:T(2,128)} %bitcast.89) | data formatting | bytes 2097152
  13.0 34.5 %all_to_all.15 = f32[16,1,16384]{2,1,0:T(1,128)S(1)} all-to-all(f32[16,1,16384]{2,1,0:T(1,128)S(1)} %reshape.62), channel_id=1, replica_groups=mesh['mode'=16,'col'=2] {'mode'}, dimensions={0} | all-to-all | bytes 2097152 | tf_op jit(solution)/shard_map/all_to_all | solution.py:23
  47.5 0.5 broadcast.201
  48.0 3.1 reduce.28
  51.1 4.9 %reshape.63 = f32[4096,2,32]{2,1,0:T(2,128)} reshape(f32[16,16384]{1,0:T(8,128)S(1)} %reduce.28) | data formatting | bytes 2097152
  56.0 5.5 %copy.36 = f32[32,2,16,256]{3,1,0,2:T(2,128)S(1)} copy(f32[32,2,16,256]{0,1,3,2:T(2,128)} %bitcast.88) | data formatting | bytes 2097152 | tf_op jit(solution)/shard_map/all_to_all | solution.py:23
  61.5 1.9 convolution_multiply_fusion
  63.4 0.6 collective-permute-start
  64.0 22.2 %collective-permute-done = f32[512,512]{0,1:T(8,128)S(1)} collective-permute-done((f32[512,512]{0,1:T(8,128)S(1)}, f32[512,512]{0,1:T(8,128)S(1)}, u32[]{:S(2)}, u32[]{:S(2)}) %collective-permute-start) | collective-permute-done | bytes 1048608 | tf_op jit(solution)/shard_map/ppermute | solution.py:15
  86.4 1.3 collective-permute-start.1
  87.8 20.6 %collective-permute-done.1 = f32[512,512]{0,1:T(8,128)S(1)} collective-permute-done((f32[512,512]{0,1:T(8,128)S(1)}, f32[512,512]{0,1:T(8,128)S(1)}, u32[]{:S(2)}, u32[]{:S(2)}) %collective-permute-start.1) | collective-permute-done | bytes 1048608 | tf_op jit(solution)/shard_map/ppermute | solution.py:15
  108.6 2.7 collective-permute-start.2
  111.3 19.9 %collective-permute-done.2 = f32[512,512]{0,1:T(8,128)S(1)} collective-permute-done((f32[512,512]{0,1:T(8,128)S(1)}, f32[512,512]{0,1:T(8,128)S(1)}, u32[]{:S(2)}, u32[]{:S(2)}) %collective-permute-start.2) | collective-permute-done | bytes 1048608 | tf_op jit(solution)/shard_map/ppermute | solution.py:15
  131.4 6.1 %collective-permute-start.3 = (f32[512,512]{0,1:T(8,128)S(1)}, f32[512,512]{0,1:T(8,128)S(1)}, u32[]{:S(2)}, u32[]{:S(2)}) collective-permute-start(f32[512,512]{0,1:T(8,128)S(1)} %add.63), channel_id=1, source_target_pairs={{0,16},{2,18},{4,20},{6,22},{8,24},{10,26},{12,28},{14,30},{16,0},... | collective-permute-start | bytes 3145736 | tf_op jit(solution)/shard_map/ppermute | solution.py:15
  137.5 40.0 %collective-permute-done.3 = f32[512,512]{0,1:T(8,128)S(1)} collective-permute-done((f32[512,512]{0,1:T(8,128)S(1)}, f32[512,512]{0,1:T(8,128)S(1)}, u32[]{:S(2)}, u32[]{:S(2)}) %collective-permute-start.3) | collective-permute-done | bytes 1048608 | tf_op jit(solution)/shard_map/ppermute | solution.py:15
  177.8 0.3 copy.41
  178.1 2.4 collective-permute-done.4
  180.6 1.4 add.65
  182.0 0.3 copy.42
  182.4 1.8 fusion.47
  184.2 0.7 copy-done.3
  184.9 0.6 fusion.48
  185.6 0.6 fusion.28
  186.2 12.5 %cholesky.325 = f32[128,128]{1,0:T(8,128)S(1)} custom-call(f32[128,128]{1,0:T(8,128)} %fusion.28), custom_call_target="Cholesky" | custom-call | tf_op jit(solution)/shard_map/jit(cholesky)/cholesky | solution.py:45
  198.8 0.6 compare_reduce_fusion.2
  199.4 0.7 fusion.11
  200.1 10.2 %custom-call.37 = f32[1,128,128]{1,2,0:T(8,128)S(1)} custom-call(f32[1,128,128]{2,1,0:T(8,128)S(1)} %fusion.11), custom_call_target="InvertDiagBlocksLowerTriangular" | custom-call | tf_op jit(solution)/shard_map/triangular_solve/custom-call.8 | solution.py:46
  210.3 1.4 convolution_bitcast_fusion.1
  211.7 1.8 fusion.49
  213.5 0.7 copy-done.1
  214.2 0.6 fusion.50
  214.9 0.6 fusion.26
  215.5 12.5 %cholesky.336 = f32[128,128]{1,0:T(8,128)S(1)} custom-call(f32[128,128]{1,0:T(8,128)} %fusion.26), custom_call_target="Cholesky" | custom-call | tf_op jit(solution)/shard_map/jit(cholesky)/cholesky | solution.py:45
  228.1 0.6 compare_reduce_fusion.1
  228.8 0.7 fusion.12
  229.4 9.8 %custom-call.38 = f32[1,128,128]{1,2,0:T(8,128)S(1)} custom-call(f32[1,128,128]{2,1,0:T(8,128)S(1)} %fusion.12), custom_call_target="InvertDiagBlocksLowerTriangular" | custom-call | tf_op jit(solution)/shard_map/triangular_solve/custom-call.8 | solution.py:46
  239.3 1.4 convolution_bitcast_fusion
  240.6 1.8 fusion.51
  242.5 0.7 copy-done.2
  243.2 0.6 fusion.52
  243.8 0.6 fusion.24
  244.5 12.7 %cholesky.347 = f32[128,128]{1,0:T(8,128)S(1)} custom-call(f32[128,128]{1,0:T(8,128)} %fusion.24), custom_call_target="Cholesky" | custom-call | tf_op jit(solution)/shard_map/jit(cholesky)/cholesky | solution.py:45
  257.2 0.6 compare_reduce_fusion
  257.9 0.7 fusion.13
  258.5 9.8 %custom-call.39 = f32[1,128,128]{1,2,0:T(8,128)S(1)} custom-call(f32[1,128,128]{2,1,0:T(8,128)S(1)} %fusion.13), custom_call_target="InvertDiagBlocksLowerTriangular" | custom-call | tf_op jit(solution)/shard_map/triangular_solve/custom-call.8 | solution.py:46
  268.3 1.4 fusion.22
  269.7 1.2 fusion.3
  270.9 0.9 copy.43
  271.8 1.8 copy.44
  273.9 11.7 %cholesky.131 = f32[128,128]{1,0:T(8,128)S(1)} custom-call(f32[128,128]{1,0:T(8,128)S(1)} %cholesky.356), custom_call_target="Cholesky" | custom-call | tf_op jit(solution)/shard_map/jit(cholesky)/cholesky | solution.py:40
  285.7 10.0 %custom-call.32 = f32[1,128,128]{1,2,0:T(8,128)S(1)} custom-call(f32[1,128,128]{2,1,0:T(8,128)S(1)} %get-tuple-element.26), custom_call_target="InvertDiagBlocksLowerTriangular" | custom-call | tf_op jit(solution)/shard_map/jit(cholesky)/cholesky | solution.py:40
  296.1 0.3 slice_subtract_fusion
  296.4 11.7 %cholesky.244 = f32[128,128]{1,0:T(8,128)S(1)} custom-call(f32[128,128]{1,0:T(8,128)S(1)} %cholesky.360), custom_call_target="Cholesky" | custom-call | tf_op jit(solution)/shard_map/jit(cholesky)/cholesky | solution.py:40
  308.2 9.8 %custom-call.33 = f32[1,128,128]{1,2,0:T(8,128)S(1)} custom-call(f32[1,128,128]{2,1,0:T(8,128)S(1)} %get-tuple-element.23), custom_call_target="InvertDiagBlocksLowerTriangular" | custom-call | tf_op jit(solution)/shard_map/jit(cholesky)/cholesky | solution.py:40
  318.3 0.4 slice_subtract_fusion.1
  318.7 11.9 %cholesky.265 = f32[128,128]{1,0:T(8,128)S(1)} custom-call(f32[128,128]{1,0:T(8,128)S(1)} %cholesky.365), custom_call_target="Cholesky" | custom-call | tf_op jit(solution)/shard_map/jit(cholesky)/cholesky | solution.py:40
  330.6 9.8 %custom-call.34 = f32[1,128,128]{1,2,0:T(8,128)S(1)} custom-call(f32[1,128,128]{2,1,0:T(8,128)S(1)} %get-tuple-element.20), custom_call_target="InvertDiagBlocksLowerTriangular" | custom-call | tf_op jit(solution)/shard_map/jit(cholesky)/cholesky | solution.py:40
  340.7 0.4 slice_subtract_fusion.2
  341.1 11.7 %cholesky.282 = f32[128,128]{1,0:T(8,128)S(1)} custom-call(f32[128,128]{1,0:T(8,128)S(1)} %slice_subtract_fusion.2), custom_call_target="Cholesky" | custom-call | tf_op jit(solution)/shard_map/jit(cholesky)/cholesky | solution.py:40
  352.8 0.7 compare_reduce_fusion.4
  353.5 0.6 compare_reduce_fusion.3
  354.1 0.7 compare_reduce_fusion.5
  357.5 1.3 copy.45
  (32 shorter events, 2.8 us)
Async XLA Ops:
  0.6 181.7 %copy-start = (f32[512,128]{1,0:T(8,128)S(1)}, f32[512,128]{1,0:T(8,128)}, u32[]{:S(2)}) copy-start(f32[512,128]{1,0:T(8,128)} %param.6) | copy-start | bytes 786436
  63.4 22.8 %collective-permute-start = (f32[512,512]{0,1:T(8,128)S(1)}, f32[512,512]{0,1:T(8,128)S(1)}, u32[]{:S(2)}, u32[]{:S(2)}) collective-permute-start(f32[512,512]{0,1:T(8,128)S(1)} %convolution_multiply_fusion), channel_id=1, source_target_pairs={{0,2},{2,0},{4,6},{6,4},{8,10},{10,8},{12,14},{14,12},{16,18},{18,... | collective-permute-start | bytes 3145736 | tf_op jit(solution)/shard_map/ppermute | solution.py:15
  86.4 21.9 %collective-permute-start.1 = (f32[512,512]{0,1:T(8,128)S(1)}, f32[512,512]{0,1:T(8,128)S(1)}, u32[]{:S(2)}, u32[]{:S(2)}) collective-permute-start(f32[512,512]{0,1:T(8,128)S(1)} %add.61), channel_id=1, source_target_pairs={{0,4},{2,6},{4,0},{6,2},{8,12},{10,14},{12,8},{14,10},{16,20},{18,... | collective-permute-start | bytes 3145736 | tf_op jit(solution)/shard_map/ppermute | solution.py:15
  108.6 22.6 %collective-permute-start.2 = (f32[512,512]{0,1:T(8,128)S(1)}, f32[512,512]{0,1:T(8,128)S(1)}, u32[]{:S(2)}, u32[]{:S(2)}) collective-permute-start(f32[512,512]{0,1:T(8,128)S(1)} %add.62), channel_id=1, source_target_pairs={{0,8},{2,10},{4,12},{6,14},{8,0},{10,2},{12,4},{14,6},{16,24},{18,... | collective-permute-start | bytes 3145736 | tf_op jit(solution)/shard_map/ppermute | solution.py:15
  131.4 46.1 %collective-permute-start.3 = (f32[512,512]{0,1:T(8,128)S(1)}, f32[512,512]{0,1:T(8,128)S(1)}, u32[]{:S(2)}, u32[]{:S(2)}) collective-permute-start(f32[512,512]{0,1:T(8,128)S(1)} %add.63), channel_id=1, source_target_pairs={{0,16},{2,18},{4,20},{6,22},{8,24},{10,26},{12,28},{14,30},{16,0},... | collective-permute-start | bytes 3145736 | tf_op jit(solution)/shard_map/ppermute | solution.py:15
  177.7 2.9 collective-permute-start.4
  184.2 0.7 copy-start.3
  213.5 0.7 copy-start.1
  242.4 0.7 copy-start.2
  269.7 1.2 copy-start.4
where the time goes:
time: 366 us; the launch traced here: 359 us
  other arithmetic  158 us (43%)
  waiting for transfers between devices  105 us (29%)
  blocking collectives  34.5 us (9%)
  local copies, waits for them, and re-layouts  30.4 us (8%)
  matrix products  16.2 us (4%)
  starting transfers between devices  10.9 us (3%)
  between operations  4.02 us (1%)
    ppermute x5, waiting for transfers between devices, swapped(): return lax.ppermute(value, axis, pairs)  105 us
    another operation x14, other arithmetic, local(): triangle = jnp.linalg.cholesky(gram_sum).T  78.9 us
    another operation x9, other arithmetic, local(): lower_factor = jnp.linalg.cholesky(inner)  39.8 us
    all_to_all x1, blocking collectives, local(): lax.all_to_all(tensor, 'mode', split_axis=2, concat_axis=0, tiled=True)  34.5 us
    another operation x6, other arithmetic, local(): lax.linalg.triangular_solve(lower_factor, product, left_side=False, lower...  31.8 us
    unnamed x17, local copies, waits for them, and re-layouts  23.4 us
    ppermute x5, starting transfers between devices, swapped(): return lax.ppermute(value, axis, pairs)  10.9 us
  transfers between devices with their start and end apart: 5, of which 5 were waited for; matrix products, arithmetic and copies ran while one was open for 0% of the time, Pallas kernels for 0%

commit v1 on v0

v1 whole, which is shorter than its diff:
```python
import jax
import jax.numpy as jnp
from jax import lax
from jax.sharding import PartitionSpec as P

ITERS = 3
TILE = 128

precise = lax.Precision.HIGHEST


def matmul(left, right):
    return jnp.dot(left, right, precision=precise, preferred_element_type=jnp.float32)


def exchanged(value, axis, distance):
    pairs = [(source, source ^ distance) for source in range(lax.axis_size(axis))]
    return lax.ppermute(value, axis, pairs)


def scattered_sum(value, axis, group):
    place = lax.axis_index(axis) % group
    rows = value.shape[0] // group
    total = lax.dynamic_slice_in_dim(value, place * rows, rows)
    parts = [
        exchanged(lax.dynamic_slice_in_dim(value, (place ^ distance) * rows, rows), axis, distance)
        for distance in range(1, group)
    ]
    for part in parts:
        total = total + part
    return total


def gathered(value, axis, group):
    place = lax.axis_index(axis) % group
    rows = value.shape[0]
    whole = jnp.zeros((group * rows,) + value.shape[1:], value.dtype)
    whole = lax.dynamic_update_slice_in_dim(whole, value, place * rows, 0)
    for distance in range(1, group):
        part = exchanged(value, axis, distance)
        whole = lax.dynamic_update_slice_in_dim(whole, part, (place ^ distance) * rows, 0)
    return whole


def summed(value):
    mode_size, col_size = lax.axis_size("mode"), lax.axis_size("col")
    col_group = min(2, col_size)
    mode_group = min(4, mode_size)
    value = scattered_sum(value, "col", col_group)
    value = scattered_sum(value, "mode", mode_group)
    distance = mode_group
    while distance < mode_size:
        value = value + exchanged(value, "mode", distance)
        distance *= 2
    distance = col_group
    while distance < col_size:
        value = value + exchanged(value, "col", distance)
        distance *= 2
    value = gathered(value, "mode", mode_group)
    return gathered(value, "col", col_group)


def local(tensor, initial):
    mode_size = lax.axis_size("mode")
    row_part, slab_count, width = tensor.shape
    cell_count = width // mode_size
    row_count = row_part * mode_size
    column_total = slab_count * width * lax.axis_size("col")
    blocks = tensor.reshape(row_part, slab_count, mode_size, cell_count).transpose(2, 0, 1, 3)
    blocks = blocks.reshape(mode_size, row_part, slab_count * cell_count)
    regrouped = lax.all_to_all(blocks, "mode", split_axis=0, concat_axis=0, tiled=True)
    unfold = regrouped.reshape(row_count, slab_count * cell_count)
    local_gram = matmul(unfold, unfold.T) / column_total
    tiles = row_count // TILE
    packed = jnp.concatenate(
        [
            local_gram[i * TILE : (i + 1) * TILE, j * TILE : (j + 1) * TILE]
            for i in range(tiles)
            for j in range(i, tiles)
        ]
    )
    packed = summed(packed)
    found = {}
    for i in range(tiles):
        for j in range(i, tiles):
            start = len(found) * TILE
            found[i, j] = packed[start : start + TILE]
    gram_sum = jnp.concatenate(
        [
            jnp.concatenate([found[i, j] if i <= j else found[j, i].T for j in range(tiles)], 1)
            for i in range(tiles)
        ]
    )
    triangle = jnp.linalg.cholesky(gram_sum).T
    current = initial
    for sweep in range(ITERS):
        product = matmul(gram_sum, current)
        inner = matmul(product.T, product)
        lower_factor = jnp.linalg.cholesky(inner)
        current = lax.linalg.triangular_solve(
            lower_factor, product, left_side=False, lower=True, transpose_a=True
        )
    core_flat = matmul(current.T, unfold)
    core_tensor = core_flat.reshape(current.shape[1], slab_count, cell_count)
    return (core_tensor, current, triangle)


def solution(mesh):
    return jax.shard_map(
        local,
        mesh=mesh,
        in_specs=(P("mode", "col", None), P()),
        out_specs=(P(None, "col", "mode"), P(), P()),
        check_vma=False,
    )
```

time: 366 us -> 266 us (0.73)
  waiting for transfers between devices: 105 us -> 46.7 us
  blocking collectives: 34.5 us -> 0 us
  local copies, waits for them, and re-layouts: 30.4 us -> 19.6 us
  starting transfers between devices: 10.9 us -> 19.6 us
    ppermute x5 -> x10, waiting for transfers between devices: 105 us -> 22.3 us  [exchanged(): return lax.ppermute(value, axis, pairs)]
    all_to_all x1 -> x0, blocking collectives: 34.5 us -> none  [local(): lax.all_to_all(tensor, 'mode', split_axis=2, concat_axis=0, tiled=True)]
    all_to_all x0 -> x1, waiting for transfers between devices: none -> 24.4 us  [local(): lax.all_to_all(blocks, 'mode', split_axis=0, concat_axis=0, tiled=True)]
    unnamed x17 -> x48, local copies, waits for them, and re-layouts: 23.4 us -> 8.08 us
    all_to_all x0 -> x1, starting transfers between devices: none -> 8.31 us  [local(): lax.all_to_all(blocks, 'mode', split_axis=0, concat_axis=0, tiled=True)]
    all_to_all x2 -> x0, local copies, waits for them, and re-layouts: 5.96 us -> none  [local(): lax.all_to_all(tensor, 'mode', split_axis=2, concat_axis=0, tiled=True)]
    dynamic_update_slice x0 -> x6, local copies, waits for them, and re-layouts: none -> 4.78 us  [the longest x4 3.67 us: gathered(): lax.dynamic_update_slice_in_dim(whole, part, (place ^ distance) * rows, 0)]
    ppermute x5 -> x10, starting transfers between devices: 10.9 us -> 11.3 us  [exchanged(): return lax.ppermute(value, axis, pairs)]
  transfers between devices with their start and end apart: 5 -> 11, of which waited for: 5 -> 10; matrix products, arithmetic and copies ran while one was open for 0% -> 1% of each run, Pallas kernels for 0% -> 0%
where the time goes in v1:
time: 266 us; the launch traced here: 260 us
  other arithmetic  155 us (58%)
  waiting for transfers between devices  46.7 us (18%)
  local copies, waits for them, and re-layouts  19.6 us (7%)
  starting transfers between devices  19.6 us (7%)
  matrix products  15.7 us (6%)
  between operations  4.19 us (2%)
    another operation x14, other arithmetic, local(): triangle = jnp.linalg.cholesky(gram_sum).T  80.3 us
    another operation x9, other arithmetic, local(): lower_factor = jnp.linalg.cholesky(inner)  38.8 us
    another operation x6, other arithmetic, local(): lax.linalg.triangular_solve(lower_factor, product, left_side=False, lower...  31.5 us
    all_to_all x1, waiting for transfers between devices, local(): lax.all_to_all(blocks, 'mode', split_axis=0, concat_axis=0, tiled=True)  24.4 us
    ppermute x10, waiting for transfers between devices, exchanged(): return lax.ppermute(value, axis, pairs)  22.3 us
    ppermute x10, starting transfers between devices, exchanged(): return lax.ppermute(value, axis, pairs)  11.3 us
    dot_general x8, matrix products, matmul(): jnp.dot(left, right, precision=precise, preferred_element_type=jnp.float32)  10.5 us
    all_to_all x1, starting transfers between devices, local(): lax.all_to_all(blocks, 'mode', split_axis=0, concat_axis=0, tiled=True)  8.31 us
  transfers between devices with their start and end apart: 11, of which 10 were waited for; matrix products, arithmetic and copies ran while one was open for 1% of the time, Pallas kernels for 0%

profile of v1, /device:TPU:0, one launch (start us, length us, event | category | flops | bytes accessed | tf_op | source)
XLA Modules:
  0.0 260.3 jit_solution(8308159838326092653)
XLA Ops:
  0.6 1.8 copy.43
  2.5 1.8 reshape.56
  4.3 8.3 %all-to-all-start = ((f32[16,32,512]{2,1,0:T(8,128)}), f32[16,32,512]{2,1,0:T(8,128)S(1)}, u32[]{:S(2)}, u32[]{:S(2)}) async-start(f32[16,32,512]{2,1,0:T(8,128)} %reshape.56), calls=%async_computation | async-start | bytes 2097152 | tf_op jit(solution)/shard_map/all_to_all | solution.py:71
  12.6 24.4 %all-to-all-done = f32[16,32,512]{2,1,0:T(8,128)S(1)} async-done(((f32[16,32,512]{2,1,0:T(8,128)}), f32[16,32,512]{2,1,0:T(8,128)S(1)}, u32[]{:S(2)}, u32[]{:S(2)}) %all-to-all-start) | async-done | bytes 1048608 | tf_op jit(solution)/shard_map/all_to_all | solution.py:71
  37.0 1.9 convolution_multiply_fusion
  39.2 1.6 collective-permute-done
  41.0 2.0 collective-permute-start.3
  43.1 1.4 collective-permute-start.1
  44.6 3.8 %collective-permute-done.3 = f32[160,128]{0,1:T(8,128)S(1)} collective-permute-done((f32[160,128]{0,1:T(8,128)S(1)}, f32[160,128]{0,1:T(8,128)S(1)}, u32[]{:S(2)}, u32[]{:S(2)}) %collective-permute-start.3) | collective-permute-done | bytes 81952 | tf_op jit(solution)/shard_map/ppermute | solution.py:18
  48.4 2.0 collective-permute-done.2
  51.0 2.5 collective-permute-start.4
  53.6 3.7 %collective-permute-done.4 = f32[160,128]{0,1:T(8,128)S(1)} collective-permute-done((f32[160,128]{0,1:T(8,128)S(1)}, f32[160,128]{0,1:T(8,128)S(1)}, u32[]{:S(2)}, u32[]{:S(2)}) %collective-permute-start.4) | collective-permute-done | bytes 81952 | tf_op jit(solution)/shard_map/ppermute | solution.py:18
  57.3 1.5 collective-permute-start.5
  58.7 7.2 %collective-permute-done.5 = f32[160,128]{0,1:T(8,128)S(1)} collective-permute-done((f32[160,128]{0,1:T(8,128)S(1)}, f32[160,128]{0,1:T(8,128)S(1)}, u32[]{:S(2)}, u32[]{:S(2)}) %collective-permute-start.5) | collective-permute-done | bytes 81952 | tf_op jit(solution)/shard_map/ppermute | solution.py:18
  66.6 1.3 collective-permute-start.7
  67.8 1.7 collective-permute-start.8
  69.5 1.1 dynamic_update_slice.18
  70.6 1.4 collective-permute-done.6
  72.0 1.2 dynamic_update_slice.19
  73.2 1.0 collective-permute-done.7
  74.2 1.0 dynamic_update_slice.20
  75.3 1.4 dynamic_update_slice.21
  77.2 1.2 collective-permute-done.9
  78.7 0.7 copy.26
  79.6 0.7 copy.25
  81.3 0.9 maximum_maximum_fusion
  82.5 1.3 fusion
  83.9 1.0 copy-done.5
  84.9 11.7 %cholesky.131 = f32[128,128]{1,0:T(8,128)S(1)} custom-call(f32[128,128]{1,0:T(8,128)S(1)} %cholesky.356), custom_call_target="Cholesky" | custom-call | tf_op jit(solution)/shard_map/jit(cholesky)/cholesky | solution.py:94
  96.7 0.6 fusion.38
  97.3 1.8 fusion.43
  99.2 0.7 copy-done.4
  100.6 0.6 fusion.23
  101.2 12.5 %cholesky.325 = f32[128,128]{1,0:T(8,128)S(1)} custom-call(f32[128,128]{1,0:T(8,128)} %fusion.23), custom_call_target="Cholesky" | custom-call | tf_op jit(solution)/shard_map/jit(cholesky)/cholesky | solution.py:99
  113.8 0.6 compare_reduce_fusion.2
  114.4 0.7 fusion.9
  115.1 9.9 %custom-call.37 = f32[1,128,128]{1,2,0:T(8,128)S(1)} custom-call(f32[1,128,128]{2,1,0:T(8,128)S(1)} %fusion.9), custom_call_target="InvertDiagBlocksLowerTriangular" | custom-call | tf_op jit(solution)/shard_map/triangular_solve/custom-call.8 | solution.py:100
  125.0 1.4 convolution_bitcast_fusion.1
  126.4 1.8 fusion.45
  128.3 0.7 copy-done.3
  129.6 0.6 fusion.21
  130.3 12.5 %cholesky.336 = f32[128,128]{1,0:T(8,128)S(1)} custom-call(f32[128,128]{1,0:T(8,128)} %fusion.21), custom_call_target="Cholesky" | custom-call | tf_op jit(solution)/shard_map/jit(cholesky)/cholesky | solution.py:99
  142.9 0.6 compare_reduce_fusion.1
  143.5 0.7 fusion.10
  144.2 9.8 %custom-call.38 = f32[1,128,128]{1,2,0:T(8,128)S(1)} custom-call(f32[1,128,128]{2,1,0:T(8,128)S(1)} %fusion.10), custom_call_target="InvertDiagBlocksLowerTriangular" | custom-call | tf_op jit(solution)/shard_map/triangular_solve/custom-call.8 | solution.py:100
  154.0 1.4 convolution_bitcast_fusion
  155.4 2.0 fusion.47
  157.4 0.7 copy-done.1
  158.8 11.7 %cholesky.347 = f32[128,128]{1,0:T(8,128)S(1)} custom-call(f32[128,128]{1,0:T(8,128)S(1)} %fusion.19), custom_call_target="Cholesky" | custom-call | tf_op jit(solution)/shard_map/jit(cholesky)/cholesky | solution.py:99
  170.6 0.6 compare_reduce_fusion
  171.2 0.7 fusion.11
  171.9 9.8 %custom-call.39 = f32[1,128,128]{1,2,0:T(8,128)S(1)} custom-call(f32[1,128,128]{2,1,0:T(8,128)S(1)} %fusion.11), custom_call_target="InvertDiagBlocksLowerTriangular" | custom-call | tf_op jit(solution)/shard_map/triangular_solve/custom-call.8 | solution.py:100
  182.2 1.2 fusion.2
  183.4 0.9 copy.34
  184.3 1.8 copy.35
  186.1 10.6 %custom-call.32 = f32[1,128,128]{1,2,0:T(8,128)S(1)} custom-call(f32[1,128,128]{2,1,0:T(8,128)} %get-tuple-element.37), custom_call_target="InvertDiagBlocksLowerTriangular" | custom-call | tf_op jit(solution)/shard_map/jit(cholesky)/cholesky | solution.py:94
  197.4 12.1 %cholesky.244 = f32[128,128]{1,0:T(8,128)S(1)} custom-call(f32[128,128]{1,0:T(8,128)S(1)} %cholesky.360), custom_call_target="Cholesky" | custom-call | tf_op jit(solution)/shard_map/jit(cholesky)/cholesky | solution.py:94
  209.5 9.8 %custom-call.33 = f32[1,128,128]{1,2,0:T(8,128)S(1)} custom-call(f32[1,128,128]{2,1,0:T(8,128)S(1)} %get-tuple-element.34), custom_call_target="InvertDiagBlocksLowerTriangular" | custom-call | tf_op jit(solution)/shard_map/jit(cholesky)/cholesky | solution.py:94
  220.0 11.7 %cholesky.265 = f32[128,128]{1,0:T(8,128)S(1)} custom-call(f32[128,128]{1,0:T(8,128)S(1)} %cholesky.365), custom_call_target="Cholesky" | custom-call | tf_op jit(solution)/shard_map/jit(cholesky)/cholesky | solution.py:94
  231.8 9.8 %custom-call.34 = f32[1,128,128]{1,2,0:T(8,128)S(1)} custom-call(f32[1,128,128]{2,1,0:T(8,128)S(1)} %get-tuple-element.31), custom_call_target="InvertDiagBlocksLowerTriangular" | custom-call | tf_op jit(solution)/shard_map/jit(cholesky)/cholesky | solution.py:94
  242.3 11.7 %cholesky.282 = f32[128,128]{1,0:T(8,128)S(1)} custom-call(f32[128,128]{1,0:T(8,128)S(1)} %convolution_subtract_fusion.2), custom_call_target="Cholesky" | custom-call | tf_op jit(solution)/shard_map/jit(cholesky)/cholesky | solution.py:94
  254.1 0.7 compare_reduce_fusion.4
  255.4 0.7 compare_reduce_fusion.5
  258.8 1.3 copy.36
  (90 shorter events, 9.6 us)
Async XLA Ops:
  0.6 96.7 %copy-start = (f32[512,128]{1,0:T(8,128)S(1)}, f32[512,128]{1,0:T(8,128)}, u32[]{:S(2)}) copy-start(f32[512,128]{1,0:T(8,128)} %param.6) | copy-start | bytes 786436
  4.3 32.8 %all-to-all-start = ((f32[16,32,512]{2,1,0:T(8,128)}), f32[16,32,512]{2,1,0:T(8,128)S(1)}, u32[]{:S(2)}, u32[]{:S(2)}) async-start(f32[16,32,512]{2,1,0:T(8,128)} %reshape.56), calls=%async_computation | async-start | bytes 2097152 | tf_op jit(solution)/shard_map/all_to_all | solution.py:71
  39.1 1.7 collective-permute-start
  41.0 7.3 %collective-permute-start.3 = (f32[160,128]{0,1:T(8,128)S(1)}, f32[160,128]{0,1:T(8,128)S(1)}, u32[]{:S(2)}, u32[]{:S(2)}) collective-permute-start(f32[160,128]{0,1:T(8,128)S(1)} %get-tuple-element.26), channel_id=1, source_target_pairs={{0,6},{2,4},{4,2},{6,0},{8,14},{10,12},{12,10},{14,8},{16,22},{18,... | collective-permute-start | bytes 245768 | tf_op jit(solution)/shard_map/ppermute | solution.py:18
  43.1 7.3 %collective-permute-start.2 = (f32[160,128]{0,1:T(8,128)S(1)}, f32[160,128]{0,1:T(8,128)S(1)}, u32[]{:S(2)}, u32[]{:S(2)}) collective-permute-start(f32[160,128]{0,1:T(8,128)S(1)} %get-tuple-element.27), channel_id=1, source_target_pairs={{0,4},{2,6},{4,0},{6,2},{8,12},{10,14},{12,8},{14,10},{16,20},{18,... | collective-permute-start | bytes 245768 | tf_op jit(solution)/shard_map/ppermute | solution.py:18
  43.1 7.8 %collective-permute-start.1 = (f32[160,128]{0,1:T(8,128)S(1)}, f32[160,128]{0,1:T(8,128)S(1)}, u32[]{:S(2)}, u32[]{:S(2)}) collective-permute-start(f32[160,128]{0,1:T(8,128)S(1)} %get-tuple-element.25), channel_id=1, source_target_pairs={{0,2},{2,0},{4,6},{6,4},{8,10},{10,8},{12,14},{14,12},{16,18},{18,... | collective-permute-start | bytes 245768 | tf_op jit(solution)/shard_map/ppermute | solution.py:18
  51.0 6.2 %collective-permute-start.4 = (f32[160,128]{0,1:T(8,128)S(1)}, f32[160,128]{0,1:T(8,128)S(1)}, u32[]{:S(2)}, u32[]{:S(2)}) collective-permute-start(f32[160,128]{0,1:T(8,128)S(1)} %add_add_fusion), channel_id=1, source_target_pairs={{0,8},{2,10},{4,12},{6,14},{8,0},{10,2},{12,4},{14,6},{16,24},{18,... | collective-permute-start | bytes 245768 | tf_op jit(solution)/shard_map/ppermute | solution.py:18
  57.3 8.7 %collective-permute-start.5 = (f32[160,128]{0,1:T(8,128)S(1)}, f32[160,128]{0,1:T(8,128)S(1)}, u32[]{:S(2)}, u32[]{:S(2)}) collective-permute-start(f32[160,128]{0,1:T(8,128)S(1)} %add.109), channel_id=1, source_target_pairs={{0,16},{2,18},{4,20},{6,22},{8,24},{10,26},{12,28},{14,30},{16,0},... | collective-permute-start | bytes 245768 | tf_op jit(solution)/shard_map/ppermute | solution.py:18
  65.9 6.0 %collective-permute-start.6 = (f32[160,128]{0,1:T(8,128)S(1)}, f32[160,128]{0,1:T(8,128)S(1)}, u32[]{:S(2)}, u32[]{:S(2)}) collective-permute-start(f32[160,128]{0,1:T(8,128)S(1)} %add.110), channel_id=1, source_target_pairs={{0,2},{2,0},{4,6},{6,4},{8,10},{10,8},{12,14},{14,12},{16,18},{18,... | collective-permute-start | bytes 245768 | tf_op jit(solution)/shard_map/ppermute | solution.py:18
  66.6 7.6 %collective-permute-start.7 = (f32[160,128]{0,1:T(8,128)S(1)}, f32[160,128]{0,1:T(8,128)S(1)}, u32[]{:S(2)}, u32[]{:S(2)}) collective-permute-start(f32[160,128]{0,1:T(8,128)S(1)} %add.110), channel_id=1, source_target_pairs={{0,4},{2,6},{4,0},{6,2},{8,12},{10,14},{12,8},{14,10},{16,20},{18,... | collective-permute-start | bytes 245768 | tf_op jit(solution)/shard_map/ppermute | solution.py:18
  67.8 7.4 %collective-permute-start.8 = (f32[160,128]{0,1:T(8,128)S(1)}, f32[160,128]{0,1:T(8,128)S(1)}, u32[]{:S(2)}, u32[]{:S(2)}) collective-permute-start(f32[160,128]{0,1:T(8,128)S(1)} %add.110), channel_id=1, source_target_pairs={{0,6},{2,4},{4,2},{6,0},{8,14},{10,12},{12,10},{14,8},{16,22},{18,... | collective-permute-start | bytes 245768 | tf_op jit(solution)/shard_map/ppermute | solution.py:18
  76.6 1.7 collective-permute-start.9
  78.5 2.1 copy-start.9
  78.5 2.1 copy-start.10
  78.5 2.1 copy-start.11
  78.5 2.1 copy-start.12
  78.5 2.1 copy-start.13
  78.5 2.1 copy-start.14
  78.5 2.1 copy-start.15
  78.6 2.0 copy-start.16
  80.6 0.7 copy-start.8
  83.9 1.0 copy-start.5
  99.2 0.7 copy-start.4
  128.2 0.7 copy-start.3
  157.4 0.7 copy-start.1
  158.7 23.0 %copy-start.2 = (f32[512,128]{1,0:T(8,128)S(1)}, f32[512,128]{1,0:T(8,128)}, u32[]{:S(2)}) copy-start(f32[512,128]{1,0:T(8,128)} %copy-done.1) | copy-start | bytes 786436
  182.1 1.2 copy-start.7
  182.2 14.6 %copy-start.6 = (f32[512,512]{1,0:T(8,128)S(1)}, f32[512,512]{1,0:T(8,128)}, u32[]{:S(2)}) copy-start(f32[512,512]{1,0:T(8,128)} %copy-done.5) | copy-start | bytes 3145732

commit v2 on v1

--- a/solution.py
+++ b/solution.py
@@ -1,16 +1,34 @@
+import functools
+
 import jax
 import jax.numpy as jnp
 from jax import lax
+from jax.experimental import pallas as pl
+from jax.experimental.pallas import tpu as pltpu
 from jax.sharding import PartitionSpec as P
 
 ITERS = 3
 TILE = 128
+SUB = 8
+PANEL = 2
 
 precise = lax.Precision.HIGHEST
 
 
 def matmul(left, right):
     return jnp.dot(left, right, precision=precise, preferred_element_type=jnp.float32)
+
+
+def matmul_tn(left, right):
+    return lax.dot_general(
+        left, right, (((0,), (0,)), ((), ())), precision=precise, preferred_element_type=jnp.float32
+    )
+
+
+def matmul_nt(left, right):
+    return lax.dot_general(
+        left, right, (((1,), (1,)), ((), ())), precision=precise, preferred_element_type=jnp.float32
+    )
 
 
 def exchanged(value, axis, distance):
@@ -60,6 +78,162 @@
     return gathered(value, "col", col_group)
 
 
+def row_of(tile, index):
+    return jnp.broadcast_to(tile[index : index + 1, :], tile.shape)
+
+
+def lane_of(tile, index):
+    return jnp.take_along_axis(tile, jnp.full(tile.shape, index, jnp.int32), axis=1)
+
+
+def factored(block, with_upper):
+    side = block.shape[0]
+    count = side // SUB
+    width = PANEL * SUB
+    row = lax.broadcasted_iota(jnp.int32, (SUB, side), 0)
+    lane = lax.broadcasted_iota(jnp.int32, (SUB, side), 1)
+    tiles = [block[SUB * t : SUB * t + SUB, :] for t in range(count)]
+    scales = [None] * count
+    for first in range(0, count, PANEL):
+        base = first * SUB
+        inside = (lane >= base) & (lane < base + width)
+        members = range(PANEL)
+        columns = [[lane_of(tiles[first + h], base + j) for h in members] for j in range(width)]
+        below = {
+            t: [lane_of(tiles[t], base + j) for j in range(width)] for t in range(first + PANEL, count)
+        }
+        upper = [tiles[first + h] for h in members]
+        inverse = [
+            jnp.where(inside, jnp.where(lane == row + base + SUB * h, 1.0, 0.0), upper[h]) for h in members
+        ]
+        kept_upper, kept_inverse, scale = list(upper), list(inverse), [None] * PANEL
+        for pivot in range(width):
+            own, place = divmod(pivot, SUB)
+            reciprocal = pl.reciprocal(row_of(columns[pivot][own], place), approx=True)
+            first_row = place == 0
+            here = row == place
+            scale[own] = reciprocal if first_row else jnp.where(here, reciprocal, scale[own])
+            kept_inverse[own] = inverse[own] if first_row else jnp.where(here, inverse[own], kept_inverse[own])
+            if with_upper:
+                kept_upper[own] = upper[own] if first_row else jnp.where(here, upper[own], kept_upper[own])
+            factor = [
+                (jnp.where(here, 0.0, columns[pivot][h]) if h == own else columns[pivot][h]) * reciprocal
+                for h in members
+            ]
+            for j in range(pivot + 1, width):
+                value = row_of(columns[j][own], place)
+                columns[j] = [columns[j][h] - factor[h] * value for h in members]
+            value = row_of(inverse[own], place)
+            inverse = [inverse[h] - factor[h] * value for h in members]
+            if with_upper:
+                value = row_of(upper[own], place)
+                upper = [upper[h] - factor[h] * value for h in members]
+        for h in members:
+            on_or_right = inside & (lane >= row + base + SUB * h)
+            tiles[first + h] = (
+                jnp.where(on_or_right, kept_upper[h], kept_inverse[h]) if with_upper else kept_inverse[h]
+            )
+            scales[first + h] = scale[h]
+        if first + PANEL < count:
+            reduced = [inverse[h] * scale[h] for h in members]
+            rows = [row_of(reduced[m // SUB], m % SUB) for m in range(width)]
+            for t in range(first + PANEL, count):
+                even = jnp.where(inside, 0.0, tiles[t])
+                odd = None
+                for m in range(width):
+                    term = below[t][m] * rows[m]
+                    if m % 2:
+                        odd = term if odd is None else odd + term
+                    else:
+                        even = even - term
+                tiles[t] = even - odd
+    uppers, inverses = [], []
+    for t in range(count):
+        root = lax.rsqrt(scales[t]) * scales[t]
+        scaled = tiles[t] * root
+        diagonal = row + SUB * t
+        uppers.append(jnp.where(lane >= diagonal, scaled, 0.0))
+        inverses.append(jnp.where(lane < diagonal, scaled, jnp.where(lane == diagonal, root, 0.0)))
+    return (jnp.concatenate(uppers) if with_upper else None), jnp.concatenate(inverses)
+
+
+def block_places(tiles):
+    return {
+        pair: place for place, pair in enumerate((i, j) for i in range(tiles) for j in range(i, tiles))
+    }
+
+
+def write_triangle(packed_ref, triangle_ref):
+    tiles = triangle_ref.shape[0] // TILE
+    places = block_places(tiles)
+    blocks = {pair: packed_ref[TILE * at : TILE * at + TILE, :] for pair, at in places.items()}
+    for k in range(tiles):
+        upper, inverse = factored(blocks[k, k], True)
+        for j in range(tiles):
+            if j < k:
+                part = jnp.zeros((TILE, TILE), jnp.float32)
+            elif j == k:
+                part = upper
+            else:
+                part = blocks[k, j] = matmul(inverse, blocks[k, j])
+            triangle_ref[TILE * k : TILE * k + TILE, TILE * j : TILE * j + TILE] = part
+        for i in range(k + 1, tiles):
+            for j in range(i, tiles):
+                blocks[i, j] = blocks[i, j] - matmul_tn(blocks[k, i], blocks[k, j])
+
+
+def write_basis(packed_ref, initial_ref, basis_ref, gram_ref):
+    tiles = gram_ref.shape[0] // TILE
+    for (i, j), at in block_places(tiles).items():
+        block = packed_ref[TILE * at : TILE * at + TILE, :]
+        gram_ref[TILE * i : TILE * i + TILE, TILE * j : TILE * j + TILE] = block
+        if i != j:
+            gram_ref[TILE * j : TILE * j + TILE, TILE * i : TILE * i + TILE] = block.T
+    product_t = matmul(initial_ref[...].T, gram_ref[...])
+    for sweep in range(ITERS):
+        inner = matmul_nt(product_t, product_t)
+        if sweep < ITERS - 1:
+            following = matmul(product_t, gram_ref[...])
+        _, inverse = factored(inner, False)
+        if sweep < ITERS - 1:
+            product_t = matmul(inverse, following)
+    basis_ref[...] = matmul(inverse, product_t).T
+
+
+def factor_kernel(part_ref, packed_ref, initial_ref, triangle_ref, basis_ref, gram_ref):
+    @pl.when(part_ref[0] != 1)
+    def _():
+        write_triangle(packed_ref, triangle_ref)
+
+    @pl.when(part_ref[0] != 0)
+    def _():
+        write_basis(packed_ref, initial_ref, basis_ref, gram_ref)
+
+
+def factors(packed, initial):
+    rows, keep = initial.shape
+    col_size = lax.axis_size("col")
+    shared = col_size % 2 == 0
+    part = lax.axis_index("col") % 2 if shared else jnp.int32(2)
+    vmem = pl.BlockSpec(memory_space=pltpu.VMEM)
+    triangle, basis = pl.pallas_call(
+        factor_kernel,
+        out_shape=[
+            jax.ShapeDtypeStruct((rows, rows), jnp.float32),
+            jax.ShapeDtypeStruct((rows, keep), jnp.float32),
+        ],
+        in_specs=[pl.BlockSpec(memory_space=pltpu.SMEM), vmem, vmem],
+        out_specs=[vmem, vmem],
+        scratch_shapes=[pltpu.VMEM((rows, rows), jnp.float32)],
+        compiler_params=pltpu.CompilerParams(vmem_limit_bytes=32 * 2**20),
+    )(jnp.full((1,), part, jnp.int32), packed, initial)
+    if not shared:
+        return triangle, basis
+    got_basis = lax.ppermute(basis, "col", [(d + 1, d) for d in range(0, col_size, 2)])
+    got_triangle = lax.ppermute(triangle, "col", [(d, d + 1) for d in range(0, col_size, 2)])
+    return jnp.where(part == 0, triangle, got_triangle), jnp.where(part == 0, got_basis, basis)
+
+
 def local(tensor, initial):
     mode_size = lax.axis_size("mode")
     row_part, slab_count, width = tensor.shape
@@ -71,35 +245,13 @@
     regrouped = lax.all_to_all(blocks, "mode", split_axis=0, concat_axis=0, tiled=True)
     unfold = regrouped.reshape(row_count, slab_count * cell_count)
     local_gram = matmul(unfold, unfold.T) / column_total
-    tiles = row_count // TILE
     packed = jnp.concatenate(
         [
             local_gram[i * TILE : (i + 1) * TILE, j * TILE : (j + 1) * TILE]
-            for i in range(tiles)
-            for j in range(i, tiles)
+            for i, j in block_places(row_count // TILE)
         ]
     )
-    packed = summed(packed)
-    found = {}
-    for i in range(tiles):
-        for j in range(i, tiles):
-            start = len(found) * TILE
-            found[i, j] = packed[start : start + TILE]
-    gram_sum = jnp.concatenate(
-        [
-            jnp.concatenate([found[i, j] if i <= j else found[j, i].T for j in range(tiles)], 1)
-            for i in range(tiles)
-        ]
-    )
-    triangle = jnp.linalg.cholesky(gram_sum).T
-    current = initial
-    for sweep in range(ITERS):
-        product = matmul(gram_sum, current)
-        inner = matmul(product.T, product)
-        lower_factor = jnp.linalg.cholesky(inner)
-        current = lax.linalg.triangular_solve(
-            lower_factor, product, left_side=False, lower=True, transpose_a=True
-        )
+    triangle, current = factors(summed(packed), initial)
     core_flat = matmul(current.T, unfold)
     core_tensor = core_flat.reshape(current.shape[1], slab_count, cell_count)
     return (core_tensor, current, triangle)

time: 266 us -> 91.8 us (0.35); the launches traced: 260 us -> 91.5 us
  other arithmetic: 155 us -> 2.24 us
  local copies, waits for them, and re-layouts: 19.6 us -> 5.14 us
  matrix products: 15.7 us -> 3.12 us
  Pallas kernels: 0 us -> 12.1 us
  starting transfers between devices: 19.6 us -> 24.4 us
  between operations: 4.19 us -> 0.95 us
  waiting for transfers between devices: 46.7 us -> 43.6 us
    another operation x29 -> x0, other arithmetic: 151 us -> none  [the longest x14 80.3 us: local(): triangle = jnp.linalg.cholesky(gram_sum).T]
    pallas_call x0 -> x1, Pallas kernels: none -> 12.1 us  [factors(): pl.pallas_call(factor_kernel, out_shape=[jax.ShapeDtypeStruct((rows, rows...]
    dot_general x8 -> x2, matrix products: 10.5 us -> 3.12 us  [matmul(): jnp.dot(left, right, precision=precise, preferred_element_type=jnp.float32)]
    unnamed x48 -> x13, local copies, waits for them, and re-layouts: 8.08 us -> 1.01 us
    another operation x9 -> x0, matrix products: 5.2 us -> none  [the longest x3 3.16 us: local(): lax.linalg.triangular_solve(lower_factor, product, left_side=False, lower...]
    ppermute x10, waiting for transfers between devices: 22.3 us -> 17.2 us  [exchanged(): return lax.ppermute(value, axis, pairs)]
    ppermute x0 -> x2, starting transfers between devices: none -> 4.5 us  [the longest x1 3.22 us: factors(): lax.ppermute(triangle, 'col', [(d, d + 1) for d in range(0, col_size, 2)])]
    dynamic_update_slice x4, local copies, waits for them, and re-layouts: 3.67 us -> 0.05 us  [gathered(): lax.dynamic_update_slice_in_dim(whole, part, (place ^ distance) * rows, 0)]
  transfers between devices with their start and end apart: 11 -> 13, of which waited for: 10 -> 12; matrix products, arithmetic and copies ran while one was open for 1% -> 4% of each run, Pallas kernels for 0% -> 0%
where the time goes in v2:
time: 91.8 us; the launch traced here: 91.5 us
  waiting for transfers between devices  43.6 us (47%)
  starting transfers between devices  24.4 us (27%)
  Pallas kernels  12.1 us (13%)
  local copies, waits for them, and re-layouts  5.14 us (6%)
  matrix products  3.12 us (3%)
  other arithmetic  2.24 us (2%)
  between operations  0.95 us (1%)
    all_to_all x1, waiting for transfers between devices, local(): lax.all_to_all(blocks, 'mode', split_axis=0, concat_axis=0, tiled=True)  24.4 us
    ppermute x10, waiting for transfers between devices, exchanged(): return lax.ppermute(value, axis, pairs)  17.2 us
    pallas_call x1, Pallas kernels, factors(): pl.pallas_call(factor_kernel, out_shape=[jax.ShapeDtypeStruct((rows, rows...  12.1 us
    ppermute x10, starting transfers between devices, exchanged(): return lax.ppermute(value, axis, pairs)  11.5 us
    all_to_all x1, starting transfers between devices, local(): lax.all_to_all(blocks, 'mode', split_axis=0, concat_axis=0, tiled=True)  8.31 us
    ppermute x1, starting transfers between devices, factors(): lax.ppermute(triangle, 'col', [(d, d + 1) for d in range(0, col_size, 2)])  3.22 us
    dot_general x2, matrix products, matmul(): jnp.dot(left, right, precision=precise, preferred_element_type=jnp.float32)  3.12 us
    ppermute x1, waiting for transfers between devices, factors(): lax.ppermute(basis, 'col', [(d + 1, d) for d in range(0, col_size, 2)])  1.92 us
  transfers between devices with their start and end apart: 13, of which 12 were waited for; matrix products, arithmetic and copies ran while one was open for 4% of the time, Pallas kernels for 0%

profile of v2, /device:TPU:0, one launch (start us, length us, event | category | flops | bytes accessed | tf_op | source)
XLA Modules:
  0.0 91.5 jit_solution(2673977778827805283)
XLA Ops:
  0.6 1.8 %copy.15 = f32[32,1,16,2,256]{4,3,1,0,2:T(2,128)S(1)} copy(f32[32,1,16,2,256]{4,3,2,1,0:T(2,128)} %bitcast.22) | data formatting | bytes 2097152 | tf_op jit(solution)/shard_map/reshape | solution.py:243
  2.4 1.8 %reshape.18 = f32[16,32,512]{2,1,0:T(8,128)} reshape(f32[16,32,2,256]{3,2,1,0:T(2,128)S(1)} %bitcast.21) | data formatting | bytes 2097152 | tf_op jit(solution)/shard_map/reshape | solution.py:244
  4.2 8.3 %all-to-all-start = ((f32[16,32,512]{2,1,0:T(8,128)}), f32[16,32,512]{2,1,0:T(8,128)S(1)}, u32[]{:S(2)}, u32[]{:S(2)}) async-start(f32[16,32,512]{2,1,0:T(8,128)} %reshape.18), calls=%async_computation | async-start | bytes 2097152 | tf_op jit(solution)/shard_map/all_to_all | solution.py:245
  12.5 24.4 %all-to-all-done = f32[16,32,512]{2,1,0:T(8,128)S(1)} async-done(((f32[16,32,512]{2,1,0:T(8,128)}), f32[16,32,512]{2,1,0:T(8,128)S(1)}, u32[]{:S(2)}, u32[]{:S(2)}) %all-to-all-start) | async-done | bytes 1048608 | tf_op jit(solution)/shard_map/all_to_all | solution.py:245
  37.0 1.9 %convolution_multiply_fusion = f32[512,512]{1,0:T(8,128)S(1)} fusion(f32[512,512]{1,0:T(8,128)S(1)} %bitcast.18), kind=kOutput, calls=%fused_computation | convolution fusion | flops 1610874880 | bytes 2097152 | tf_op jit(solution)/shard_map/dot_general | solution.py:19
  39.1 0.1 collective-permute-start
  39.2 1.6 %collective-permute-done = f32[640,128]{1,0:T(8,128)S(1)} collective-permute-done((f32[640,128]{1,0:T(8,128)S(1)}, f32[640,128]{1,0:T(8,128)S(1)}, u32[]{:S(2)}, u32[]{:S(2)}) %collective-permute-start) | collective-permute-done | bytes 327712 | tf_op jit(solution)/shard_map/ppermute | solution.py:36
  40.8 2.0 %collective-permute-start.3 = (f32[160,128]{1,0:T(8,128)S(1)}, f32[160,128]{1,0:T(8,128)S(1)}, u32[]{:S(2)}, u32[]{:S(2)}) collective-permute-start(f32[160,128]{1,0:T(8,128)S(1)} %get-tuple-element.16), channel_id=1, source_target_pairs={{0,6},{2,4},{4,2},{6,0},{8,14},{10,12},{12,10},{14,8},{16,22},{18,... | collective-permute-start | bytes 245768 | tf_op jit(solution)/shard_map/ppermute | solution.py:36
  42.9 0.1 collective-permute-start.2
  42.9 1.4 %collective-permute-start.1 = (f32[160,128]{1,0:T(8,128)S(1)}, f32[160,128]{1,0:T(8,128)S(1)}, u32[]{:S(2)}, u32[]{:S(2)}) collective-permute-start(f32[160,128]{1,0:T(8,128)S(1)} %get-tuple-element.15), channel_id=1, source_target_pairs={{0,2},{2,0},{4,6},{6,4},{8,10},{10,8},{12,14},{14,12},{16,18},{18,... | collective-permute-start | bytes 245768 | tf_op jit(solution)/shard_map/ppermute | solution.py:36
  44.4 2.0 %collective-permute-done.3 = f32[160,128]{1,0:T(8,128)S(1)} collective-permute-done((f32[160,128]{1,0:T(8,128)S(1)}, f32[160,128]{1,0:T(8,128)S(1)}, u32[]{:S(2)}, u32[]{:S(2)}) %collective-permute-start.3) | collective-permute-done | bytes 81952 | tf_op jit(solution)/shard_map/ppermute | solution.py:36
  46.4 1.7 %collective-permute-done.2 = f32[160,128]{1,0:T(8,128)S(1)} collective-permute-done((f32[160,128]{1,0:T(8,128)S(1)}, f32[160,128]{1,0:T(8,128)S(1)}, u32[]{:S(2)}, u32[]{:S(2)}) %collective-permute-start.2) | collective-permute-done | bytes 81952 | tf_op jit(solution)/shard_map/ppermute | solution.py:36
  48.0 0.5 collective-permute-done.1
  48.6 2.6 %collective-permute-start.4 = (f32[160,128]{1,0:T(8,128)S(1)}, f32[160,128]{1,0:T(8,128)S(1)}, u32[]{:S(2)}, u32[]{:S(2)}) collective-permute-start(f32[160,128]{1,0:T(8,128)S(1)} %add_add_fusion), channel_id=1, source_target_pairs={{0,8},{2,10},{4,12},{6,14},{8,0},{10,2},{12,4},{14,6},{16,24},{18,... | collective-permute-start | bytes 245768 | tf_op jit(solution)/shard_map/ppermute | solution.py:36
  51.1 2.6 %collective-permute-done.4 = f32[160,128]{1,0:T(8,128)S(1)} collective-permute-done((f32[160,128]{1,0:T(8,128)S(1)}, f32[160,128]{1,0:T(8,128)S(1)}, u32[]{:S(2)}, u32[]{:S(2)}) %collective-permute-start.4) | collective-permute-done | bytes 81952 | tf_op jit(solution)/shard_map/ppermute | solution.py:36
  53.8 1.7 %collective-permute-start.5 = (f32[160,128]{1,0:T(8,128)S(1)}, f32[160,128]{1,0:T(8,128)S(1)}, u32[]{:S(2)}, u32[]{:S(2)}) collective-permute-start(f32[160,128]{1,0:T(8,128)S(1)} %add.64), channel_id=1, source_target_pairs={{0,16},{2,18},{4,20},{6,22},{8,24},{10,26},{12,28},{14,30},{16,0},... | collective-permute-start | bytes 245768 | tf_op jit(solution)/shard_map/ppermute | solution.py:36
  55.5 3.9 %collective-permute-done.5 = f32[160,128]{1,0:T(8,128)S(1)} collective-permute-done((f32[160,128]{1,0:T(8,128)S(1)}, f32[160,128]{1,0:T(8,128)S(1)}, u32[]{:S(2)}, u32[]{:S(2)}) %collective-permute-start.5) | collective-permute-done | bytes 81952 | tf_op jit(solution)/shard_map/ppermute | solution.py:36
  59.5 0.4 collective-permute-start.6
  59.9 1.3 %collective-permute-start.7 = (f32[160,128]{1,0:T(8,128)S(1)}, f32[160,128]{1,0:T(8,128)S(1)}, u32[]{:S(2)}, u32[]{:S(2)}) collective-permute-start(f32[160,128]{1,0:T(8,128)S(1)} %get-tuple-element.14), channel_id=1, source_target_pairs={{0,4},{2,6},{4,0},{6,2},{8,12},{10,14},{12,8},{14,10},{16,20},{18,... | collective-permute-start | bytes 245768 | tf_op jit(solution)/shard_map/ppermute | solution.py:36
  61.2 1.9 %collective-permute-start.8 = (f32[160,128]{1,0:T(8,128)S(1)}, f32[160,128]{1,0:T(8,128)S(1)}, u32[]{:S(2)}, u32[]{:S(2)}) collective-permute-start(f32[160,128]{1,0:T(8,128)S(1)} %get-tuple-element.14), channel_id=1, source_target_pairs={{0,6},{2,4},{4,2},{6,0},{8,14},{10,12},{12,10},{14,8},{16,22},{18,... | collective-permute-start | bytes 245768 | tf_op jit(solution)/shard_map/ppermute | solution.py:36
  63.1 1.4 %collective-permute-done.6 = f32[160,128]{1,0:T(8,128)S(1)} collective-permute-done((f32[160,128]{1,0:T(8,128)S(1)}, f32[160,128]{1,0:T(8,128)S(1)}, u32[]{:S(2)}, u32[]{:S(2)}) %collective-permute-start.6) | collective-permute-done | bytes 81952 | tf_op jit(solution)/shard_map/ppermute | solution.py:36
  64.5 0.2 collective-permute-done.7
  64.7 1.8 %collective-permute-done.8 = f32[160,128]{1,0:T(8,128)S(1)} collective-permute-done((f32[160,128]{1,0:T(8,128)S(1)}, f32[160,128]{1,0:T(8,128)S(1)}, u32[]{:S(2)}, u32[]{:S(2)}) %collective-permute-start.8) | collective-permute-done | bytes 81952 | tf_op jit(solution)/shard_map/ppermute | solution.py:36
  66.5 0.1 collective-permute-start.9
  66.7 0.0 copy-start
  66.7 1.5 %collective-permute-done.9 = f32[640,128]{1,0:T(8,128)S(1)} collective-permute-done((f32[640,128]{1,0:T(8,128)S(1)}, f32[640,128]{1,0:T(8,128)S(1)}, u32[]{:S(2)}, u32[]{:S(2)}) %collective-permute-start.9) | collective-permute-done | bytes 327712 | tf_op jit(solution)/shard_map/ppermute | solution.py:36
  68.2 0.0 copy-done
  68.2 12.1 %shard_map.49 = (f32[512,512]{1,0:T(8,128)S(1)}, f32[512,128]{1,0:T(8,128)S(1)}) custom-call(s32[1]{0:T(128)} %bitcast.part_ref, f32[1280,128]{1,0:T(8,128)S(1)} %constant_dynamic-update-slice_fusion.packed_ref, f32[512,128]{1,0:T(8,128)S(1)} %copy-done), custom_call_target="tpu_custom_call" | custom-call | tf_op jit(solution)/shard_map/pallas_call | solution.py:219
  80.4 3.2 %collective-permute-start.11 = (f32[512,512]{1,0:T(8,128)S(1)}, f32[512,512]{1,0:T(8,128)}, u32[]{:S(2)}, u32[]{:S(2)}) collective-permute-start(f32[512,512]{1,0:T(8,128)S(1)} %get-tuple-element.6), channel_id=1, source_target_pairs={{0,1},{2,3},{4,5},{6,7},{8,9},{10,11},{12,13},{14,15},{16,17},{18,... | collective-permute-start | bytes 3145736 | tf_op jit(solution)/shard_map/ppermute | solution.py:233
  83.6 1.3 %collective-permute-start.10 = (f32[512,128]{1,0:T(8,128)S(1)}, f32[512,128]{1,0:T(8,128)}, u32[]{:S(2)}, u32[]{:S(2)}) collective-permute-start(f32[512,128]{1,0:T(8,128)S(1)} %get-tuple-element.5), channel_id=1, source_target_pairs={{1,0},{3,2},{5,4},{7,6},{9,8},{11,10},{13,12},{15,14},{17,16},{19,... | collective-permute-start | bytes 786440 | tf_op jit(solution)/shard_map/ppermute | solution.py:232
  84.9 0.3 copy.8
  85.2 1.9 %collective-permute-done.10 = f32[512,128]{1,0:T(8,128)} collective-permute-done((f32[512,128]{1,0:T(8,128)S(1)}, f32[512,128]{1,0:T(8,128)}, u32[]{:S(2)}, u32[]{:S(2)}) %collective-permute-start.10) | collective-permute-done | bytes 262176 | tf_op jit(solution)/shard_map/ppermute | solution.py:232
  87.2 1.0 %broadcast_select_fusion.1 = f32[512,128]{1,0:T(8,128)S(1)} fusion(f32[512,128]{1,0:T(8,128)} %collective-permute-done.10, f32[512,128]{1,0:T(8,128)S(1)} %get-tuple-element.5, pred[]{:T(512)S(6)} %eq.10), kind=kLoop, calls=%fused_computation.7 | loop fusion | flops 65536 | bytes 786433 | tf_op jit(solution)/shard_map/jit(_where)/select_n | solution.py:234
  88.1 0.0 copy-start.1
  88.2 1.3 %fusion = f32[128,2,256]{2,0,1:T(8,128)S(1)} fusion(f32[2,256,512]{2,1,0:T(8,128)S(1)} %bitcast.20, f32[512,128]{1,0:T(8,128)S(1)} %broadcast_select_fusion.1), kind=kOutput, calls=%fused_computation.4 | convolution fusion | flops 402653184 | bytes 1572864 | tf_op jit(solution)/shard_map/dot_general | solution.py:19
  89.4 0.0 copy-done.1
  89.4 0.9 copy.10
  90.3 0.0 collective-permute-done.11
  90.3 1.2 %broadcast_select_fusion = f32[512,512]{1,0:T(8,128)} fusion(f32[512,512]{1,0:T(8,128)S(1)} %get-tuple-element.6, f32[512,512]{1,0:T(8,128)} %collective-permute-done.11, pred[]{:T(512)S(6)} %eq.10), kind=kLoop, calls=%fused_computation.2 | loop fusion | flops 262144 | bytes 3145729 | tf_op jit(solution)/shard_map/jit(_where)/select_n | solution.py:234
  (22 shorter events, 0.4 us)
Async XLA Ops:
  4.2 32.8 %all-to-all-start = ((f32[16,32,512]{2,1,0:T(8,128)}), f32[16,32,512]{2,1,0:T(8,128)S(1)}, u32[]{:S(2)}, u32[]{:S(2)}) async-start(f32[16,32,512]{2,1,0:T(8,128)} %reshape.18), calls=%async_computation | async-start | bytes 2097152 | tf_op jit(solution)/shard_map/all_to_all | solution.py:245
  39.1 1.7 %collective-permute-start = (f32[640,128]{1,0:T(8,128)S(1)}, f32[640,128]{1,0:T(8,128)S(1)}, u32[]{:S(2)}, u32[]{:S(2)}) collective-permute-start(f32[640,128]{1,0:T(8,128)S(1)} %constant_dynamic-slice_fusion.3), channel_id=1, source_target_pairs={{0,1},{1,0},{2,3},{3,2},{4,5},{5,4},{6,7},{7,6},{8,9},{9,8},{10,11... | collective-permute-start | bytes 983048 | tf_op jit(solution)/shard_map/ppermute | solution.py:36
  40.8 5.6 %collective-permute-start.3 = (f32[160,128]{1,0:T(8,128)S(1)}, f32[160,128]{1,0:T(8,128)S(1)}, u32[]{:S(2)}, u32[]{:S(2)}) collective-permute-start(f32[160,128]{1,0:T(8,128)S(1)} %get-tuple-element.16), channel_id=1, source_target_pairs={{0,6},{2,4},{4,2},{6,0},{8,14},{10,12},{12,10},{14,8},{16,22},{18,... | collective-permute-start | bytes 245768 | tf_op jit(solution)/shard_map/ppermute | solution.py:36
  42.9 5.2 %collective-permute-start.2 = (f32[160,128]{1,0:T(8,128)S(1)}, f32[160,128]{1,0:T(8,128)S(1)}, u32[]{:S(2)}, u32[]{:S(2)}) collective-permute-start(f32[160,128]{1,0:T(8,128)S(1)} %get-tuple-element.17), channel_id=1, source_target_pairs={{0,4},{2,6},{4,0},{6,2},{8,12},{10,14},{12,8},{14,10},{16,20},{18,... | collective-permute-start | bytes 245768 | tf_op jit(solution)/shard_map/ppermute | solution.py:36
  42.9 5.6 %collective-permute-start.1 = (f32[160,128]{1,0:T(8,128)S(1)}, f32[160,128]{1,0:T(8,128)S(1)}, u32[]{:S(2)}, u32[]{:S(2)}) collective-permute-start(f32[160,128]{1,0:T(8,128)S(1)} %get-tuple-element.15), channel_id=1, source_target_pairs={{0,2},{2,0},{4,6},{6,4},{8,10},{10,8},{12,14},{14,12},{16,18},{18,... | collective-permute-start | bytes 245768 | tf_op jit(solution)/shard_map/ppermute | solution.py:36
  48.6 5.2 %collective-permute-start.4 = (f32[160,128]{1,0:T(8,128)S(1)}, f32[160,128]{1,0:T(8,128)S(1)}, u32[]{:S(2)}, u32[]{:S(2)}) collective-permute-start(f32[160,128]{1,0:T(8,128)S(1)} %add_add_fusion), channel_id=1, source_target_pairs={{0,8},{2,10},{4,12},{6,14},{8,0},{10,2},{12,4},{14,6},{16,24},{18,... | collective-permute-start | bytes 245768 | tf_op jit(solution)/shard_map/ppermute | solution.py:36
  53.8 5.7 %collective-permute-start.5 = (f32[160,128]{1,0:T(8,128)S(1)}, f32[160,128]{1,0:T(8,128)S(1)}, u32[]{:S(2)}, u32[]{:S(2)}) collective-permute-start(f32[160,128]{1,0:T(8,128)S(1)} %add.64), channel_id=1, source_target_pairs={{0,16},{2,18},{4,20},{6,22},{8,24},{10,26},{12,28},{14,30},{16,0},... | collective-permute-start | bytes 245768 | tf_op jit(solution)/shard_map/ppermute | solution.py:36
  59.5 5.0 %collective-permute-start.6 = (f32[160,128]{1,0:T(8,128)S(1)}, f32[160,128]{1,0:T(8,128)S(1)}, u32[]{:S(2)}, u32[]{:S(2)}) collective-permute-start(f32[160,128]{1,0:T(8,128)S(1)} %get-tuple-element.14), channel_id=1, source_target_pairs={{0,2},{2,0},{4,6},{6,4},{8,10},{10,8},{12,14},{14,12},{16,18},{18,... | collective-permute-start | bytes 245768 | tf_op jit(solution)/shard_map/ppermute | solution.py:36
  59.9 4.8 %collective-permute-start.7 = (f32[160,128]{1,0:T(8,128)S(1)}, f32[160,128]{1,0:T(8,128)S(1)}, u32[]{:S(2)}, u32[]{:S(2)}) collective-permute-start(f32[160,128]{1,0:T(8,128)S(1)} %get-tuple-element.14), channel_id=1, source_target_pairs={{0,4},{2,6},{4,0},{6,2},{8,12},{10,14},{12,8},{14,10},{16,20},{18,... | collective-permute-start | bytes 245768 | tf_op jit(solution)/shard_map/ppermute | solution.py:36
  61.2 5.3 %collective-permute-start.8 = (f32[160,128]{1,0:T(8,128)S(1)}, f32[160,128]{1,0:T(8,128)S(1)}, u32[]{:S(2)}, u32[]{:S(2)}) collective-permute-start(f32[160,128]{1,0:T(8,128)S(1)} %get-tuple-element.14), channel_id=1, source_target_pairs={{0,6},{2,4},{4,2},{6,0},{8,14},{10,12},{12,10},{14,8},{16,22},{18,... | collective-permute-start | bytes 245768 | tf_op jit(solution)/shard_map/ppermute | solution.py:36
  66.5 1.7 %collective-permute-start.9 = (f32[640,128]{1,0:T(8,128)S(1)}, f32[640,128]{1,0:T(8,128)S(1)}, u32[]{:S(2)}, u32[]{:S(2)}) collective-permute-start(f32[640,128]{1,0:T(8,128)S(1)} %constant_dynamic-update-slice_fusion.2), channel_id=1, source_target_pairs={{0,1},{1,0},{2,3},{3,2},{4,5},{5,4},{6,7},{7,6},{8,9},{9,8},{10,11... | collective-permute-start | bytes 983048 | tf_op jit(solution)/shard_map/ppermute | solution.py:36
  66.7 1.6 %copy-start = (f32[512,128]{1,0:T(8,128)S(1)}, f32[512,128]{1,0:T(8,128)}, u32[]{:S(2)}) copy-start(f32[512,128]{1,0:T(8,128)} %initial_ref.1) | copy-start | bytes 786436
  80.4 10.0 %collective-permute-start.11 = (f32[512,512]{1,0:T(8,128)S(1)}, f32[512,512]{1,0:T(8,128)}, u32[]{:S(2)}, u32[]{:S(2)}) collective-permute-start(f32[512,512]{1,0:T(8,128)S(1)} %get-tuple-element.6), channel_id=1, source_target_pairs={{0,1},{2,3},{4,5},{6,7},{8,9},{10,11},{12,13},{14,15},{16,17},{18,... | collective-permute-start | bytes 3145736 | tf_op jit(solution)/shard_map/ppermute | solution.py:233
  83.6 3.5 %collective-permute-start.10 = (f32[512,128]{1,0:T(8,128)S(1)}, f32[512,128]{1,0:T(8,128)}, u32[]{:S(2)}, u32[]{:S(2)}) collective-permute-start(f32[512,128]{1,0:T(8,128)S(1)} %get-tuple-element.5), channel_id=1, source_target_pairs={{1,0},{3,2},{5,4},{7,6},{9,8},{11,10},{13,12},{15,14},{17,16},{19,... | collective-permute-start | bytes 786440 | tf_op jit(solution)/shard_map/ppermute | solution.py:232
  88.1 1.3 %copy-start.1 = (f32[512,128]{1,0:T(8,128)}, f32[512,128]{1,0:T(8,128)S(1)}, u32[]{:S(2)}) copy-start(f32[512,128]{1,0:T(8,128)S(1)} %broadcast_select_fusion.1) | copy-start | bytes 786436

commit v3 on v2

--- a/solution.py
+++ b/solution.py
@@ -94,28 +94,25 @@
     lane = lax.broadcasted_iota(jnp.int32, (SUB, side), 1)
     tiles = [block[SUB * t : SUB * t + SUB, :] for t in range(count)]
     scales = [None] * count
+    members = range(PANEL)
     for first in range(0, count, PANEL):
         base = first * SUB
         inside = (lane >= base) & (lane < base + width)
-        members = range(PANEL)
         columns = [[lane_of(tiles[first + h], base + j) for h in members] for j in range(width)]
-        below = {
-            t: [lane_of(tiles[t], base + j) for j in range(width)] for t in range(first + PANEL, count)
-        }
-        upper = [tiles[first + h] for h in members]
-        inverse = [
-            jnp.where(inside, jnp.where(lane == row + base + SUB * h, 1.0, 0.0), upper[h]) for h in members
-        ]
-        kept_upper, kept_inverse, scale = list(upper), list(inverse), [None] * PANEL
+        near = range(first + PANEL, min(first + 2 * PANEL, count))
+        far = range(first + 2 * PANEL, count)
+        below = {t: [lane_of(tiles[t], base + j) for j in range(width)] for t in near}
+        panel = [tiles[first + h] for h in members]
+        if far:
+            sent = jnp.concatenate([jnp.where(lane >= base + width + width, panel[h], 0.0) for h in members])
+        kept, scale = list(panel), [None] * PANEL
         for pivot in range(width):
             own, place = divmod(pivot, SUB)
+            here = row == place
+            cleared = lane == base + pivot
             reciprocal = pl.reciprocal(row_of(columns[pivot][own], place), approx=True)
-            first_row = place == 0
-            here = row == place
-            scale[own] = reciprocal if first_row else jnp.where(here, reciprocal, scale[own])
-            kept_inverse[own] = inverse[own] if first_row else jnp.where(here, inverse[own], kept_inverse[own])
-            if with_upper:
-                kept_upper[own] = upper[own] if first_row else jnp.where(here, upper[own], kept_upper[own])
+            scale[own] = jnp.where(here, reciprocal, scale[own]) if place else reciprocal
+            kept[own] = jnp.where(here, panel[own], kept[own]) if place else panel[own]
             factor = [
                 (jnp.where(here, 0.0, columns[pivot][h]) if h == own else columns[pivot][h]) * reciprocal
                 for h in members
@@ -123,21 +120,18 @@
             for j in range(pivot + 1, width):
                 value = row_of(columns[j][own], place)
                 columns[j] = [columns[j][h] - factor[h] * value for h in members]
-            value = row_of(inverse[own], place)
-            inverse = [inverse[h] - factor[h] * value for h in members]
-            if with_upper:
-                value = row_of(upper[own], place)
-                upper = [upper[h] - factor[h] * value for h in members]
+            value = jnp.where(cleared, 1.0, row_of(panel[own], place))
+            panel = [
+                jnp.where(cleared, jnp.where(here, 1.0, 0.0) if h == own else 0.0, panel[h]) - factor[h] * value
+                for h in members
+            ]
         for h in members:
-            on_or_right = inside & (lane >= row + base + SUB * h)
-            tiles[first + h] = (
-                jnp.where(on_or_right, kept_upper[h], kept_inverse[h]) if with_upper else kept_inverse[h]
-            )
+            tiles[first + h] = kept[h]
             scales[first + h] = scale[h]
-        if first + PANEL < count:
-            reduced = [inverse[h] * scale[h] for h in members]
+        if near:
+            reduced = [panel[h] * scale[h] for h in members]
             rows = [row_of(reduced[m // SUB], m % SUB) for m in range(width)]
-            for t in range(first + PANEL, count):
+            for t in near:
                 even = jnp.where(inside, 0.0, tiles[t])
                 odd = None
                 for m in range(width):
@@ -147,6 +141,10 @@
                     else:
                         even = even - term
                 tiles[t] = even - odd
+            if far:
+                update = matmul_tn(sent, jnp.concatenate(reduced))
+                for t in far:
+                    tiles[t] = jnp.where(inside, 0.0, tiles[t]) - update[SUB * t : SUB * t + SUB]
     uppers, inverses = [], []
     for t in range(count):
         root = lax.rsqrt(scales[t]) * scales[t]
@@ -163,27 +161,22 @@
     }
 
 
-def write_triangle(packed_ref, triangle_ref):
-    tiles = triangle_ref.shape[0] // TILE
+def write_triangle(packed_ref, outbox_ref, tiles):
     places = block_places(tiles)
     blocks = {pair: packed_ref[TILE * at : TILE * at + TILE, :] for pair, at in places.items()}
     for k in range(tiles):
-        upper, inverse = factored(blocks[k, k], True)
-        for j in range(tiles):
-            if j < k:
-                part = jnp.zeros((TILE, TILE), jnp.float32)
-            elif j == k:
-                part = upper
-            else:
-                part = blocks[k, j] = matmul(inverse, blocks[k, j])
-            triangle_ref[TILE * k : TILE * k + TILE, TILE * j : TILE * j + TILE] = part
+        blocks[k, k], inverse = factored(blocks[k, k], True)
+        for j in range(k + 1, tiles):
+            blocks[k, j] = matmul(inverse, blocks[k, j])
+        for j in range(k, tiles):
+            at = places[k, j]
+            outbox_ref[TILE * at : TILE * at + TILE, :] = blocks[k, j]
         for i in range(k + 1, tiles):
             for j in range(i, tiles):
                 blocks[i, j] = blocks[i, j] - matmul_tn(blocks[k, i], blocks[k, j])
 
 
-def write_basis(packed_ref, initial_ref, basis_ref, gram_ref):
-    tiles = gram_ref.shape[0] // TILE
+def write_basis(packed_ref, initial_ref, outbox_ref, gram_ref, tiles):
     for (i, j), at in block_places(tiles).items():
         block = packed_ref[TILE * at : TILE * at + TILE, :]
         gram_ref[TILE * i : TILE * i + TILE, TILE * j : TILE * j + TILE] = block
@@ -197,41 +190,89 @@
         _, inverse = factored(inner, False)
         if sweep < ITERS - 1:
             product_t = matmul(inverse, following)
-    basis_ref[...] = matmul(inverse, product_t).T
-
-
-def factor_kernel(part_ref, packed_ref, initial_ref, triangle_ref, basis_ref, gram_ref):
-    @pl.when(part_ref[0] != 1)
+    current_t = matmul(inverse, product_t)
+    rows = current_t.shape[1]
+    outbox_ref[:rows, :] = current_t.T
+    for i in range(tiles):
+        outbox_ref[rows + TILE * i : rows + TILE * i + TILE, :] = current_t[:, TILE * i : TILE * i + TILE]
+
+
+def factor_kernel(tiles, part_ref, packed_ref, initial_ref, outbox_ref, gram_ref):
+    @pl.when(part_ref[0] == 0)
     def _():
-        write_triangle(packed_ref, triangle_ref)
+        write_triangle(packed_ref, outbox_ref, tiles)
 
     @pl.when(part_ref[0] != 0)
     def _():
-        write_basis(packed_ref, initial_ref, basis_ref, gram_ref)
-
-
-def factors(packed, initial):
+        write_basis(packed_ref, initial_ref, outbox_ref, gram_ref, tiles)
+
+
+def closing_kernel(tiles, part_ref, outbox_ref, inbox_ref, unfold_ref, core_ref, basis_ref, triangle_ref):
+    def close(triangle_box, basis_box):
+        places = block_places(tiles)
+        rows = basis_ref.shape[0]
+        current_t = jnp.concatenate(
+            [basis_box[rows + TILE * i : rows + TILE * i + TILE, :] for i in range(tiles)], axis=1
+        )
+        core_ref[...] = matmul(current_t, unfold_ref[...])
+        basis_ref[...] = basis_box[:rows, :]
+        for i in range(tiles):
+            for j in range(tiles):
+                at = places.get((i, j))
+                triangle_ref[TILE * i : TILE * i + TILE, TILE * j : TILE * j + TILE] = (
+                    jnp.zeros((TILE, TILE), jnp.float32)
+                    if at is None
+                    else triangle_box[TILE * at : TILE * at + TILE, :]
+                )
+
+    @pl.when(part_ref[0] == 0)
+    def _():
+        close(outbox_ref, inbox_ref)
+
+    @pl.when(part_ref[0] != 0)
+    def _():
+        close(inbox_ref, outbox_ref)
+
+
+VMEM_LIMIT = 32 * 2**20
+
+
+def factors(packed, initial, part):
     rows, keep = initial.shape
-    col_size = lax.axis_size("col")
-    shared = col_size % 2 == 0
-    part = lax.axis_index("col") % 2 if shared else jnp.int32(2)
+    tiles = rows // TILE
     vmem = pl.BlockSpec(memory_space=pltpu.VMEM)
-    triangle, basis = pl.pallas_call(
-        factor_kernel,
+    return pl.pallas_call(
+        functools.partial(factor_kernel, tiles),
+        out_shape=jax.ShapeDtypeStruct((max(packed.shape[0], rows + tiles * keep), TILE), jnp.float32),
+        in_specs=[pl.BlockSpec(memory_space=pltpu.SMEM), vmem, vmem],
+        out_specs=vmem,
+        scratch_shapes=[pltpu.VMEM((rows, rows), jnp.float32)],
+        compiler_params=pltpu.CompilerParams(vmem_limit_bytes=VMEM_LIMIT),
+    )(part, packed, initial)
+
+
+def finished(packed, initial, unfold):
+    rows, keep = initial.shape
+    if lax.axis_size("col") % 2 == 0:
+        part = jnp.full((1,), lax.axis_index("col") % 2, jnp.int32)
+        outbox = factors(packed, initial, part)
+        inbox = exchanged(outbox, "col", 1)
+    else:
+        part = jnp.zeros((1,), jnp.int32)
+        outbox = factors(packed, initial, part)
+        inbox = factors(packed, initial, part + 1)
+    vmem = pl.BlockSpec(memory_space=pltpu.VMEM)
+    return pl.pallas_call(
+        functools.partial(closing_kernel, rows // TILE),
         out_shape=[
+            jax.ShapeDtypeStruct((keep, unfold.shape[1]), jnp.float32),
+            jax.ShapeDtypeStruct((rows, keep), jnp.float32),
             jax.ShapeDtypeStruct((rows, rows), jnp.float32),
-            jax.ShapeDtypeStruct((rows, keep), jnp.float32),
         ],
-        in_specs=[pl.BlockSpec(memory_space=pltpu.SMEM), vmem, vmem],
-        out_specs=[vmem, vmem],
-        scratch_shapes=[pltpu.VMEM((rows, rows), jnp.float32)],
-        compiler_params=pltpu.CompilerParams(vmem_limit_bytes=32 * 2**20),
-    )(jnp.full((1,), part, jnp.int32), packed, initial)
-    if not shared:
-        return triangle, basis
-    got_basis = lax.ppermute(basis, "col", [(d + 1, d) for d in range(0, col_size, 2)])
-    got_triangle = lax.ppermute(triangle, "col", [(d, d + 1) for d in range(0, col_size, 2)])
-    return jnp.where(part == 0, triangle, got_triangle), jnp.where(part == 0, got_basis, basis)
+        in_specs=[pl.BlockSpec(memory_space=pltpu.SMEM), vmem, vmem, vmem],
+        out_specs=[vmem, vmem, vmem],
+        compiler_params=pltpu.CompilerParams(vmem_limit_bytes=VMEM_LIMIT),
+    )(part, outbox, inbox, unfold)
 
 
 def local(tensor, initial):
@@ -251,8 +292,7 @@
             for i, j in block_places(row_count // TILE)
         ]
     )
-    triangle, current = factors(summed(packed), initial)
-    core_flat = matmul(current.T, unfold)
+    core_flat, current, triangle = finished(summed(packed), initial, unfold)
     core_tensor = core_flat.reshape(current.shape[1], slab_count, cell_count)
     return (core_tensor, current, triangle)
 

time: 91.8 us -> 87.1 us (0.949)
  starting transfers between devices: 24.4 us -> 20 us
  other arithmetic: 2.24 us -> 0.08 us
  Pallas kernels: 12.1 us -> 14.1 us
  matrix products: 3.12 us -> 1.86 us
    ppermute x2 -> x0, starting transfers between devices: 4.5 us -> none  [the longest x1 3.22 us: factors(): lax.ppermute(triangle, 'col', [(d, d + 1) for d in range(0, col_size, 2)])]
    ppermute x10 -> x11, waiting for transfers between devices: 17.2 us -> 19.5 us  [exchanged(): return lax.ppermute(value, axis, pairs)]
    select_n x2 -> x0, other arithmetic: 2.16 us -> none  [the longest x1 1.18 us: factors(): jnp.where(part == 0, triangle, got_triangle)]
    pallas_call x1 -> x2, Pallas kernels: 12.1 us -> 14.1 us  [the longest x1 12.3 us: factors(): pl.pallas_call(functools.partial(factor_kernel, tiles), out_shape=jax.Sha...]
    ppermute x2 -> x0, waiting for transfers between devices: 1.92 us -> none  [the longest x1 1.92 us: factors(): lax.ppermute(basis, 'col', [(d + 1, d) for d in range(0, col_size, 2)])]
    dot_general x2 -> x1, matrix products: 3.12 us -> 1.86 us  [matmul(): jnp.dot(left, right, precision=precise, preferred_element_type=jnp.float32)]
    ppermute x10 -> x11, starting transfers between devices: 11.5 us -> 11.7 us  [exchanged(): return lax.ppermute(value, axis, pairs)]
  transfers between devices with their start and end apart: 13 -> 12, of which waited for: 12 -> 12; matrix products, arithmetic and copies ran while one was open for 4% -> 0% of each run, Pallas kernels for 0% -> 0%
where the time goes in v3:
time: 87.1 us; the launch traced here: 86.8 us
  waiting for transfers between devices  43.9 us (50%)
  starting transfers between devices  20 us (23%)
  Pallas kernels  14.1 us (16%)
  local copies, waits for them, and re-layouts  5.93 us (7%)
  matrix products  1.86 us (2%)
  between operations  0.92 us (1%)
    all_to_all x1, waiting for transfers between devices, local(): lax.all_to_all(blocks, 'mode', split_axis=0, concat_axis=0, tiled=True)  24.4 us
    ppermute x11, waiting for transfers between devices, exchanged(): return lax.ppermute(value, axis, pairs)  19.5 us
    pallas_call x1, Pallas kernels, factors(): pl.pallas_call(functools.partial(factor_kernel, tiles), out_shape=jax.Sha...  12.3 us
    ppermute x11, starting transfers between devices, exchanged(): return lax.ppermute(value, axis, pairs)  11.7 us
    all_to_all x1, starting transfers between devices, local(): lax.all_to_all(blocks, 'mode', split_axis=0, concat_axis=0, tiled=True)  8.31 us
    reshape x1, local copies, waits for them, and re-layouts, local(): tensor.reshape(row_part, slab_count, mode_size, cell_count)  2.13 us
    dot_general x1, matrix products, matmul(): jnp.dot(left, right, precision=precise, preferred_element_type=jnp.float32)  1.86 us
    reshape x1, local copies, waits for them, and re-layouts, local(): blocks = blocks.reshape(mode_size, row_part, slab_count * cell_count)  1.81 us
  transfers between devices with their start and end apart: 12, of which 12 were waited for; matrix products, arithmetic and copies ran while one was open for 0% of the time, Pallas kernels for 0%

profile of v3, /device:TPU:0, one launch (start us, length us, event | category | flops | bytes accessed | tf_op | source)
XLA Modules:
  0.0 86.8 jit_solution(11521178525187547989)
XLA Ops:
  0.6 2.1 %reshape.18 = f32[32,2,16,256]{3,2,1,0:T(8,128)S(1)} reshape(f32[32,2,4096]{2,1,0:T(2,128)} %param.2) | data formatting | bytes 2097152 | tf_op jit(solution)/shard_map/reshape | solution.py:284
  2.8 0.8 copy.5
  3.6 1.8 %reshape.19 = f32[16,32,512]{2,1,0:T(8,128)} reshape(f32[16,32,2,256]{3,2,1,0:T(2,128)S(1)} %copy.5) | data formatting | bytes 2097152 | tf_op jit(solution)/shard_map/reshape | solution.py:285
  5.4 8.3 %all-to-all-start = ((f32[16,32,512]{2,1,0:T(8,128)}), f32[16,32,512]{2,1,0:T(8,128)S(1)}, u32[]{:S(2)}, u32[]{:S(2)}) async-start(f32[16,32,512]{2,1,0:T(8,128)} %reshape.19), calls=%async_computation | async-start | bytes 2097152 | tf_op jit(solution)/shard_map/all_to_all | solution.py:286
  13.7 24.4 %all-to-all-done = f32[16,32,512]{2,1,0:T(8,128)S(1)} async-done(((f32[16,32,512]{2,1,0:T(8,128)}), f32[16,32,512]{2,1,0:T(8,128)S(1)}, u32[]{:S(2)}, u32[]{:S(2)}) %all-to-all-start) | async-done | bytes 1048608 | tf_op jit(solution)/shard_map/all_to_all | solution.py:286
  38.1 1.9 %convolution_multiply_fusion = f32[512,512]{1,0:T(8,128)S(1)} fusion(f32[512,512]{1,0:T(8,128)S(1)} %bitcast.5), kind=kOutput, calls=%fused_computation | convolution fusion | flops 1610874880 | bytes 2097152 | tf_op jit(solution)/shard_map/dot_general | solution.py:19
  40.2 0.1 collective-permute-start
  40.4 1.6 %collective-permute-done = f32[640,128]{1,0:T(8,128)S(1)} collective-permute-done((f32[640,128]{1,0:T(8,128)S(1)}, f32[640,128]{1,0:T(8,128)S(1)}, u32[]{:S(2)}, u32[]{:S(2)}) %collective-permute-start) | collective-permute-done | bytes 327712 | tf_op jit(solution)/shard_map/ppermute | solution.py:36
  42.0 0.6 collective-permute-start.1
  42.6 2.0 %collective-permute-start.2 = (f32[160,128]{1,0:T(8,128)S(1)}, f32[160,128]{1,0:T(8,128)S(1)}, u32[]{:S(2)}, u32[]{:S(2)}) collective-permute-start(f32[160,128]{1,0:T(8,128)S(1)} %get-tuple-element.13), channel_id=1, source_target_pairs={{0,4},{2,6},{4,0},{6,2},{8,12},{10,14},{12,8},{14,10},{16,20},{18,... | collective-permute-start | bytes 245768 | tf_op jit(solution)/shard_map/ppermute | solution.py:36
  44.6 1.0 %collective-permute-start.3 = (f32[160,128]{1,0:T(8,128)S(1)}, f32[160,128]{1,0:T(8,128)S(1)}, u32[]{:S(2)}, u32[]{:S(2)}) collective-permute-start(f32[160,128]{1,0:T(8,128)S(1)} %get-tuple-element.12), channel_id=1, source_target_pairs={{0,6},{2,4},{4,2},{6,0},{8,14},{10,12},{12,10},{14,8},{16,22},{18,... | collective-permute-start | bytes 245768 | tf_op jit(solution)/shard_map/ppermute | solution.py:36
  45.6 1.1 %collective-permute-done.1 = f32[160,128]{1,0:T(8,128)S(1)} collective-permute-done((f32[160,128]{1,0:T(8,128)S(1)}, f32[160,128]{1,0:T(8,128)S(1)}, u32[]{:S(2)}, u32[]{:S(2)}) %collective-permute-start.1) | collective-permute-done | bytes 81952 | tf_op jit(solution)/shard_map/ppermute | solution.py:36
  46.6 1.6 %collective-permute-done.2 = f32[160,128]{1,0:T(8,128)S(1)} collective-permute-done((f32[160,128]{1,0:T(8,128)S(1)}, f32[160,128]{1,0:T(8,128)S(1)}, u32[]{:S(2)}, u32[]{:S(2)}) %collective-permute-start.2) | collective-permute-done | bytes 81952 | tf_op jit(solution)/shard_map/ppermute | solution.py:36
  48.2 1.7 %collective-permute-done.3 = f32[160,128]{1,0:T(8,128)S(1)} collective-permute-done((f32[160,128]{1,0:T(8,128)S(1)}, f32[160,128]{1,0:T(8,128)S(1)}, u32[]{:S(2)}, u32[]{:S(2)}) %collective-permute-start.3) | collective-permute-done | bytes 81952 | tf_op jit(solution)/shard_map/ppermute | solution.py:36
  50.0 2.4 %collective-permute-start.4 = (f32[160,128]{1,0:T(8,128)S(1)}, f32[160,128]{1,0:T(8,128)S(1)}, u32[]{:S(2)}, u32[]{:S(2)}) collective-permute-start(f32[160,128]{1,0:T(8,128)S(1)} %add_add_fusion), channel_id=1, source_target_pairs={{0,8},{2,10},{4,12},{6,14},{8,0},{10,2},{12,4},{14,6},{16,24},{18,... | collective-permute-start | bytes 245768 | tf_op jit(solution)/shard_map/ppermute | solution.py:36
  52.3 2.4 %collective-permute-done.4 = f32[160,128]{1,0:T(8,128)S(1)} collective-permute-done((f32[160,128]{1,0:T(8,128)S(1)}, f32[160,128]{1,0:T(8,128)S(1)}, u32[]{:S(2)}, u32[]{:S(2)}) %collective-permute-start.4) | collective-permute-done | bytes 81952 | tf_op jit(solution)/shard_map/ppermute | solution.py:36
  54.8 2.0 %collective-permute-start.5 = (f32[160,128]{1,0:T(8,128)S(1)}, f32[160,128]{1,0:T(8,128)S(1)}, u32[]{:S(2)}, u32[]{:S(2)}) collective-permute-start(f32[160,128]{1,0:T(8,128)S(1)} %add.64), channel_id=1, source_target_pairs={{0,16},{2,18},{4,20},{6,22},{8,24},{10,26},{12,28},{14,30},{16,0},... | collective-permute-start | bytes 245768 | tf_op jit(solution)/shard_map/ppermute | solution.py:36
  56.8 3.4 %collective-permute-done.5 = f32[160,128]{1,0:T(8,128)S(1)} collective-permute-done((f32[160,128]{1,0:T(8,128)S(1)}, f32[160,128]{1,0:T(8,128)S(1)}, u32[]{:S(2)}, u32[]{:S(2)}) %collective-permute-start.5) | collective-permute-done | bytes 81952 | tf_op jit(solution)/shard_map/ppermute | solution.py:36
  60.2 1.7 %collective-permute-start.6 = (f32[160,128]{1,0:T(8,128)S(1)}, f32[160,128]{1,0:T(8,128)S(1)}, u32[]{:S(2)}, u32[]{:S(2)}) collective-permute-start(f32[160,128]{1,0:T(8,128)S(1)} %get-tuple-element.10), channel_id=1, source_target_pairs={{0,2},{2,0},{4,6},{6,4},{8,10},{10,8},{12,14},{14,12},{16,18},{18,... | collective-permute-start | bytes 245768 | tf_op jit(solution)/shard_map/ppermute | solution.py:36
  61.9 0.7 collective-permute-start.7
  62.6 1.2 %collective-permute-start.8 = (f32[160,128]{1,0:T(8,128)S(1)}, f32[160,128]{1,0:T(8,128)S(1)}, u32[]{:S(2)}, u32[]{:S(2)}) collective-permute-start(f32[160,128]{1,0:T(8,128)S(1)} %get-tuple-element.10), channel_id=1, source_target_pairs={{0,6},{2,4},{4,2},{6,0},{8,14},{10,12},{12,10},{14,8},{16,22},{18,... | collective-permute-start | bytes 245768 | tf_op jit(solution)/shard_map/ppermute | solution.py:36
  63.8 1.0 %collective-permute-done.6 = f32[160,128]{1,0:T(8,128)S(1)} collective-permute-done((f32[160,128]{1,0:T(8,128)S(1)}, f32[160,128]{1,0:T(8,128)S(1)}, u32[]{:S(2)}, u32[]{:S(2)}) %collective-permute-start.6) | collective-permute-done | bytes 81952 | tf_op jit(solution)/shard_map/ppermute | solution.py:36
  64.8 1.6 %collective-permute-done.7 = f32[160,128]{1,0:T(8,128)S(1)} collective-permute-done((f32[160,128]{1,0:T(8,128)S(1)}, f32[160,128]{1,0:T(8,128)S(1)}, u32[]{:S(2)}, u32[]{:S(2)}) %collective-permute-start.7) | collective-permute-done | bytes 81952 | tf_op jit(solution)/shard_map/ppermute | solution.py:36
  66.4 1.6 %collective-permute-done.8 = f32[160,128]{1,0:T(8,128)S(1)} collective-permute-done((f32[160,128]{1,0:T(8,128)S(1)}, f32[160,128]{1,0:T(8,128)S(1)}, u32[]{:S(2)}, u32[]{:S(2)}) %collective-permute-start.8) | collective-permute-done | bytes 81952 | tf_op jit(solution)/shard_map/ppermute | solution.py:36
  68.0 0.1 collective-permute-start.9
  68.2 0.0 copy-start
  68.2 1.5 %collective-permute-done.9 = f32[640,128]{1,0:T(8,128)S(1)} collective-permute-done((f32[640,128]{1,0:T(8,128)S(1)}, f32[640,128]{1,0:T(8,128)S(1)}, u32[]{:S(2)}, u32[]{:S(2)}) %collective-permute-start.9) | collective-permute-done | bytes 327712 | tf_op jit(solution)/shard_map/ppermute | solution.py:36
  69.7 0.0 copy-done
  69.7 12.3 %shard_map.49.outbox_ref = f32[1280,128]{1,0:T(8,128)S(1)} custom-call(s32[1]{0:T(128)} %bitcast.part_ref, f32[1280,128]{1,0:T(8,128)S(1)} %constant_dynamic-update-slice_fusion.packed_ref, f32[512,128]{1,0:T(8,128)S(1)} %copy-done), custom_call_target="tpu_custom_call" | custom-call | tf_op jit(solution)/shard_map/pallas_call | solution.py:244
  82.1 0.1 collective-permute-start.10
  82.1 2.1 %collective-permute-done.10.inbox_ref = f32[1280,128]{1,0:T(8,128)S(1)} collective-permute-done((f32[1280,128]{1,0:T(8,128)S(1)}, f32[1280,128]{1,0:T(8,128)S(1)}, u32[]{:S(2)}, u32[]{:S(2)}) %collective-permute-start.10) | collective-permute-done | bytes 655392 | tf_op jit(solution)/shard_map/ppermute | solution.py:36
  84.2 1.7 %shard_map.50 = (f32[128,512]{1,0:T(8,128)S(1)}, f32[512,128]{1,0:T(8,128)}, f32[512,512]{1,0:T(8,128)}) custom-call(s32[1]{0:T(128)} %bitcast.part_ref, f32[1280,128]{1,0:T(8,128)S(1)} %shard_map.49.outbox_ref, f32[1280,128]{1,0:T(8,128)S(1)} %collective-permute-done.10.inbox_ref, f32[512,512]{1,0:T(8,128)S(1)} %bitcast.6), custom_call_target="tpu_custom_call" | custom-call | tf_op jit(solution)/shard_map/pallas_call | solution.py:265
  86.0 0.9 reshape.21
  (22 shorter events, 0.4 us)
Async XLA Ops:
  5.4 32.8 %all-to-all-start = ((f32[16,32,512]{2,1,0:T(8,128)}), f32[16,32,512]{2,1,0:T(8,128)S(1)}, u32[]{:S(2)}, u32[]{:S(2)}) async-start(f32[16,32,512]{2,1,0:T(8,128)} %reshape.19), calls=%async_computation | async-start | bytes 2097152 | tf_op jit(solution)/shard_map/all_to_all | solution.py:286
  40.2 1.7 %collective-permute-start = (f32[640,128]{1,0:T(8,128)S(1)}, f32[640,128]{1,0:T(8,128)S(1)}, u32[]{:S(2)}, u32[]{:S(2)}) collective-permute-start(f32[640,128]{1,0:T(8,128)S(1)} %constant_dynamic-slice_fusion.3), channel_id=1, source_target_pairs={{0,1},{1,0},{2,3},{3,2},{4,5},{5,4},{6,7},{7,6},{8,9},{9,8},{10,11... | collective-permute-start | bytes 983048 | tf_op jit(solution)/shard_map/ppermute | solution.py:36
  42.0 4.6 %collective-permute-start.1 = (f32[160,128]{1,0:T(8,128)S(1)}, f32[160,128]{1,0:T(8,128)S(1)}, u32[]{:S(2)}, u32[]{:S(2)}) collective-permute-start(f32[160,128]{1,0:T(8,128)S(1)} %get-tuple-element.11), channel_id=1, source_target_pairs={{0,2},{2,0},{4,6},{6,4},{8,10},{10,8},{12,14},{14,12},{16,18},{18,... | collective-permute-start | bytes 245768 | tf_op jit(solution)/shard_map/ppermute | solution.py:36
  42.6 5.6 %collective-permute-start.2 = (f32[160,128]{1,0:T(8,128)S(1)}, f32[160,128]{1,0:T(8,128)S(1)}, u32[]{:S(2)}, u32[]{:S(2)}) collective-permute-start(f32[160,128]{1,0:T(8,128)S(1)} %get-tuple-element.13), channel_id=1, source_target_pairs={{0,4},{2,6},{4,0},{6,2},{8,12},{10,14},{12,8},{14,10},{16,20},{18,... | collective-permute-start | bytes 245768 | tf_op jit(solution)/shard_map/ppermute | solution.py:36
  44.6 5.3 %collective-permute-start.3 = (f32[160,128]{1,0:T(8,128)S(1)}, f32[160,128]{1,0:T(8,128)S(1)}, u32[]{:S(2)}, u32[]{:S(2)}) collective-permute-start(f32[160,128]{1,0:T(8,128)S(1)} %get-tuple-element.12), channel_id=1, source_target_pairs={{0,6},{2,4},{4,2},{6,0},{8,14},{10,12},{12,10},{14,8},{16,22},{18,... | collective-permute-start | bytes 245768 | tf_op jit(solution)/shard_map/ppermute | solution.py:36
  50.0 4.8 %collective-permute-start.4 = (f32[160,128]{1,0:T(8,128)S(1)}, f32[160,128]{1,0:T(8,128)S(1)}, u32[]{:S(2)}, u32[]{:S(2)}) collective-permute-start(f32[160,128]{1,0:T(8,128)S(1)} %add_add_fusion), channel_id=1, source_target_pairs={{0,8},{2,10},{4,12},{6,14},{8,0},{10,2},{12,4},{14,6},{16,24},{18,... | collective-permute-start | bytes 245768 | tf_op jit(solution)/shard_map/ppermute | solution.py:36
  54.8 5.4 %collective-permute-start.5 = (f32[160,128]{1,0:T(8,128)S(1)}, f32[160,128]{1,0:T(8,128)S(1)}, u32[]{:S(2)}, u32[]{:S(2)}) collective-permute-start(f32[160,128]{1,0:T(8,128)S(1)} %add.64), channel_id=1, source_target_pairs={{0,16},{2,18},{4,20},{6,22},{8,24},{10,26},{12,28},{14,30},{16,0},... | collective-permute-start | bytes 245768 | tf_op jit(solution)/shard_map/ppermute | solution.py:36
  60.2 4.5 %collective-permute-start.6 = (f32[160,128]{1,0:T(8,128)S(1)}, f32[160,128]{1,0:T(8,128)S(1)}, u32[]{:S(2)}, u32[]{:S(2)}) collective-permute-start(f32[160,128]{1,0:T(8,128)S(1)} %get-tuple-element.10), channel_id=1, source_target_pairs={{0,2},{2,0},{4,6},{6,4},{8,10},{10,8},{12,14},{14,12},{16,18},{18,... | collective-permute-start | bytes 245768 | tf_op jit(solution)/shard_map/ppermute | solution.py:36
  61.9 4.4 %collective-permute-start.7 = (f32[160,128]{1,0:T(8,128)S(1)}, f32[160,128]{1,0:T(8,128)S(1)}, u32[]{:S(2)}, u32[]{:S(2)}) collective-permute-start(f32[160,128]{1,0:T(8,128)S(1)} %get-tuple-element.10), channel_id=1, source_target_pairs={{0,4},{2,6},{4,0},{6,2},{8,12},{10,14},{12,8},{14,10},{16,20},{18,... | collective-permute-start | bytes 245768 | tf_op jit(solution)/shard_map/ppermute | solution.py:36
  62.6 5.3 %collective-permute-start.8 = (f32[160,128]{1,0:T(8,128)S(1)}, f32[160,128]{1,0:T(8,128)S(1)}, u32[]{:S(2)}, u32[]{:S(2)}) collective-permute-start(f32[160,128]{1,0:T(8,128)S(1)} %get-tuple-element.10), channel_id=1, source_target_pairs={{0,6},{2,4},{4,2},{6,0},{8,14},{10,12},{12,10},{14,8},{16,22},{18,... | collective-permute-start | bytes 245768 | tf_op jit(solution)/shard_map/ppermute | solution.py:36
  68.0 1.7 %collective-permute-start.9 = (f32[640,128]{1,0:T(8,128)S(1)}, f32[640,128]{1,0:T(8,128)S(1)}, u32[]{:S(2)}, u32[]{:S(2)}) collective-permute-start(f32[640,128]{1,0:T(8,128)S(1)} %constant_dynamic-update-slice_fusion.2), channel_id=1, source_target_pairs={{0,1},{1,0},{2,3},{3,2},{4,5},{5,4},{6,7},{7,6},{8,9},{9,8},{10,11... | collective-permute-start | bytes 983048 | tf_op jit(solution)/shard_map/ppermute | solution.py:36
  68.2 1.6 %copy-start = (f32[512,128]{1,0:T(8,128)S(1)}, f32[512,128]{1,0:T(8,128)}, u32[]{:S(2)}) copy-start(f32[512,128]{1,0:T(8,128)} %initial_ref.1) | copy-start | bytes 786436
  82.1 2.2 %collective-permute-start.10 = (f32[1280,128]{1,0:T(8,128)S(1)}, f32[1280,128]{1,0:T(8,128)S(1)}, u32[]{:S(2)}, u32[]{:S(2)}) collective-permute-start(f32[1280,128]{1,0:T(8,128)S(1)} %shard_map.49.outbox_ref), channel_id=1, source_target_pairs={{0,1},{1,0},{2,3},{3,2},{4,5},{5,4},{6,7},{7,6},{8,9},{9,8},{10,11... | collective-permute-start | bytes 1966088 | tf_op jit(solution)/shard_map/ppermute | solution.py:36

commit v4 on v3

--- a/solution.py
+++ b/solution.py
@@ -214,7 +214,10 @@
         current_t = jnp.concatenate(
             [basis_box[rows + TILE * i : rows + TILE * i + TILE, :] for i in range(tiles)], axis=1
         )
-        core_ref[...] = matmul(current_t, unfold_ref[...])
+        core_flat = matmul(current_t, unfold_ref[...])
+        cells = core_ref.shape[2]
+        for slab in range(core_ref.shape[1]):
+            core_ref[:, slab, :] = core_flat[:, slab * cells : slab * cells + cells]
         basis_ref[...] = basis_box[:rows, :]
         for i in range(tiles):
             for j in range(tiles):
@@ -251,7 +254,7 @@
     )(part, packed, initial)
 
 
-def finished(packed, initial, unfold):
+def finished(packed, initial, unfold, slab_count):
     rows, keep = initial.shape
     if lax.axis_size("col") % 2 == 0:
         part = jnp.full((1,), lax.axis_index("col") % 2, jnp.int32)
@@ -265,7 +268,7 @@
     return pl.pallas_call(
         functools.partial(closing_kernel, rows // TILE),
         out_shape=[
-            jax.ShapeDtypeStruct((keep, unfold.shape[1]), jnp.float32),
+            jax.ShapeDtypeStruct((keep, slab_count, unfold.shape[1] // slab_count), jnp.float32),
             jax.ShapeDtypeStruct((rows, keep), jnp.float32),
             jax.ShapeDtypeStruct((rows, rows), jnp.float32),
         ],
@@ -275,16 +278,36 @@
     )(part, outbox, inbox, unfold)
 
 
+def blocks_kernel(tensor_ref, blocks_ref):
+    count, _, columns = blocks_ref.shape
+    slab_count = tensor_ref.shape[1]
+    cells = columns // slab_count
+    for part in range(count):
+        for slab in range(slab_count):
+            blocks_ref[part, :, slab * cells : slab * cells + cells] = tensor_ref[
+                :, slab, part * cells : part * cells + cells
+            ]
+
+
+def blocks_of(tensor, count):
+    rows, slab_count, width = tensor.shape
+    vmem = pl.BlockSpec(memory_space=pltpu.VMEM)
+    return pl.pallas_call(
+        blocks_kernel,
+        out_shape=jax.ShapeDtypeStruct((count, rows, slab_count * width // count), jnp.float32),
+        in_specs=[vmem],
+        out_specs=vmem,
+        compiler_params=pltpu.CompilerParams(vmem_limit_bytes=VMEM_LIMIT),
+    )(tensor)
+
+
 def local(tensor, initial):
     mode_size = lax.axis_size("mode")
     row_part, slab_count, width = tensor.shape
-    cell_count = width // mode_size
     row_count = row_part * mode_size
     column_total = slab_count * width * lax.axis_size("col")
-    blocks = tensor.reshape(row_part, slab_count, mode_size, cell_count).transpose(2, 0, 1, 3)
-    blocks = blocks.reshape(mode_size, row_part, slab_count * cell_count)
-    regrouped = lax.all_to_all(blocks, "mode", split_axis=0, concat_axis=0, tiled=True)
-    unfold = regrouped.reshape(row_count, slab_count * cell_count)
+    regrouped = lax.all_to_all(blocks_of(tensor, mode_size), "mode", split_axis=0, concat_axis=0, tiled=True)
+    unfold = regrouped.reshape(row_count, slab_count * width // mode_size)
     local_gram = matmul(unfold, unfold.T) / column_total
     packed = jnp.concatenate(
         [
@@ -292,9 +315,7 @@
             for i, j in block_places(row_count // TILE)
         ]
     )
-    core_flat, current, triangle = finished(summed(packed), initial, unfold)
-    core_tensor = core_flat.reshape(current.shape[1], slab_count, cell_count)
-    return (core_tensor, current, triangle)
+    return finished(summed(packed), initial, unfold, slab_count)
 
 
 def solution(mesh):

time: 87.1 us -> 84.2 us (0.967)
  local copies, waits for them, and re-layouts: 5.93 us -> 1.54 us
  Pallas kernels: 14.1 us -> 15.6 us
    reshape x3 -> x0, local copies, waits for them, and re-layouts: 4.8 us -> none  [the longest x1 2.13 us: local(): tensor.reshape(row_part, slab_count, mode_size, cell_count)]
    pallas_call x0 -> x1, Pallas kernels: none -> 1.31 us  [blocks_of(): pl.pallas_call(blocks_kernel, out_shape=jax.ShapeDtypeStruct((count, rows...]
    unnamed x10 -> x12, local copies, waits for them, and re-layouts: 0.09 us -> 1.31 us
where the time goes in v4:
time: 84.2 us; the launch traced here: 83.9 us
  waiting for transfers between devices  43.9 us (52%)
  starting transfers between devices  20 us (24%)
  Pallas kernels  15.6 us (19%)
  matrix products  1.86 us (2%)
  local copies, waits for them, and re-layouts  1.54 us (2%)
  between operations  0.91 us (1%)
    all_to_all x1, waiting for transfers between devices, local(): lax.all_to_all(blocks_of(tensor, mode_size), 'mode', split_axis=0, concat...  24.4 us
    ppermute x11, waiting for transfers between devices, exchanged(): return lax.ppermute(value, axis, pairs)  19.5 us
    pallas_call x1, Pallas kernels, factors(): pl.pallas_call(functools.partial(factor_kernel, tiles), out_shape=jax.Sha...  12.3 us
    ppermute x11, starting transfers between devices, exchanged(): return lax.ppermute(value, axis, pairs)  11.7 us
    all_to_all x1, starting transfers between devices, local(): lax.all_to_all(blocks_of(tensor, mode_size), 'mode', split_axis=0, concat...  8.31 us
    pallas_call x1, Pallas kernels, finished(): pl.pallas_call(functools.partial(closing_kernel, rows // TILE), out_shape...  1.91 us
    dot_general x1, matrix products, matmul(): jnp.dot(left, right, precision=precise, preferred_element_type=jnp.float32)  1.86 us
  transfers between devices with their start and end apart: 12, of which 12 were waited for; matrix products, arithmetic and copies ran while one was open for 0% of the time, Pallas kernels for 0%

profile of v4, /device:TPU:0, one launch (start us, length us, event | category | flops | bytes accessed | tf_op | source)
XLA Modules:
  0.0 83.9 jit_solution(5498892377416456923)
XLA Ops:
  0.6 0.0 copy-start
  0.6 1.2 %copy-done = f32[32,2,4096]{2,1,0:T(2,128)S(1)} copy-done((f32[32,2,4096]{2,1,0:T(2,128)S(1)}, f32[32,2,4096]{2,1,0:T(2,128)}, u32[]{:S(2)}) %copy-start) | copy-done | bytes 1048600
  1.9 1.3 %shard_map.49 = f32[16,32,512]{2,1,0:T(8,128)} custom-call(f32[32,2,4096]{2,1,0:T(2,128)S(1)} %copy-done), custom_call_target="tpu_custom_call" | custom-call | tf_op jit(solution)/shard_map/pallas_call | solution.py:295
  3.2 8.3 %all-to-all-start = ((f32[16,32,512]{2,1,0:T(8,128)}), f32[16,32,512]{2,1,0:T(8,128)S(1)}, u32[]{:S(2)}, u32[]{:S(2)}) async-start(f32[16,32,512]{2,1,0:T(8,128)} %shard_map.49), calls=%async_computation | async-start | bytes 2097152 | tf_op jit(solution)/shard_map/all_to_all | solution.py:309
  11.5 24.4 %all-to-all-done = f32[16,32,512]{2,1,0:T(8,128)S(1)} async-done(((f32[16,32,512]{2,1,0:T(8,128)}), f32[16,32,512]{2,1,0:T(8,128)S(1)}, u32[]{:S(2)}, u32[]{:S(2)}) %all-to-all-start) | async-done | bytes 1048608 | tf_op jit(solution)/shard_map/all_to_all | solution.py:309
  35.9 1.9 %convolution_multiply_fusion = f32[512,512]{1,0:T(8,128)S(1)} fusion(f32[512,512]{1,0:T(8,128)S(1)} %bitcast.4), kind=kOutput, calls=%fused_computation | convolution fusion | flops 1610874880 | bytes 2097152 | tf_op jit(solution)/shard_map/dot_general | solution.py:19
  38.0 0.1 collective-permute-start
  38.1 1.6 %collective-permute-done = f32[640,128]{1,0:T(8,128)S(1)} collective-permute-done((f32[640,128]{1,0:T(8,128)S(1)}, f32[640,128]{1,0:T(8,128)S(1)}, u32[]{:S(2)}, u32[]{:S(2)}) %collective-permute-start) | collective-permute-done | bytes 327712 | tf_op jit(solution)/shard_map/ppermute | solution.py:36
  39.8 0.6 collective-permute-start.1
  40.4 2.0 %collective-permute-start.2 = (f32[160,128]{1,0:T(8,128)S(1)}, f32[160,128]{1,0:T(8,128)S(1)}, u32[]{:S(2)}, u32[]{:S(2)}) collective-permute-start(f32[160,128]{1,0:T(8,128)S(1)} %get-tuple-element.7), channel_id=1, source_target_pairs={{0,4},{2,6},{4,0},{6,2},{8,12},{10,14},{12,8},{14,10},{16,20},{18,... | collective-permute-start | bytes 245768 | tf_op jit(solution)/shard_map/ppermute | solution.py:36
  42.4 1.0 %collective-permute-start.3 = (f32[160,128]{1,0:T(8,128)S(1)}, f32[160,128]{1,0:T(8,128)S(1)}, u32[]{:S(2)}, u32[]{:S(2)}) collective-permute-start(f32[160,128]{1,0:T(8,128)S(1)} %get-tuple-element.6), channel_id=1, source_target_pairs={{0,6},{2,4},{4,2},{6,0},{8,14},{10,12},{12,10},{14,8},{16,22},{18,... | collective-permute-start | bytes 245768 | tf_op jit(solution)/shard_map/ppermute | solution.py:36
  43.3 1.1 %collective-permute-done.1 = f32[160,128]{1,0:T(8,128)S(1)} collective-permute-done((f32[160,128]{1,0:T(8,128)S(1)}, f32[160,128]{1,0:T(8,128)S(1)}, u32[]{:S(2)}, u32[]{:S(2)}) %collective-permute-start.1) | collective-permute-done | bytes 81952 | tf_op jit(solution)/shard_map/ppermute | solution.py:36
  44.4 1.6 %collective-permute-done.2 = f32[160,128]{1,0:T(8,128)S(1)} collective-permute-done((f32[160,128]{1,0:T(8,128)S(1)}, f32[160,128]{1,0:T(8,128)S(1)}, u32[]{:S(2)}, u32[]{:S(2)}) %collective-permute-start.2) | collective-permute-done | bytes 81952 | tf_op jit(solution)/shard_map/ppermute | solution.py:36
  46.0 1.7 %collective-permute-done.3 = f32[160,128]{1,0:T(8,128)S(1)} collective-permute-done((f32[160,128]{1,0:T(8,128)S(1)}, f32[160,128]{1,0:T(8,128)S(1)}, u32[]{:S(2)}, u32[]{:S(2)}) %collective-permute-start.3) | collective-permute-done | bytes 81952 | tf_op jit(solution)/shard_map/ppermute | solution.py:36
  47.7 2.4 %collective-permute-start.4 = (f32[160,128]{1,0:T(8,128)S(1)}, f32[160,128]{1,0:T(8,128)S(1)}, u32[]{:S(2)}, u32[]{:S(2)}) collective-permute-start(f32[160,128]{1,0:T(8,128)S(1)} %add_add_fusion), channel_id=1, source_target_pairs={{0,8},{2,10},{4,12},{6,14},{8,0},{10,2},{12,4},{14,6},{16,24},{18,... | collective-permute-start | bytes 245768 | tf_op jit(solution)/shard_map/ppermute | solution.py:36
  50.1 2.4 %collective-permute-done.4 = f32[160,128]{1,0:T(8,128)S(1)} collective-permute-done((f32[160,128]{1,0:T(8,128)S(1)}, f32[160,128]{1,0:T(8,128)S(1)}, u32[]{:S(2)}, u32[]{:S(2)}) %collective-permute-start.4) | collective-permute-done | bytes 81952 | tf_op jit(solution)/shard_map/ppermute | solution.py:36
  52.6 2.0 %collective-permute-start.5 = (f32[160,128]{1,0:T(8,128)S(1)}, f32[160,128]{1,0:T(8,128)S(1)}, u32[]{:S(2)}, u32[]{:S(2)}) collective-permute-start(f32[160,128]{1,0:T(8,128)S(1)} %add.64), channel_id=1, source_target_pairs={{0,16},{2,18},{4,20},{6,22},{8,24},{10,26},{12,28},{14,30},{16,0},... | collective-permute-start | bytes 245768 | tf_op jit(solution)/shard_map/ppermute | solution.py:36
  54.6 3.4 %collective-permute-done.5 = f32[160,128]{1,0:T(8,128)S(1)} collective-permute-done((f32[160,128]{1,0:T(8,128)S(1)}, f32[160,128]{1,0:T(8,128)S(1)}, u32[]{:S(2)}, u32[]{:S(2)}) %collective-permute-start.5) | collective-permute-done | bytes 81952 | tf_op jit(solution)/shard_map/ppermute | solution.py:36
  58.0 1.7 %collective-permute-start.6 = (f32[160,128]{1,0:T(8,128)S(1)}, f32[160,128]{1,0:T(8,128)S(1)}, u32[]{:S(2)}, u32[]{:S(2)}) collective-permute-start(f32[160,128]{1,0:T(8,128)S(1)} %get-tuple-element.4), channel_id=1, source_target_pairs={{0,2},{2,0},{4,6},{6,4},{8,10},{10,8},{12,14},{14,12},{16,18},{18,... | collective-permute-start | bytes 245768 | tf_op jit(solution)/shard_map/ppermute | solution.py:36
  59.7 0.7 collective-permute-start.7
  60.4 1.2 %collective-permute-start.8 = (f32[160,128]{1,0:T(8,128)S(1)}, f32[160,128]{1,0:T(8,128)S(1)}, u32[]{:S(2)}, u32[]{:S(2)}) collective-permute-start(f32[160,128]{1,0:T(8,128)S(1)} %get-tuple-element.4), channel_id=1, source_target_pairs={{0,6},{2,4},{4,2},{6,0},{8,14},{10,12},{12,10},{14,8},{16,22},{18,... | collective-permute-start | bytes 245768 | tf_op jit(solution)/shard_map/ppermute | solution.py:36
  61.6 1.0 %collective-permute-done.6 = f32[160,128]{1,0:T(8,128)S(1)} collective-permute-done((f32[160,128]{1,0:T(8,128)S(1)}, f32[160,128]{1,0:T(8,128)S(1)}, u32[]{:S(2)}, u32[]{:S(2)}) %collective-permute-start.6) | collective-permute-done | bytes 81952 | tf_op jit(solution)/shard_map/ppermute | solution.py:36
  62.5 1.6 %collective-permute-done.7 = f32[160,128]{1,0:T(8,128)S(1)} collective-permute-done((f32[160,128]{1,0:T(8,128)S(1)}, f32[160,128]{1,0:T(8,128)S(1)}, u32[]{:S(2)}, u32[]{:S(2)}) %collective-permute-start.7) | collective-permute-done | bytes 81952 | tf_op jit(solution)/shard_map/ppermute | solution.py:36
  64.1 1.6 %collective-permute-done.8 = f32[160,128]{1,0:T(8,128)S(1)} collective-permute-done((f32[160,128]{1,0:T(8,128)S(1)}, f32[160,128]{1,0:T(8,128)S(1)}, u32[]{:S(2)}, u32[]{:S(2)}) %collective-permute-start.8) | collective-permute-done | bytes 81952 | tf_op jit(solution)/shard_map/ppermute | solution.py:36
  65.8 0.1 collective-permute-start.9
  65.9 0.0 copy-start.1
  65.9 1.5 %collective-permute-done.9 = f32[640,128]{1,0:T(8,128)S(1)} collective-permute-done((f32[640,128]{1,0:T(8,128)S(1)}, f32[640,128]{1,0:T(8,128)S(1)}, u32[]{:S(2)}, u32[]{:S(2)}) %collective-permute-start.9) | collective-permute-done | bytes 327712 | tf_op jit(solution)/shard_map/ppermute | solution.py:36
  67.5 0.0 copy-done.1
  67.5 12.3 %shard_map.50.outbox_ref = f32[1280,128]{1,0:T(8,128)S(1)} custom-call(s32[1]{0:T(128)} %bitcast.part_ref, f32[1280,128]{1,0:T(8,128)S(1)} %constant_dynamic-update-slice_fusion.packed_ref, f32[512,128]{1,0:T(8,128)S(1)} %copy-done.1), custom_call_target="tpu_custom_call" | custom-call | tf_op jit(solution)/shard_map/pallas_call | solution.py:247
  79.8 0.1 collective-permute-start.10
  79.9 2.1 %collective-permute-done.10.inbox_ref = f32[1280,128]{1,0:T(8,128)S(1)} collective-permute-done((f32[1280,128]{1,0:T(8,128)S(1)}, f32[1280,128]{1,0:T(8,128)S(1)}, u32[]{:S(2)}, u32[]{:S(2)}) %collective-permute-start.10) | collective-permute-done | bytes 655392 | tf_op jit(solution)/shard_map/ppermute | solution.py:36
  82.0 1.9 %shard_map.51 = (f32[128,2,256]{2,1,0:T(2,128)}, f32[512,128]{1,0:T(8,128)}, f32[512,512]{1,0:T(8,128)}) custom-call(s32[1]{0:T(128)} %bitcast.part_ref, f32[1280,128]{1,0:T(8,128)S(1)} %shard_map.50.outbox_ref, f32[1280,128]{1,0:T(8,128)S(1)} %collective-permute-done.10.inbox_ref, f32[512,512]{1,0:T(8,128)S(1)} %bitcast.5), custom_call_target="tpu_custom_call" | custom-call | tf_op jit(solution)/shard_map/pallas_call | solution.py:268
  (22 shorter events, 0.4 us)
Async XLA Ops:
  0.6 1.2 %copy-start = (f32[32,2,4096]{2,1,0:T(2,128)S(1)}, f32[32,2,4096]{2,1,0:T(2,128)}, u32[]{:S(2)}) copy-start(f32[32,2,4096]{2,1,0:T(2,128)} %tensor_ref.1) | copy-start | bytes 3145732
  3.2 32.8 %all-to-all-start = ((f32[16,32,512]{2,1,0:T(8,128)}), f32[16,32,512]{2,1,0:T(8,128)S(1)}, u32[]{:S(2)}, u32[]{:S(2)}) async-start(f32[16,32,512]{2,1,0:T(8,128)} %shard_map.49), calls=%async_computation | async-start | bytes 2097152 | tf_op jit(solution)/shard_map/all_to_all | solution.py:309
  38.0 1.7 %collective-permute-start = (f32[640,128]{1,0:T(8,128)S(1)}, f32[640,128]{1,0:T(8,128)S(1)}, u32[]{:S(2)}, u32[]{:S(2)}) collective-permute-start(f32[640,128]{1,0:T(8,128)S(1)} %constant_dynamic-slice_fusion.3), channel_id=1, source_target_pairs={{0,1},{1,0},{2,3},{3,2},{4,5},{5,4},{6,7},{7,6},{8,9},{9,8},{10,11... | collective-permute-start | bytes 983048 | tf_op jit(solution)/shard_map/ppermute | solution.py:36
  39.8 4.6 %collective-permute-start.1 = (f32[160,128]{1,0:T(8,128)S(1)}, f32[160,128]{1,0:T(8,128)S(1)}, u32[]{:S(2)}, u32[]{:S(2)}) collective-permute-start(f32[160,128]{1,0:T(8,128)S(1)} %get-tuple-element.5), channel_id=1, source_target_pairs={{0,2},{2,0},{4,6},{6,4},{8,10},{10,8},{12,14},{14,12},{16,18},{18,... | collective-permute-start | bytes 245768 | tf_op jit(solution)/shard_map/ppermute | solution.py:36
  40.4 5.6 %collective-permute-start.2 = (f32[160,128]{1,0:T(8,128)S(1)}, f32[160,128]{1,0:T(8,128)S(1)}, u32[]{:S(2)}, u32[]{:S(2)}) collective-permute-start(f32[160,128]{1,0:T(8,128)S(1)} %get-tuple-element.7), channel_id=1, source_target_pairs={{0,4},{2,6},{4,0},{6,2},{8,12},{10,14},{12,8},{14,10},{16,20},{18,... | collective-permute-start | bytes 245768 | tf_op jit(solution)/shard_map/ppermute | solution.py:36
  42.4 5.3 %collective-permute-start.3 = (f32[160,128]{1,0:T(8,128)S(1)}, f32[160,128]{1,0:T(8,128)S(1)}, u32[]{:S(2)}, u32[]{:S(2)}) collective-permute-start(f32[160,128]{1,0:T(8,128)S(1)} %get-tuple-element.6), channel_id=1, source_target_pairs={{0,6},{2,4},{4,2},{6,0},{8,14},{10,12},{12,10},{14,8},{16,22},{18,... | collective-permute-start | bytes 245768 | tf_op jit(solution)/shard_map/ppermute | solution.py:36
  47.7 4.8 %collective-permute-start.4 = (f32[160,128]{1,0:T(8,128)S(1)}, f32[160,128]{1,0:T(8,128)S(1)}, u32[]{:S(2)}, u32[]{:S(2)}) collective-permute-start(f32[160,128]{1,0:T(8,128)S(1)} %add_add_fusion), channel_id=1, source_target_pairs={{0,8},{2,10},{4,12},{6,14},{8,0},{10,2},{12,4},{14,6},{16,24},{18,... | collective-permute-start | bytes 245768 | tf_op jit(solution)/shard_map/ppermute | solution.py:36
  52.6 5.4 %collective-permute-start.5 = (f32[160,128]{1,0:T(8,128)S(1)}, f32[160,128]{1,0:T(8,128)S(1)}, u32[]{:S(2)}, u32[]{:S(2)}) collective-permute-start(f32[160,128]{1,0:T(8,128)S(1)} %add.64), channel_id=1, source_target_pairs={{0,16},{2,18},{4,20},{6,22},{8,24},{10,26},{12,28},{14,30},{16,0},... | collective-permute-start | bytes 245768 | tf_op jit(solution)/shard_map/ppermute | solution.py:36
  58.0 4.5 %collective-permute-start.6 = (f32[160,128]{1,0:T(8,128)S(1)}, f32[160,128]{1,0:T(8,128)S(1)}, u32[]{:S(2)}, u32[]{:S(2)}) collective-permute-start(f32[160,128]{1,0:T(8,128)S(1)} %get-tuple-element.4), channel_id=1, source_target_pairs={{0,2},{2,0},{4,6},{6,4},{8,10},{10,8},{12,14},{14,12},{16,18},{18,... | collective-permute-start | bytes 245768 | tf_op jit(solution)/shard_map/ppermute | solution.py:36
  59.7 4.4 %collective-permute-start.7 = (f32[160,128]{1,0:T(8,128)S(1)}, f32[160,128]{1,0:T(8,128)S(1)}, u32[]{:S(2)}, u32[]{:S(2)}) collective-permute-start(f32[160,128]{1,0:T(8,128)S(1)} %get-tuple-element.4), channel_id=1, source_target_pairs={{0,4},{2,6},{4,0},{6,2},{8,12},{10,14},{12,8},{14,10},{16,20},{18,... | collective-permute-start | bytes 245768 | tf_op jit(solution)/shard_map/ppermute | solution.py:36
  60.4 5.3 %collective-permute-start.8 = (f32[160,128]{1,0:T(8,128)S(1)}, f32[160,128]{1,0:T(8,128)S(1)}, u32[]{:S(2)}, u32[]{:S(2)}) collective-permute-start(f32[160,128]{1,0:T(8,128)S(1)} %get-tuple-element.4), channel_id=1, source_target_pairs={{0,6},{2,4},{4,2},{6,0},{8,14},{10,12},{12,10},{14,8},{16,22},{18,... | collective-permute-start | bytes 245768 | tf_op jit(solution)/shard_map/ppermute | solution.py:36
  65.8 1.7 %collective-permute-start.9 = (f32[640,128]{1,0:T(8,128)S(1)}, f32[640,128]{1,0:T(8,128)S(1)}, u32[]{:S(2)}, u32[]{:S(2)}) collective-permute-start(f32[640,128]{1,0:T(8,128)S(1)} %constant_dynamic-update-slice_fusion.2), channel_id=1, source_target_pairs={{0,1},{1,0},{2,3},{3,2},{4,5},{5,4},{6,7},{7,6},{8,9},{9,8},{10,11... | collective-permute-start | bytes 983048 | tf_op jit(solution)/shard_map/ppermute | solution.py:36
  65.9 1.6 %copy-start.1 = (f32[512,128]{1,0:T(8,128)S(1)}, f32[512,128]{1,0:T(8,128)}, u32[]{:S(2)}) copy-start(f32[512,128]{1,0:T(8,128)} %initial_ref.1) | copy-start | bytes 786436
  79.8 2.2 %collective-permute-start.10 = (f32[1280,128]{1,0:T(8,128)S(1)}, f32[1280,128]{1,0:T(8,128)S(1)}, u32[]{:S(2)}, u32[]{:S(2)}) collective-permute-start(f32[1280,128]{1,0:T(8,128)S(1)} %shard_map.50.outbox_ref), channel_id=1, source_target_pairs={{0,1},{1,0},{2,3},{3,2},{4,5},{5,4},{6,7},{7,6},{8,9},{9,8},{10,11... | collective-permute-start | bytes 1966088 | tf_op jit(solution)/shard_map/ppermute | solution.py:36

commit v5 on v3

--- a/solution.py
+++ b/solution.py
@@ -207,14 +207,21 @@
         write_basis(packed_ref, initial_ref, outbox_ref, gram_ref, tiles)
 
 
-def closing_kernel(tiles, part_ref, outbox_ref, inbox_ref, unfold_ref, core_ref, basis_ref, triangle_ref):
+def closing_kernel(tiles, part_ref, outbox_ref, inbox_ref, *refs):
+    *unfold_refs, core_ref, basis_ref, triangle_ref = refs
+
     def close(triangle_box, basis_box):
         places = block_places(tiles)
         rows = basis_ref.shape[0]
         current_t = jnp.concatenate(
             [basis_box[rows + TILE * i : rows + TILE * i + TILE, :] for i in range(tiles)], axis=1
         )
-        core_ref[...] = matmul(current_t, unfold_ref[...])
+        slabs = core_ref.shape[1] // len(unfold_refs)
+        cells = core_ref.shape[2]
+        for half, unfold_ref in enumerate(unfold_refs):
+            core_flat = matmul(current_t, unfold_ref[...])
+            for slab in range(slabs):
+                core_ref[:, half * slabs + slab, :] = core_flat[:, slab * cells : slab * cells + cells]
         basis_ref[...] = basis_box[:rows, :]
         for i in range(tiles):
             for j in range(tiles):
@@ -251,8 +258,9 @@
     )(part, packed, initial)
 
 
-def finished(packed, initial, unfold):
+def finished(packed, initial, unfolds, slab_count):
     rows, keep = initial.shape
+    columns = sum(unfold.shape[1] for unfold in unfolds)
     if lax.axis_size("col") % 2 == 0:
         part = jnp.full((1,), lax.axis_index("col") % 2, jnp.int32)
         outbox = factors(packed, initial, part)
@@ -265,36 +273,137 @@
     return pl.pallas_call(
         functools.partial(closing_kernel, rows // TILE),
         out_shape=[
-            jax.ShapeDtypeStruct((keep, unfold.shape[1]), jnp.float32),
+            jax.ShapeDtypeStruct((keep, slab_count, columns // slab_count), jnp.float32),
             jax.ShapeDtypeStruct((rows, keep), jnp.float32),
             jax.ShapeDtypeStruct((rows, rows), jnp.float32),
         ],
-        in_specs=[pl.BlockSpec(memory_space=pltpu.SMEM), vmem, vmem, vmem],
+        in_specs=[pl.BlockSpec(memory_space=pltpu.SMEM)] + [vmem] * (2 + len(unfolds)),
         out_specs=[vmem, vmem, vmem],
         compiler_params=pltpu.CompilerParams(vmem_limit_bytes=VMEM_LIMIT),
-    )(part, outbox, inbox, unfold)
+    )(part, outbox, inbox, *unfolds)
+
+
+def digits_of(size):
+    digits, stride = [], 1
+    while stride < size:
+        extent = min(4, size // stride)
+        digits.append((stride, extent))
+        stride *= extent
+    return digits or [(1, 1)]
+
+
+def digit(code, stride_extent):
+    stride, extent = stride_extent
+    return code // stride % extent
+
+
+def blocks_kernel(layout, me_ref, tensor_ref, *out_refs):
+    for (slabs, codes), out_ref in zip(layout, out_refs):
+        cells = out_ref.shape[2] // len(slabs)
+        for at, code in enumerate(codes):
+            start = pl.multiple_of((me_ref[0] ^ code) * cells, cells)
+            for place, slab in enumerate(slabs):
+                out_ref[at, :, place * cells : place * cells + cells] = tensor_ref[:, slab, pl.ds(start, cells)]
+
+
+def blocks_of(tensor, layout, cells, me):
+    rows = tensor.shape[0]
+    vmem = pl.BlockSpec(memory_space=pltpu.VMEM)
+    return pl.pallas_call(
+        functools.partial(blocks_kernel, layout),
+        out_shape=[
+            jax.ShapeDtypeStruct((len(codes), rows, len(slabs) * cells), jnp.float32) for slabs, codes in layout
+        ],
+        in_specs=[pl.BlockSpec(memory_space=pltpu.SMEM), vmem],
+        out_specs=[vmem] * len(layout),
+        compiler_params=pltpu.CompilerParams(vmem_limit_bytes=VMEM_LIMIT),
+    )(me, tensor)
+
+
+def regrouped(tensor, me):
+    size = lax.axis_size("mode")
+    slab_count, width = tensor.shape[1:]
+    digits = digits_of(size)
+    halves = 2 if slab_count % 2 == 0 else 1
+    part = slab_count // halves
+    orders = [digits, digits[::-1]][:halves]
+    layout = [
+        (tuple(range(half * part, half * part + part)), tuple(c for c in range(size) if digit(c, order[0]) == value))
+        for half, order in enumerate(orders)
+        for value in range(order[0][1])
+    ]
+    blocks = iter(blocks_of(tensor, layout, width // size, me))
+    codes_of = iter([codes for _, codes in layout])
+    groups = [[(next(blocks), next(codes_of)) for _ in range(order[0][1])] for order in orders]
+    for step in range(len(digits)):
+        for half in reversed(range(halves)):
+            order = orders[half]
+            if step:
+                pieces = {code: array[at] for array, codes in groups[half] for at, code in enumerate(codes)}
+                groups[half] = []
+                for value in range(order[step][1]):
+                    codes = tuple(c for c in range(size) if digit(c, order[step]) == value)
+                    groups[half].append((jnp.stack([pieces[c] for c in codes]), codes))
+            groups[half] = [
+                (exchanged(array, "mode", value * order[step][0]) if value else array, codes)
+                for value, (array, codes) in reversed(list(enumerate(groups[half])))
+            ]
+    return groups
+
+
+def gram_kernel(codes_of, scale, me_ref, *refs):
+    count = len(codes_of)
+    block_refs, before_refs, (unfold_ref, packed_ref, rows_ref) = refs[:count], refs[count:-3], refs[-3:]
+    for block_ref, codes in zip(block_refs, codes_of):
+        for at, code in enumerate(codes):
+            rows_ref[me_ref[0] ^ code] = block_ref[at]
+    unfold = rows_ref[...].reshape(unfold_ref.shape)
+    unfold_ref[...] = unfold
+    tiles = unfold.shape[0] // TILE
+    places = block_places(tiles)
+    for i in range(tiles):
+        products = matmul_nt(unfold[TILE * i : TILE * i + TILE], unfold[TILE * i :])
+        for j in range(i, tiles):
+            at = places[i, j]
+            share = products[:, TILE * (j - i) : TILE * (j - i) + TILE] * scale
+            for before_ref in before_refs:
+                share = share + before_ref[TILE * at : TILE * at + TILE, :]
+            packed_ref[TILE * at : TILE * at + TILE, :] = share
+
+
+def gram_of(group, before, scale, me):
+    arrays = [array for array, _ in group]
+    codes_of = [codes for _, codes in group]
+    size = sum(len(codes) for codes in codes_of)
+    rows, columns = arrays[0].shape[1:]
+    blocks = len(block_places(size * rows // TILE))
+    vmem = pl.BlockSpec(memory_space=pltpu.VMEM)
+    return pl.pallas_call(
+        functools.partial(gram_kernel, codes_of, scale),
+        out_shape=[
+            jax.ShapeDtypeStruct((size * rows, columns), jnp.float32),
+            jax.ShapeDtypeStruct((blocks * TILE, TILE), jnp.float32),
+        ],
+        in_specs=[pl.BlockSpec(memory_space=pltpu.SMEM)] + [vmem] * (len(arrays) + len(before)),
+        out_specs=[vmem, vmem],
+        scratch_shapes=[pltpu.VMEM((size, rows, columns), jnp.float32)],
+        compiler_params=pltpu.CompilerParams(vmem_limit_bytes=VMEM_LIMIT),
+        cost_estimate=pl.CostEstimate(
+            flops=2 * columns * (size * rows) ** 2, bytes_accessed=8 * size * rows * columns, transcendentals=0
+        ),
+    )(me, *arrays, *before)
 
 
 def local(tensor, initial):
-    mode_size = lax.axis_size("mode")
-    row_part, slab_count, width = tensor.shape
-    cell_count = width // mode_size
-    row_count = row_part * mode_size
+    _, slab_count, width = tensor.shape
     column_total = slab_count * width * lax.axis_size("col")
-    blocks = tensor.reshape(row_part, slab_count, mode_size, cell_count).transpose(2, 0, 1, 3)
-    blocks = blocks.reshape(mode_size, row_part, slab_count * cell_count)
-    regrouped = lax.all_to_all(blocks, "mode", split_axis=0, concat_axis=0, tiled=True)
-    unfold = regrouped.reshape(row_count, slab_count * cell_count)
-    local_gram = matmul(unfold, unfold.T) / column_total
-    packed = jnp.concatenate(
-        [
-            local_gram[i * TILE : (i + 1) * TILE, j * TILE : (j + 1) * TILE]
-            for i, j in block_places(row_count // TILE)
-        ]
-    )
-    core_flat, current, triangle = finished(summed(packed), initial, unfold)
-    core_tensor = core_flat.reshape(current.shape[1], slab_count, cell_count)
-    return (core_tensor, current, triangle)
+    me = jnp.full((1,), lax.axis_index("mode"), jnp.int32)
+    groups = regrouped(tensor, me)
+    unfolds, packed = [None] * len(groups), []
+    for half in reversed(range(len(groups))):
+        unfolds[half], total = gram_of(groups[half], packed, 1.0 / column_total, me)
+        packed = [total]
+    return finished(summed(packed[0]), initial, unfolds, slab_count)
 
 
 def solution(mesh):

time: 87.1 us -> 89.5 us (1.028)
  starting transfers between devices: 20 us -> 34.9 us
  waiting for transfers between devices: 43.9 us -> 34.1 us
  local copies, waits for them, and re-layouts: 5.93 us -> 1.51 us
  Pallas kernels: 14.1 us -> 17.6 us
  matrix products: 1.86 us -> 0 us
    all_to_all x1 -> x0, waiting for transfers between devices: 24.4 us -> none  [local(): lax.all_to_all(blocks, 'mode', split_axis=0, concat_axis=0, tiled=True)]
    ppermute x11 -> x23, starting transfers between devices: 11.7 us -> 34.9 us  [exchanged(): return lax.ppermute(value, axis, pairs)]
    ppermute x11 -> x23, waiting for transfers between devices: 19.5 us -> 34.1 us  [exchanged(): return lax.ppermute(value, axis, pairs)]
    all_to_all x1 -> x0, starting transfers between devices: 8.31 us -> none  [local(): lax.all_to_all(blocks, 'mode', split_axis=0, concat_axis=0, tiled=True)]
    reshape x3 -> x0, local copies, waits for them, and re-layouts: 4.8 us -> none  [the longest x1 2.13 us: local(): tensor.reshape(row_part, slab_count, mode_size, cell_count)]
    pallas_call x0 -> x3, Pallas kernels: none -> 3.38 us  [the longest x2 2.85 us: gram_of(): pl.pallas_call(functools.partial(gram_kernel, codes_of, scale), out_shape...]
    dot_general x1 -> x0, matrix products: 1.86 us -> none  [matmul(): jnp.dot(left, right, precision=precise, preferred_element_type=jnp.float32)]
    unnamed x10 -> x4, local copies, waits for them, and re-layouts: 0.09 us -> 1.22 us
  transfers between devices with their start and end apart: 12 -> 23, of which waited for: 12 -> 14; matrix products, arithmetic and copies ran while one was open for 0% -> 0% of each run, Pallas kernels for 0% -> 2%
where the time goes in v5:
time: 89.5 us; the launch traced here: 89.3 us
  starting transfers between devices  34.9 us (39%)
  waiting for transfers between devices  34.1 us (38%)
  Pallas kernels  17.6 us (20%)
  local copies, waits for them, and re-layouts  1.51 us (2%)
  between operations  0.98 us (1%)
    ppermute x23, starting transfers between devices, exchanged(): return lax.ppermute(value, axis, pairs)  34.9 us
    ppermute x23, waiting for transfers between devices, exchanged(): return lax.ppermute(value, axis, pairs)  34.1 us
    pallas_call x1, Pallas kernels, factors(): pl.pallas_call(functools.partial(factor_kernel, tiles), out_shape=jax.Sha...  12.3 us
    pallas_call x2, Pallas kernels, gram_of(): pl.pallas_call(functools.partial(gram_kernel, codes_of, scale), out_shape...  2.85 us
    pallas_call x1, Pallas kernels, finished(): pl.pallas_call(functools.partial(closing_kernel, rows // TILE), out_shape...  1.91 us
  transfers between devices with their start and end apart: 23, of which 14 were waited for; matrix products, arithmetic and copies ran while one was open for 0% of the time, Pallas kernels for 2%

profile of v5, /device:TPU:0, one launch (start us, length us, event | category | flops | bytes accessed | tf_op | source)
XLA Modules:
  0.0 89.3 jit_solution(4408594399731899389)
XLA Ops:
  0.6 0.0 copy-start
  0.6 1.2 %copy-done = f32[32,2,4096]{2,1,0:T(2,128)S(1)} copy-done((f32[32,2,4096]{2,1,0:T(2,128)S(1)}, f32[32,2,4096]{2,1,0:T(2,128)}, u32[]{:S(2)}) %copy-start) | copy-done | bytes 1048600
  1.9 0.5 shard_map.49
  2.4 3.0 %collective-permute-start = (f32[4,32,256]{2,1,0:T(8,128)S(1)}, f32[4,32,256]{2,1,0:T(8,128)S(1)}, u32[]{:S(2)}, u32[]{:S(2)}) collective-permute-start(f32[4,32,256]{2,1,0:T(8,128)S(1)} %get-tuple-element.16), channel_id=1, source_target_pairs={{0,2},{2,0},{4,6},{6,4},{8,10},{10,8},{12,14},{14,12},{16,18},{18,... | collective-permute-start | bytes 393224 | tf_op jit(solution)/shard_map/ppermute | solution.py:36
  5.4 1.5 %collective-permute-start.1 = (f32[4,32,256]{2,1,0:T(8,128)S(1)}, f32[4,32,256]{2,1,0:T(8,128)S(1)}, u32[]{:S(2)}, u32[]{:S(2)}) collective-permute-start(f32[4,32,256]{2,1,0:T(8,128)S(1)} %get-tuple-element.17), channel_id=1, source_target_pairs={{0,4},{2,6},{4,0},{6,2},{8,12},{10,14},{12,8},{14,10},{16,20},{18,... | collective-permute-start | bytes 393224 | tf_op jit(solution)/shard_map/ppermute | solution.py:36
  6.9 0.0 collective-permute-start.2
  6.9 2.0 %collective-permute-start.6 = (f32[4,32,256]{2,1,0:T(8,128)S(1)}, f32[4,32,256]{2,1,0:T(8,128)S(1)}, u32[]{:S(2)}, u32[]{:S(2)}) collective-permute-start(f32[4,32,256]{2,1,0:T(8,128)S(1)} %get-tuple-element.20), channel_id=1, source_target_pairs={{0,8},{2,10},{4,12},{6,14},{8,0},{10,2},{12,4},{14,6},{16,24},{18,... | collective-permute-start | bytes 393224 | tf_op jit(solution)/shard_map/ppermute | solution.py:36
  9.0 2.6 %collective-permute-start.7 = (f32[4,32,256]{2,1,0:T(8,128)S(1)}, f32[4,32,256]{2,1,0:T(8,128)S(1)}, u32[]{:S(2)}, u32[]{:S(2)}) collective-permute-start(f32[4,32,256]{2,1,0:T(8,128)S(1)} %get-tuple-element.21), channel_id=1, source_target_pairs={{0,16},{2,18},{4,20},{6,22},{8,24},{10,26},{12,28},{14,30},{16,0},... | collective-permute-start | bytes 393224 | tf_op jit(solution)/shard_map/ppermute | solution.py:36
  11.6 0.0 collective-permute-done
  11.6 1.5 %collective-permute-start.8 = (f32[4,32,256]{2,1,0:T(8,128)S(1)}, f32[4,32,256]{2,1,0:T(8,128)S(1)}, u32[]{:S(2)}, u32[]{:S(2)}) collective-permute-start(f32[4,32,256]{2,1,0:T(8,128)S(1)} %get-tuple-element.22), channel_id=1, source_target_pairs={{0,24},{2,26},{4,28},{6,30},{8,16},{10,18},{12,20},{14,22},{16,8},... | collective-permute-start | bytes 393224 | tf_op jit(solution)/shard_map/ppermute | solution.py:36
  13.1 0.0 collective-permute-done.1
  13.2 0.0 collective-permute-done.2
  13.2 3.7 %collective-permute-start.3 = (f32[4,32,256]{2,1,0:T(8,128)S(1)}, f32[4,32,256]{2,1,0:T(8,128)S(1)}, u32[]{:S(2)}, u32[]{:S(2)}) collective-permute-start(f32[4,32,256]{2,1,0:T(8,128)S(1)} %pad_maximum_fusion), channel_id=1, source_target_pairs={{0,24},{2,26},{4,28},{6,30},{8,16},{10,18},{12,20},{14,22},{16,8},... | collective-permute-start | bytes 393224 | tf_op jit(solution)/shard_map/ppermute | solution.py:36
  16.9 0.1 collective-permute-start.4
  17.0 0.0 collective-permute-done.6
  17.0 0.8 collective-permute-start.5
  17.9 8.9 %collective-permute-done.7 = f32[4,32,256]{2,1,0:T(8,128)S(1)} collective-permute-done((f32[4,32,256]{2,1,0:T(8,128)S(1)}, f32[4,32,256]{2,1,0:T(8,128)S(1)}, u32[]{:S(2)}, u32[]{:S(2)}) %collective-permute-start.7) | collective-permute-done | bytes 131104 | tf_op jit(solution)/shard_map/ppermute | solution.py:36
  26.8 0.0 collective-permute-done.8
  26.8 2.5 %collective-permute-start.9 = (f32[4,32,256]{2,1,0:T(8,128)S(1)}, f32[4,32,256]{2,1,0:T(8,128)S(1)}, u32[]{:S(2)}, u32[]{:S(2)}) collective-permute-start(f32[4,32,256]{2,1,0:T(8,128)S(1)} %pad_maximum_fusion.4), channel_id=1, source_target_pairs={{0,6},{2,4},{4,2},{6,0},{8,14},{10,12},{12,10},{14,8},{16,22},{18,... | collective-permute-start | bytes 393224 | tf_op jit(solution)/shard_map/ppermute | solution.py:36
  29.4 0.6 collective-permute-start.10
  29.9 2.8 %collective-permute-done.9.refs_0_ = f32[4,32,256]{2,1,0:T(8,128)S(1)} collective-permute-done((f32[4,32,256]{2,1,0:T(8,128)S(1)}, f32[4,32,256]{2,1,0:T(8,128)S(1)}, u32[]{:S(2)}, u32[]{:S(2)}) %collective-permute-start.9) | collective-permute-done | bytes 131104 | tf_op jit(solution)/shard_map/ppermute | solution.py:36
  32.8 1.6 %collective-permute-start.11 = (f32[4,32,256]{2,1,0:T(8,128)S(1)}, f32[4,32,256]{2,1,0:T(8,128)S(1)}, u32[]{:S(2)}, u32[]{:S(2)}) collective-permute-start(f32[4,32,256]{2,1,0:T(8,128)S(1)} %pad_maximum_fusion.6), channel_id=1, source_target_pairs={{0,2},{2,0},{4,6},{6,4},{8,10},{10,8},{12,14},{14,12},{16,18},{18,... | collective-permute-start | bytes 393224 | tf_op jit(solution)/shard_map/ppermute | solution.py:36
  34.4 0.0 collective-permute-done.10.refs_1_
  34.4 3.3 %collective-permute-done.11.refs_2_ = f32[4,32,256]{2,1,0:T(8,128)S(1)} collective-permute-done((f32[4,32,256]{2,1,0:T(8,128)S(1)}, f32[4,32,256]{2,1,0:T(8,128)S(1)}, u32[]{:S(2)}, u32[]{:S(2)}) %collective-permute-start.11) | collective-permute-done | bytes 131104 | tf_op jit(solution)/shard_map/ppermute | solution.py:36
  37.7 1.4 %shard_map.50 = (f32[512,256]{1,0:T(8,128)S(1)}, f32[1280,128]{1,0:T(8,128)S(1)}) custom-call(s32[1]{0:T(128)} %bitcast.1.me_ref, f32[4,32,256]{2,1,0:T(8,128)S(1)} %collective-permute-done.9.refs_0_, f32[4,32,256]{2,1,0:T(8,128)S(1)} %collective-permute-done.10.refs_1_, f32[4,32,256]{2,1,0:T(8,128)S(1)} %collective-permute-done.11.refs_2_, ...), custom_call_target="tpu_custom_call" | custom-call | flops 134217728 | bytes 1048576 | tf_op jit(solution)/shard_map/pallas_call | solution.py:381
  39.1 0.0 collective-permute-done.3.refs_0_
  39.2 0.0 collective-permute-done.4.refs_1_
  39.2 0.0 collective-permute-done.5.refs_2_
  39.2 1.4 %shard_map.51 = (f32[512,256]{1,0:T(8,128)S(1)}, f32[1280,128]{1,0:T(8,128)S(1)}) custom-call(s32[1]{0:T(128)} %bitcast.1.me_ref, f32[4,32,256]{2,1,0:T(8,128)S(1)} %collective-permute-done.3.refs_0_, f32[4,32,256]{2,1,0:T(8,128)S(1)} %collective-permute-done.4.refs_1_, f32[4,32,256]{2,1,0:T(8,128)S(1)} %collective-permute-done.5.refs_2_, ...), custom_call_target="tpu_custom_call" | custom-call | flops 134217728 | bytes 1048576 | tf_op jit(solution)/shard_map/pallas_call | solution.py:381
  40.7 0.1 collective-permute-start.12
  40.8 1.6 %collective-permute-done.12 = f32[640,128]{1,0:T(8,128)S(1)} collective-permute-done((f32[640,128]{1,0:T(8,128)S(1)}, f32[640,128]{1,0:T(8,128)S(1)}, u32[]{:S(2)}, u32[]{:S(2)}) %collective-permute-start.12) | collective-permute-done | bytes 327712 | tf_op jit(solution)/shard_map/ppermute | solution.py:36
  42.4 1.6 %collective-permute-start.13 = (f32[160,128]{1,0:T(8,128)S(1)}, f32[160,128]{1,0:T(8,128)S(1)}, u32[]{:S(2)}, u32[]{:S(2)}) collective-permute-start(f32[160,128]{1,0:T(8,128)S(1)} %get-tuple-element.29), channel_id=1, source_target_pairs={{0,2},{2,0},{4,6},{6,4},{8,10},{10,8},{12,14},{14,12},{16,18},{18,... | collective-permute-start | bytes 245768 | tf_op jit(solution)/shard_map/ppermute | solution.py:36
  44.1 1.5 %collective-permute-start.15 = (f32[160,128]{1,0:T(8,128)S(1)}, f32[160,128]{1,0:T(8,128)S(1)}, u32[]{:S(2)}, u32[]{:S(2)}) collective-permute-start(f32[160,128]{1,0:T(8,128)S(1)} %get-tuple-element.30), channel_id=1, source_target_pairs={{0,6},{2,4},{4,2},{6,0},{8,14},{10,12},{12,10},{14,8},{16,22},{18,... | collective-permute-start | bytes 245768 | tf_op jit(solution)/shard_map/ppermute | solution.py:36
  45.6 0.4 collective-permute-start.14
  46.0 1.0 %collective-permute-done.13 = f32[160,128]{1,0:T(8,128)S(1)} collective-permute-done((f32[160,128]{1,0:T(8,128)S(1)}, f32[160,128]{1,0:T(8,128)S(1)}, u32[]{:S(2)}, u32[]{:S(2)}) %collective-permute-start.13) | collective-permute-done | bytes 81952 | tf_op jit(solution)/shard_map/ppermute | solution.py:36
  47.0 2.9 %collective-permute-done.15 = f32[160,128]{1,0:T(8,128)S(1)} collective-permute-done((f32[160,128]{1,0:T(8,128)S(1)}, f32[160,128]{1,0:T(8,128)S(1)}, u32[]{:S(2)}, u32[]{:S(2)}) %collective-permute-start.15) | collective-permute-done | bytes 81952 | tf_op jit(solution)/shard_map/ppermute | solution.py:36
  49.9 1.2 %collective-permute-done.14 = f32[160,128]{1,0:T(8,128)S(1)} collective-permute-done((f32[160,128]{1,0:T(8,128)S(1)}, f32[160,128]{1,0:T(8,128)S(1)}, u32[]{:S(2)}, u32[]{:S(2)}) %collective-permute-start.14) | collective-permute-done | bytes 81952 | tf_op jit(solution)/shard_map/ppermute | solution.py:36
  51.1 4.6 %collective-permute-start.16 = (f32[160,128]{1,0:T(8,128)S(1)}, f32[160,128]{1,0:T(8,128)S(1)}, u32[]{:S(2)}, u32[]{:S(2)}) collective-permute-start(f32[160,128]{1,0:T(8,128)S(1)} %add_add_fusion), channel_id=1, source_target_pairs={{0,8},{2,10},{4,12},{6,14},{8,0},{10,2},{12,4},{14,6},{16,24},{18,... | collective-permute-start | bytes 245768 | tf_op jit(solution)/shard_map/ppermute | solution.py:36
  55.7 2.4 %collective-permute-done.16 = f32[160,128]{1,0:T(8,128)S(1)} collective-permute-done((f32[160,128]{1,0:T(8,128)S(1)}, f32[160,128]{1,0:T(8,128)S(1)}, u32[]{:S(2)}, u32[]{:S(2)}) %collective-permute-start.16) | collective-permute-done | bytes 81952 | tf_op jit(solution)/shard_map/ppermute | solution.py:36
  58.2 3.0 %collective-permute-start.17 = (f32[160,128]{1,0:T(8,128)S(1)}, f32[160,128]{1,0:T(8,128)S(1)}, u32[]{:S(2)}, u32[]{:S(2)}) collective-permute-start(f32[160,128]{1,0:T(8,128)S(1)} %add.64), channel_id=1, source_target_pairs={{0,16},{2,18},{4,20},{6,22},{8,24},{10,26},{12,28},{14,30},{16,0},... | collective-permute-start | bytes 245768 | tf_op jit(solution)/shard_map/ppermute | solution.py:36
  61.2 2.4 %collective-permute-done.17 = f32[160,128]{1,0:T(8,128)S(1)} collective-permute-done((f32[160,128]{1,0:T(8,128)S(1)}, f32[160,128]{1,0:T(8,128)S(1)}, u32[]{:S(2)}, u32[]{:S(2)}) %collective-permute-start.17) | collective-permute-done | bytes 81952 | tf_op jit(solution)/shard_map/ppermute | solution.py:36
  63.7 1.6 %collective-permute-start.18 = (f32[160,128]{1,0:T(8,128)S(1)}, f32[160,128]{1,0:T(8,128)S(1)}, u32[]{:S(2)}, u32[]{:S(2)}) collective-permute-start(f32[160,128]{1,0:T(8,128)S(1)} %get-tuple-element.28), channel_id=1, source_target_pairs={{0,2},{2,0},{4,6},{6,4},{8,10},{10,8},{12,14},{14,12},{16,18},{18,... | collective-permute-start | bytes 245768 | tf_op jit(solution)/shard_map/ppermute | solution.py:36
  65.2 0.6 collective-permute-start.19
  65.8 1.4 %collective-permute-start.20 = (f32[160,128]{1,0:T(8,128)S(1)}, f32[160,128]{1,0:T(8,128)S(1)}, u32[]{:S(2)}, u32[]{:S(2)}) collective-permute-start(f32[160,128]{1,0:T(8,128)S(1)} %get-tuple-element.28), channel_id=1, source_target_pairs={{0,6},{2,4},{4,2},{6,0},{8,14},{10,12},{12,10},{14,8},{16,22},{18,... | collective-permute-start | bytes 245768 | tf_op jit(solution)/shard_map/ppermute | solution.py:36
  67.2 1.0 %collective-permute-done.18 = f32[160,128]{1,0:T(8,128)S(1)} collective-permute-done((f32[160,128]{1,0:T(8,128)S(1)}, f32[160,128]{1,0:T(8,128)S(1)}, u32[]{:S(2)}, u32[]{:S(2)}) %collective-permute-start.18) | collective-permute-done | bytes 81952 | tf_op jit(solution)/shard_map/ppermute | solution.py:36
  68.2 1.5 %collective-permute-done.19 = f32[160,128]{1,0:T(8,128)S(1)} collective-permute-done((f32[160,128]{1,0:T(8,128)S(1)}, f32[160,128]{1,0:T(8,128)S(1)}, u32[]{:S(2)}, u32[]{:S(2)}) %collective-permute-start.19) | collective-permute-done | bytes 81952 | tf_op jit(solution)/shard_map/ppermute | solution.py:36
  69.7 1.5 %collective-permute-done.20 = f32[160,128]{1,0:T(8,128)S(1)} collective-permute-done((f32[160,128]{1,0:T(8,128)S(1)}, f32[160,128]{1,0:T(8,128)S(1)}, u32[]{:S(2)}, u32[]{:S(2)}) %collective-permute-start.20) | collective-permute-done | bytes 81952 | tf_op jit(solution)/shard_map/ppermute | solution.py:36
  71.1 0.1 collective-permute-start.21
  71.3 0.0 copy-start.1
  71.3 1.5 %collective-permute-done.21 = f32[640,128]{1,0:T(8,128)S(1)} collective-permute-done((f32[640,128]{1,0:T(8,128)S(1)}, f32[640,128]{1,0:T(8,128)S(1)}, u32[]{:S(2)}, u32[]{:S(2)}) %collective-permute-start.21) | collective-permute-done | bytes 327712 | tf_op jit(solution)/shard_map/ppermute | solution.py:36
  72.9 0.0 copy-done.1
  72.9 12.3 %shard_map.52.outbox_ref = f32[1280,128]{1,0:T(8,128)S(1)} custom-call(s32[1]{0:T(128)} %bitcast.part_ref, f32[1280,128]{1,0:T(8,128)S(1)} %constant_dynamic-update-slice_fusion.packed_ref, f32[512,128]{1,0:T(8,128)S(1)} %copy-done.1), custom_call_target="tpu_custom_call" | custom-call | tf_op jit(solution)/shard_map/pallas_call | solution.py:251
  85.2 0.1 collective-permute-start.22
  85.3 2.1 %collective-permute-done.22.inbox_ref = f32[1280,128]{1,0:T(8,128)S(1)} collective-permute-done((f32[1280,128]{1,0:T(8,128)S(1)}, f32[1280,128]{1,0:T(8,128)S(1)}, u32[]{:S(2)}, u32[]{:S(2)}) %collective-permute-start.22) | collective-permute-done | bytes 655392 | tf_op jit(solution)/shard_map/ppermute | solution.py:36
  87.4 1.9 %shard_map.53 = (f32[128,2,256]{2,1,0:T(2,128)}, f32[512,128]{1,0:T(8,128)}, f32[512,512]{1,0:T(8,128)}) custom-call(s32[1]{0:T(128)} %bitcast.part_ref, f32[1280,128]{1,0:T(8,128)S(1)} %shard_map.52.outbox_ref, f32[1280,128]{1,0:T(8,128)S(1)} %collective-permute-done.22.inbox_ref, f32[512,256]{1,0:T(8,128)S(1)} %get-tuple-element.25.refs_0_, ...), custom_call_target="tpu_custom_call" | custom-call | tf_op jit(solution)/shard_map/pallas_call | solution.py:273
  (28 shorter events, 0.5 us)
Async XLA Ops:
  0.6 1.2 %copy-start = (f32[32,2,4096]{2,1,0:T(2,128)S(1)}, f32[32,2,4096]{2,1,0:T(2,128)}, u32[]{:S(2)}) copy-start(f32[32,2,4096]{2,1,0:T(2,128)} %tensor_ref.1) | copy-start | bytes 3145732
  2.4 9.2 %collective-permute-start = (f32[4,32,256]{2,1,0:T(8,128)S(1)}, f32[4,32,256]{2,1,0:T(8,128)S(1)}, u32[]{:S(2)}, u32[]{:S(2)}) collective-permute-start(f32[4,32,256]{2,1,0:T(8,128)S(1)} %get-tuple-element.16), channel_id=1, source_target_pairs={{0,2},{2,0},{4,6},{6,4},{8,10},{10,8},{12,14},{14,12},{16,18},{18,... | collective-permute-start | bytes 393224 | tf_op jit(solution)/shard_map/ppermute | solution.py:36
  5.4 7.8 %collective-permute-start.1 = (f32[4,32,256]{2,1,0:T(8,128)S(1)}, f32[4,32,256]{2,1,0:T(8,128)S(1)}, u32[]{:S(2)}, u32[]{:S(2)}) collective-permute-start(f32[4,32,256]{2,1,0:T(8,128)S(1)} %get-tuple-element.17), channel_id=1, source_target_pairs={{0,4},{2,6},{4,0},{6,2},{8,12},{10,14},{12,8},{14,10},{16,20},{18,... | collective-permute-start | bytes 393224 | tf_op jit(solution)/shard_map/ppermute | solution.py:36
  6.9 6.3 %collective-permute-start.2 = (f32[4,32,256]{2,1,0:T(8,128)S(1)}, f32[4,32,256]{2,1,0:T(8,128)S(1)}, u32[]{:S(2)}, u32[]{:S(2)}) collective-permute-start(f32[4,32,256]{2,1,0:T(8,128)S(1)} %get-tuple-element.18), channel_id=1, source_target_pairs={{0,6},{2,4},{4,2},{6,0},{8,14},{10,12},{12,10},{14,8},{16,22},{18,... | collective-permute-start | bytes 393224 | tf_op jit(solution)/shard_map/ppermute | solution.py:36
  6.9 10.1 %collective-permute-start.6 = (f32[4,32,256]{2,1,0:T(8,128)S(1)}, f32[4,32,256]{2,1,0:T(8,128)S(1)}, u32[]{:S(2)}, u32[]{:S(2)}) collective-permute-start(f32[4,32,256]{2,1,0:T(8,128)S(1)} %get-tuple-element.20), channel_id=1, source_target_pairs={{0,8},{2,10},{4,12},{6,14},{8,0},{10,2},{12,4},{14,6},{16,24},{18,... | collective-permute-start | bytes 393224 | tf_op jit(solution)/shard_map/ppermute | solution.py:36
  9.0 17.8 %collective-permute-start.7 = (f32[4,32,256]{2,1,0:T(8,128)S(1)}, f32[4,32,256]{2,1,0:T(8,128)S(1)}, u32[]{:S(2)}, u32[]{:S(2)}) collective-permute-start(f32[4,32,256]{2,1,0:T(8,128)S(1)} %get-tuple-element.21), channel_id=1, source_target_pairs={{0,16},{2,18},{4,20},{6,22},{8,24},{10,26},{12,28},{14,30},{16,0},... | collective-permute-start | bytes 393224 | tf_op jit(solution)/shard_map/ppermute | solution.py:36
  11.6 15.2 %collective-permute-start.8 = (f32[4,32,256]{2,1,0:T(8,128)S(1)}, f32[4,32,256]{2,1,0:T(8,128)S(1)}, u32[]{:S(2)}, u32[]{:S(2)}) collective-permute-start(f32[4,32,256]{2,1,0:T(8,128)S(1)} %get-tuple-element.22), channel_id=1, source_target_pairs={{0,24},{2,26},{4,28},{6,30},{8,16},{10,18},{12,20},{14,22},{16,8},... | collective-permute-start | bytes 393224 | tf_op jit(solution)/shard_map/ppermute | solution.py:36
  13.2 25.9 %collective-permute-start.3 = (f32[4,32,256]{2,1,0:T(8,128)S(1)}, f32[4,32,256]{2,1,0:T(8,128)S(1)}, u32[]{:S(2)}, u32[]{:S(2)}) collective-permute-start(f32[4,32,256]{2,1,0:T(8,128)S(1)} %pad_maximum_fusion), channel_id=1, source_target_pairs={{0,24},{2,26},{4,28},{6,30},{8,16},{10,18},{12,20},{14,22},{16,8},... | collective-permute-start | bytes 393224 | tf_op jit(solution)/shard_map/ppermute | solution.py:36
  16.9 22.2 %collective-permute-start.4 = (f32[4,32,256]{2,1,0:T(8,128)S(1)}, f32[4,32,256]{2,1,0:T(8,128)S(1)}, u32[]{:S(2)}, u32[]{:S(2)}) collective-permute-start(f32[4,32,256]{2,1,0:T(8,128)S(1)} %pad_maximum_fusion.1), channel_id=1, source_target_pairs={{0,16},{2,18},{4,20},{6,22},{8,24},{10,26},{12,28},{14,30},{16,0},... | collective-permute-start | bytes 393224 | tf_op jit(solution)/shard_map/ppermute | solution.py:36
  17.0 22.1 %collective-permute-start.5 = (f32[4,32,256]{2,1,0:T(8,128)S(1)}, f32[4,32,256]{2,1,0:T(8,128)S(1)}, u32[]{:S(2)}, u32[]{:S(2)}) collective-permute-start(f32[4,32,256]{2,1,0:T(8,128)S(1)} %pad_maximum_fusion.2), channel_id=1, source_target_pairs={{0,8},{2,10},{4,12},{6,14},{8,0},{10,2},{12,4},{14,6},{16,24},{18,... | collective-permute-start | bytes 393224 | tf_op jit(solution)/shard_map/ppermute | solution.py:36
  26.8 5.9 %collective-permute-start.9 = (f32[4,32,256]{2,1,0:T(8,128)S(1)}, f32[4,32,256]{2,1,0:T(8,128)S(1)}, u32[]{:S(2)}, u32[]{:S(2)}) collective-permute-start(f32[4,32,256]{2,1,0:T(8,128)S(1)} %pad_maximum_fusion.4), channel_id=1, source_target_pairs={{0,6},{2,4},{4,2},{6,0},{8,14},{10,12},{12,10},{14,8},{16,22},{18,... | collective-permute-start | bytes 393224 | tf_op jit(solution)/shard_map/ppermute | solution.py:36
  29.4 5.0 %collective-permute-start.10 = (f32[4,32,256]{2,1,0:T(8,128)S(1)}, f32[4,32,256]{2,1,0:T(8,128)S(1)}, u32[]{:S(2)}, u32[]{:S(2)}) collective-permute-start(f32[4,32,256]{2,1,0:T(8,128)S(1)} %pad_maximum_fusion.5), channel_id=1, source_target_pairs={{0,4},{2,6},{4,0},{6,2},{8,12},{10,14},{12,8},{14,10},{16,20},{18,... | collective-permute-start | bytes 393224 | tf_op jit(solution)/shard_map/ppermute | solution.py:36
  32.8 5.0 %collective-permute-start.11 = (f32[4,32,256]{2,1,0:T(8,128)S(1)}, f32[4,32,256]{2,1,0:T(8,128)S(1)}, u32[]{:S(2)}, u32[]{:S(2)}) collective-permute-start(f32[4,32,256]{2,1,0:T(8,128)S(1)} %pad_maximum_fusion.6), channel_id=1, source_target_pairs={{0,2},{2,0},{4,6},{6,4},{8,10},{10,8},{12,14},{14,12},{16,18},{18,... | collective-permute-start | bytes 393224 | tf_op jit(solution)/shard_map/ppermute | solution.py:36
  40.7 1.7 %collective-permute-start.12 = (f32[640,128]{1,0:T(8,128)S(1)}, f32[640,128]{1,0:T(8,128)S(1)}, u32[]{:S(2)}, u32[]{:S(2)}) collective-permute-start(f32[640,128]{1,0:T(8,128)S(1)} %constant_dynamic-slice_fusion.3), channel_id=1, source_target_pairs={{0,1},{1,0},{2,3},{3,2},{4,5},{5,4},{6,7},{7,6},{8,9},{9,8},{10,11... | collective-permute-start | bytes 983048 | tf_op jit(solution)/shard_map/ppermute | solution.py:36
  42.4 4.6 %collective-permute-start.13 = (f32[160,128]{1,0:T(8,128)S(1)}, f32[160,128]{1,0:T(8,128)S(1)}, u32[]{:S(2)}, u32[]{:S(2)}) collective-permute-start(f32[160,128]{1,0:T(8,128)S(1)} %get-tuple-element.29), channel_id=1, source_target_pairs={{0,2},{2,0},{4,6},{6,4},{8,10},{10,8},{12,14},{14,12},{16,18},{18,... | collective-permute-start | bytes 245768 | tf_op jit(solution)/shard_map/ppermute | solution.py:36
  44.1 5.8 %collective-permute-start.15 = (f32[160,128]{1,0:T(8,128)S(1)}, f32[160,128]{1,0:T(8,128)S(1)}, u32[]{:S(2)}, u32[]{:S(2)}) collective-permute-start(f32[160,128]{1,0:T(8,128)S(1)} %get-tuple-element.30), channel_id=1, source_target_pairs={{0,6},{2,4},{4,2},{6,0},{8,14},{10,12},{12,10},{14,8},{16,22},{18,... | collective-permute-start | bytes 245768 | tf_op jit(solution)/shard_map/ppermute | solution.py:36
  45.6 5.5 %collective-permute-start.14 = (f32[160,128]{1,0:T(8,128)S(1)}, f32[160,128]{1,0:T(8,128)S(1)}, u32[]{:S(2)}, u32[]{:S(2)}) collective-permute-start(f32[160,128]{1,0:T(8,128)S(1)} %get-tuple-element.31), channel_id=1, source_target_pairs={{0,4},{2,6},{4,0},{6,2},{8,12},{10,14},{12,8},{14,10},{16,20},{18,... | collective-permute-start | bytes 245768 | tf_op jit(solution)/shard_map/ppermute | solution.py:36
  51.1 7.0 %collective-permute-start.16 = (f32[160,128]{1,0:T(8,128)S(1)}, f32[160,128]{1,0:T(8,128)S(1)}, u32[]{:S(2)}, u32[]{:S(2)}) collective-permute-start(f32[160,128]{1,0:T(8,128)S(1)} %add_add_fusion), channel_id=1, source_target_pairs={{0,8},{2,10},{4,12},{6,14},{8,0},{10,2},{12,4},{14,6},{16,24},{18,... | collective-permute-start | bytes 245768 | tf_op jit(solution)/shard_map/ppermute | solution.py:36
  58.2 5.4 %collective-permute-start.17 = (f32[160,128]{1,0:T(8,128)S(1)}, f32[160,128]{1,0:T(8,128)S(1)}, u32[]{:S(2)}, u32[]{:S(2)}) collective-permute-start(f32[160,128]{1,0:T(8,128)S(1)} %add.64), channel_id=1, source_target_pairs={{0,16},{2,18},{4,20},{6,22},{8,24},{10,26},{12,28},{14,30},{16,0},... | collective-permute-start | bytes 245768 | tf_op jit(solution)/shard_map/ppermute | solution.py:36
  63.7 4.5 %collective-permute-start.18 = (f32[160,128]{1,0:T(8,128)S(1)}, f32[160,128]{1,0:T(8,128)S(1)}, u32[]{:S(2)}, u32[]{:S(2)}) collective-permute-start(f32[160,128]{1,0:T(8,128)S(1)} %get-tuple-element.28), channel_id=1, source_target_pairs={{0,2},{2,0},{4,6},{6,4},{8,10},{10,8},{12,14},{14,12},{16,18},{18,... | collective-permute-start | bytes 245768 | tf_op jit(solution)/shard_map/ppermute | solution.py:36
  65.2 4.4 %collective-permute-start.19 = (f32[160,128]{1,0:T(8,128)S(1)}, f32[160,128]{1,0:T(8,128)S(1)}, u32[]{:S(2)}, u32[]{:S(2)}) collective-permute-start(f32[160,128]{1,0:T(8,128)S(1)} %get-tuple-element.28), channel_id=1, source_target_pairs={{0,4},{2,6},{4,0},{6,2},{8,12},{10,14},{12,8},{14,10},{16,20},{18,... | collective-permute-start | bytes 245768 | tf_op jit(solution)/shard_map/ppermute | solution.py:36
  65.8 5.3 %collective-permute-start.20 = (f32[160,128]{1,0:T(8,128)S(1)}, f32[160,128]{1,0:T(8,128)S(1)}, u32[]{:S(2)}, u32[]{:S(2)}) collective-permute-start(f32[160,128]{1,0:T(8,128)S(1)} %get-tuple-element.28), channel_id=1, source_target_pairs={{0,6},{2,4},{4,2},{6,0},{8,14},{10,12},{12,10},{14,8},{16,22},{18,... | collective-permute-start | bytes 245768 | tf_op jit(solution)/shard_map/ppermute | solution.py:36
  71.1 1.7 %collective-permute-start.21 = (f32[640,128]{1,0:T(8,128)S(1)}, f32[640,128]{1,0:T(8,128)S(1)}, u32[]{:S(2)}, u32[]{:S(2)}) collective-permute-start(f32[640,128]{1,0:T(8,128)S(1)} %constant_dynamic-update-slice_fusion.2), channel_id=1, source_target_pairs={{0,1},{1,0},{2,3},{3,2},{4,5},{5,4},{6,7},{7,6},{8,9},{9,8},{10,11... | collective-permute-start | bytes 983048 | tf_op jit(solution)/shard_map/ppermute | solution.py:36
  71.3 1.6 %copy-start.1 = (f32[512,128]{1,0:T(8,128)S(1)}, f32[512,128]{1,0:T(8,128)}, u32[]{:S(2)}) copy-start(f32[512,128]{1,0:T(8,128)} %initial_ref.1) | copy-start | bytes 786436
  85.2 2.2 %collective-permute-start.22 = (f32[1280,128]{1,0:T(8,128)S(1)}, f32[1280,128]{1,0:T(8,128)S(1)}, u32[]{:S(2)}, u32[]{:S(2)}) collective-permute-start(f32[1280,128]{1,0:T(8,128)S(1)} %shard_map.52.outbox_ref), channel_id=1, source_target_pairs={{0,1},{1,0},{2,3},{3,2},{4,5},{5,4},{6,7},{7,6},{8,9},{9,8},{10,11... | collective-permute-start | bytes 1966088 | tf_op jit(solution)/shard_map/ppermute | solution.py:36

commit v6 on v4

--- a/solution.py
+++ b/solution.py
@@ -60,22 +60,21 @@
     return whole
 
 
-def summed(value):
+def summed(share, other_share=None):
     mode_size, col_size = lax.axis_size("mode"), lax.axis_size("col")
-    col_group = min(2, col_size)
     mode_group = min(4, mode_size)
-    value = scattered_sum(value, "col", col_group)
+    value = share if other_share is None else share + exchanged(other_share, "col", 1)
     value = scattered_sum(value, "mode", mode_group)
     distance = mode_group
     while distance < mode_size:
         value = value + exchanged(value, "mode", distance)
         distance *= 2
-    distance = col_group
+    distance = 1 if other_share is None else 2
     while distance < col_size:
         value = value + exchanged(value, "col", distance)
         distance *= 2
     value = gathered(value, "mode", mode_group)
-    return gathered(value, "col", col_group)
+    return value if other_share is None else gathered(value, "col", 2)
 
 
 def row_of(tile, index):
@@ -207,10 +206,23 @@
         write_basis(packed_ref, initial_ref, outbox_ref, gram_ref, tiles)
 
 
-def closing_kernel(tiles, part_ref, outbox_ref, inbox_ref, unfold_ref, core_ref, basis_ref, triangle_ref):
+def closing_kernel(
+    tiles, part_ref, outbox_ref, inbox_ref, unfold_ref, core_ref, basis_ref, triangle_ref, zero_ref, semaphores
+):
     def close(triangle_box, basis_box):
         places = block_places(tiles)
         rows = basis_ref.shape[0]
+        copies = [(basis_box.at[pl.ds(0, rows)], basis_ref)]
+        for i in range(tiles):
+            for j in range(tiles):
+                at = places.get((i, j))
+                source = zero_ref if at is None else triangle_box.at[pl.ds(TILE * at, TILE)]
+                copies.append((source, triangle_ref.at[pl.ds(TILE * i, TILE), pl.ds(TILE * j, TILE)]))
+        copies = [
+            pltpu.make_async_copy(source, target, semaphores.at[n]) for n, (source, target) in enumerate(copies)
+        ]
+        for copy in copies:
+            copy.start()
         current_t = jnp.concatenate(
             [basis_box[rows + TILE * i : rows + TILE * i + TILE, :] for i in range(tiles)], axis=1
         )
@@ -218,15 +230,10 @@
         cells = core_ref.shape[2]
         for slab in range(core_ref.shape[1]):
             core_ref[:, slab, :] = core_flat[:, slab * cells : slab * cells + cells]
-        basis_ref[...] = basis_box[:rows, :]
-        for i in range(tiles):
-            for j in range(tiles):
-                at = places.get((i, j))
-                triangle_ref[TILE * i : TILE * i + TILE, TILE * j : TILE * j + TILE] = (
-                    jnp.zeros((TILE, TILE), jnp.float32)
-                    if at is None
-                    else triangle_box[TILE * at : TILE * at + TILE, :]
-                )
+        for copy in copies:
+            copy.wait()
+
+    zero_ref[...] = jnp.zeros_like(zero_ref)
 
     @pl.when(part_ref[0] == 0)
     def _():
@@ -273,7 +280,11 @@
             jax.ShapeDtypeStruct((rows, rows), jnp.float32),
         ],
         in_specs=[pl.BlockSpec(memory_space=pltpu.SMEM), vmem, vmem, vmem],
-        out_specs=[vmem, vmem, vmem],
+        out_specs=[vmem, pl.BlockSpec(memory_space=pl.ANY), pl.BlockSpec(memory_space=pl.ANY)],
+        scratch_shapes=[
+            pltpu.VMEM((TILE, TILE), jnp.float32),
+            pltpu.SemaphoreType.DMA((1 + (rows // TILE) ** 2,)),
+        ],
         compiler_params=pltpu.CompilerParams(vmem_limit_bytes=VMEM_LIMIT),
     )(part, outbox, inbox, unfold)
 
@@ -301,6 +312,39 @@
     )(tensor)
 
 
+def gram_kernel(halves, scale, half_ref, unfold_ref, blocks_ref):
+    for half, pairs in enumerate(halves):
+
+        @pl.when(half_ref[0] == half)
+        def _(pairs=pairs):
+            at = 0
+            for i in sorted({i for i, _ in pairs}):
+                columns = [j for first, j in pairs if first == i]
+                left = unfold_ref[TILE * i : TILE * i + TILE, :]
+                products = matmul_nt(left, unfold_ref[TILE * columns[0] : TILE * columns[-1] + TILE, :]) * scale
+                for n in range(len(columns)):
+                    blocks_ref[TILE * at : TILE * at + TILE, :] = products[:, TILE * n : TILE * n + TILE]
+                    at += 1
+
+
+def gram_blocks(unfold, scale, half, halves):
+    rows, columns = unfold.shape
+    pairs = list(block_places(rows // TILE))
+    each = len(pairs) // halves
+    parts = [pairs[each * n : each * n + each] for n in range(halves)]
+    vmem = pl.BlockSpec(memory_space=pltpu.VMEM)
+    return pl.pallas_call(
+        functools.partial(gram_kernel, parts, scale),
+        out_shape=jax.ShapeDtypeStruct((each * TILE, TILE), jnp.float32),
+        in_specs=[pl.BlockSpec(memory_space=pltpu.SMEM), vmem],
+        out_specs=vmem,
+        compiler_params=pltpu.CompilerParams(vmem_limit_bytes=VMEM_LIMIT),
+        cost_estimate=pl.CostEstimate(
+            flops=2 * each * TILE * TILE * columns, bytes_accessed=4 * rows * columns, transcendentals=0
+        ),
+    )(jnp.full((1,), half, jnp.int32), unfold)
+
+
 def local(tensor, initial):
     mode_size = lax.axis_size("mode")
     row_part, slab_count, width = tensor.shape
@@ -308,14 +352,14 @@
     column_total = slab_count * width * lax.axis_size("col")
     regrouped = lax.all_to_all(blocks_of(tensor, mode_size), "mode", split_axis=0, concat_axis=0, tiled=True)
     unfold = regrouped.reshape(row_count, slab_count * width // mode_size)
-    local_gram = matmul(unfold, unfold.T) / column_total
-    packed = jnp.concatenate(
-        [
-            local_gram[i * TILE : (i + 1) * TILE, j * TILE : (j + 1) * TILE]
-            for i, j in block_places(row_count // TILE)
-        ]
-    )
-    return finished(summed(packed), initial, unfold, slab_count)
+    scale = 1.0 / column_total
+    if lax.axis_size("col") % 2 or len(block_places(row_count // TILE)) % 2:
+        packed = summed(gram_blocks(unfold, scale, jnp.int32(0), 1))
+    else:
+        half = lax.axis_index("col") % 2
+        other = gram_blocks(unfold, scale, 1 - half, 2)
+        packed = summed(gram_blocks(unfold, scale, half, 2), other)
+    return finished(packed, initial, unfold, slab_count)
 
 
 def solution(mesh):

time: 84.2 us -> 83.9 us (level)
  Pallas kernels: 15.6 us -> 18.2 us
  matrix products: 1.86 us -> 0 us
    pallas_call x0 -> x2, Pallas kernels: none -> 2.7 us  [gram_blocks(): pl.pallas_call(functools.partial(gram_kernel, parts, scale), out_shape=ja...]
    dot_general x1 -> x0, matrix products: 1.86 us -> none  [matmul(): jnp.dot(left, right, precision=precise, preferred_element_type=jnp.float32)]
  transfers between devices with their start and end apart: 12 -> 12, of which waited for: 12 -> 12; matrix products, arithmetic and copies ran while one was open for 0% -> 0% of each run, Pallas kernels for 0% -> 2%
where the time goes in v6:
time: 83.9 us; the launch traced here: 83.7 us
  waiting for transfers between devices  43.6 us (52%)
  starting transfers between devices  19.4 us (23%)
  Pallas kernels  18.2 us (22%)
  local copies, waits for them, and re-layouts  1.4 us (2%)
  between operations  1.02 us (1%)
    all_to_all x1, waiting for transfers between devices, local(): lax.all_to_all(blocks_of(tensor, mode_size), 'mode', split_axis=0, concat...  24.4 us
    ppermute x11, waiting for transfers between devices, exchanged(): return lax.ppermute(value, axis, pairs)  19.2 us
    pallas_call x1, Pallas kernels, factors(): pl.pallas_call(functools.partial(factor_kernel, tiles), out_shape=jax.Sha...  12.3 us
    ppermute x11, starting transfers between devices, exchanged(): return lax.ppermute(value, axis, pairs)  11 us
    all_to_all x1, starting transfers between devices, local(): lax.all_to_all(blocks_of(tensor, mode_size), 'mode', split_axis=0, concat...  8.31 us
    pallas_call x2, Pallas kernels, gram_blocks(): pl.pallas_call(functools.partial(gram_kernel, parts, scale), out_shape=ja...  2.7 us
    pallas_call x1, Pallas kernels, finished(): pl.pallas_call(functools.partial(closing_kernel, rows // TILE), out_shape...  1.89 us
  transfers between devices with their start and end apart: 12, of which 12 were waited for; matrix products, arithmetic and copies ran while one was open for 0% of the time, Pallas kernels for 2%

profile of v6, /device:TPU:0, one launch (start us, length us, event | category | flops | bytes accessed | tf_op | source)
XLA Modules:
  0.0 83.7 jit_solution(17453504881877993969)
XLA Ops:
  0.6 0.0 copy-start
  0.6 1.2 %copy-done = f32[32,2,4096]{2,1,0:T(2,128)S(1)} copy-done((f32[32,2,4096]{2,1,0:T(2,128)S(1)}, f32[32,2,4096]{2,1,0:T(2,128)}, u32[]{:S(2)}) %copy-start) | copy-done | bytes 1048600
  1.9 1.3 %shard_map.49 = f32[16,32,512]{2,1,0:T(8,128)} custom-call(f32[32,2,4096]{2,1,0:T(2,128)S(1)} %copy-done), custom_call_target="tpu_custom_call" | custom-call | tf_op jit(solution)/shard_map/pallas_call | solution.py:306
  3.2 8.3 %all-to-all-start = ((f32[16,32,512]{2,1,0:T(8,128)}), f32[16,32,512]{2,1,0:T(8,128)S(1)}, u32[]{:S(2)}, u32[]{:S(2)}) async-start(f32[16,32,512]{2,1,0:T(8,128)} %shard_map.49), calls=%async_computation | async-start | bytes 2097152 | tf_op jit(solution)/shard_map/all_to_all | solution.py:353
  11.5 24.4 %all-to-all-done = f32[16,32,512]{2,1,0:T(8,128)S(1)} async-done(((f32[16,32,512]{2,1,0:T(8,128)}), f32[16,32,512]{2,1,0:T(8,128)S(1)}, u32[]{:S(2)}, u32[]{:S(2)}) %all-to-all-start) | async-done | bytes 1048608 | tf_op jit(solution)/shard_map/all_to_all | solution.py:353
  35.9 1.3 %shard_map.51 = f32[640,128]{1,0:T(8,128)S(1)} custom-call(s32[1]{0:T(128)} %bitcast.2.half_ref, f32[512,512]{1,0:T(8,128)S(1)} %bitcast.3), custom_call_target="tpu_custom_call" | custom-call | flops 83886080 | bytes 1048576 | tf_op jit(solution)/shard_map/pallas_call | solution.py:336
  37.3 0.1 collective-permute-start
  37.4 1.4 %shard_map.50 = f32[640,128]{1,0:T(8,128)S(1)} custom-call(s32[1]{0:T(128)} %bitcast.half_ref.part_ref, f32[512,512]{1,0:T(8,128)S(1)} %bitcast.4), custom_call_target="tpu_custom_call" | custom-call | flops 83886080 | bytes 1048576 | tf_op jit(solution)/shard_map/pallas_call | solution.py:336
  38.8 0.2 collective-permute-done
  39.1 0.6 collective-permute-start.1
  39.7 2.9 %collective-permute-start.3 = (f32[160,128]{1,0:T(8,128)S(1)}, f32[160,128]{1,0:T(8,128)S(1)}, u32[]{:S(2)}, u32[]{:S(2)}) collective-permute-start(f32[160,128]{1,0:T(8,128)S(1)} %get-tuple-element.6), channel_id=1, source_target_pairs={{0,6},{2,4},{4,2},{6,0},{8,14},{10,12},{12,10},{14,8},{16,22},{18,... | collective-permute-start | bytes 245768 | tf_op jit(solution)/shard_map/ppermute | solution.py:36
  42.5 0.1 collective-permute-start.2
  42.6 1.2 %collective-permute-done.1 = f32[160,128]{1,0:T(8,128)S(1)} collective-permute-done((f32[160,128]{1,0:T(8,128)S(1)}, f32[160,128]{1,0:T(8,128)S(1)}, u32[]{:S(2)}, u32[]{:S(2)}) %collective-permute-start.1) | collective-permute-done | bytes 81952 | tf_op jit(solution)/shard_map/ppermute | solution.py:36
  43.8 3.2 %collective-permute-done.3 = f32[160,128]{1,0:T(8,128)S(1)} collective-permute-done((f32[160,128]{1,0:T(8,128)S(1)}, f32[160,128]{1,0:T(8,128)S(1)}, u32[]{:S(2)}, u32[]{:S(2)}) %collective-permute-start.3) | collective-permute-done | bytes 81952 | tf_op jit(solution)/shard_map/ppermute | solution.py:36
  47.0 1.2 %collective-permute-done.2 = f32[160,128]{1,0:T(8,128)S(1)} collective-permute-done((f32[160,128]{1,0:T(8,128)S(1)}, f32[160,128]{1,0:T(8,128)S(1)}, u32[]{:S(2)}, u32[]{:S(2)}) %collective-permute-start.2) | collective-permute-done | bytes 81952 | tf_op jit(solution)/shard_map/ppermute | solution.py:36
  48.2 2.4 %collective-permute-start.4 = (f32[160,128]{1,0:T(8,128)S(1)}, f32[160,128]{1,0:T(8,128)S(1)}, u32[]{:S(2)}, u32[]{:S(2)}) collective-permute-start(f32[160,128]{1,0:T(8,128)S(1)} %add_add_fusion), channel_id=1, source_target_pairs={{0,8},{2,10},{4,12},{6,14},{8,0},{10,2},{12,4},{14,6},{16,24},{18,... | collective-permute-start | bytes 245768 | tf_op jit(solution)/shard_map/ppermute | solution.py:36
  50.5 2.4 %collective-permute-done.4 = f32[160,128]{1,0:T(8,128)S(1)} collective-permute-done((f32[160,128]{1,0:T(8,128)S(1)}, f32[160,128]{1,0:T(8,128)S(1)}, u32[]{:S(2)}, u32[]{:S(2)}) %collective-permute-start.4) | collective-permute-done | bytes 81952 | tf_op jit(solution)/shard_map/ppermute | solution.py:36
  53.0 1.3 %collective-permute-start.5 = (f32[160,128]{1,0:T(8,128)S(1)}, f32[160,128]{1,0:T(8,128)S(1)}, u32[]{:S(2)}, u32[]{:S(2)}) collective-permute-start(f32[160,128]{1,0:T(8,128)S(1)} %add.60), channel_id=1, source_target_pairs={{0,16},{2,18},{4,20},{6,22},{8,24},{10,26},{12,28},{14,30},{16,0},... | collective-permute-start | bytes 245768 | tf_op jit(solution)/shard_map/ppermute | solution.py:36
  54.3 4.1 %collective-permute-done.5 = f32[160,128]{1,0:T(8,128)S(1)} collective-permute-done((f32[160,128]{1,0:T(8,128)S(1)}, f32[160,128]{1,0:T(8,128)S(1)}, u32[]{:S(2)}, u32[]{:S(2)}) %collective-permute-start.5) | collective-permute-done | bytes 81952 | tf_op jit(solution)/shard_map/ppermute | solution.py:36
  58.4 0.8 collective-permute-start.6
  59.2 0.8 collective-permute-start.7
  60.0 2.0 %collective-permute-start.8 = (f32[160,128]{1,0:T(8,128)S(1)}, f32[160,128]{1,0:T(8,128)S(1)}, u32[]{:S(2)}, u32[]{:S(2)}) collective-permute-start(f32[160,128]{1,0:T(8,128)S(1)} %get-tuple-element.4), channel_id=1, source_target_pairs={{0,6},{2,4},{4,2},{6,0},{8,14},{10,12},{12,10},{14,8},{16,22},{18,... | collective-permute-start | bytes 245768 | tf_op jit(solution)/shard_map/ppermute | solution.py:36
  62.0 1.0 %collective-permute-done.6 = f32[160,128]{1,0:T(8,128)S(1)} collective-permute-done((f32[160,128]{1,0:T(8,128)S(1)}, f32[160,128]{1,0:T(8,128)S(1)}, u32[]{:S(2)}, u32[]{:S(2)}) %collective-permute-start.6) | collective-permute-done | bytes 81952 | tf_op jit(solution)/shard_map/ppermute | solution.py:36
  63.0 0.7 collective-permute-done.7
  63.6 1.7 %collective-permute-done.8 = f32[160,128]{1,0:T(8,128)S(1)} collective-permute-done((f32[160,128]{1,0:T(8,128)S(1)}, f32[160,128]{1,0:T(8,128)S(1)}, u32[]{:S(2)}, u32[]{:S(2)}) %collective-permute-start.8) | collective-permute-done | bytes 81952 | tf_op jit(solution)/shard_map/ppermute | solution.py:36
  65.4 0.1 collective-permute-start.9
  65.6 0.0 copy-start.1
  65.6 1.5 %collective-permute-done.9 = f32[640,128]{1,0:T(8,128)S(1)} collective-permute-done((f32[640,128]{1,0:T(8,128)S(1)}, f32[640,128]{1,0:T(8,128)S(1)}, u32[]{:S(2)}, u32[]{:S(2)}) %collective-permute-start.9) | collective-permute-done | bytes 327712 | tf_op jit(solution)/shard_map/ppermute | solution.py:36
  67.1 0.0 copy-done.1
  67.1 12.3 %shard_map.52.outbox_ref = f32[1280,128]{1,0:T(8,128)S(1)} custom-call(s32[1]{0:T(128)} %bitcast.half_ref.part_ref, f32[1280,128]{1,0:T(8,128)S(1)} %constant_dynamic-update-slice_fusion.packed_ref, f32[512,128]{1,0:T(8,128)S(1)} %copy-done.1), custom_call_target="tpu_custom_call" | custom-call | tf_op jit(solution)/shard_map/pallas_call | solution.py:254
  79.5 0.1 collective-permute-start.10
  79.5 2.1 %collective-permute-done.10.inbox_ref = f32[1280,128]{1,0:T(8,128)S(1)} collective-permute-done((f32[1280,128]{1,0:T(8,128)S(1)}, f32[1280,128]{1,0:T(8,128)S(1)}, u32[]{:S(2)}, u32[]{:S(2)}) %collective-permute-start.10) | collective-permute-done | bytes 655392 | tf_op jit(solution)/shard_map/ppermute | solution.py:36
  81.6 1.9 %shard_map.53 = (f32[128,2,256]{2,1,0:T(2,128)}, f32[512,128]{1,0:T(8,128)}, f32[512,512]{1,0:T(8,128)}) custom-call(s32[1]{0:T(128)} %bitcast.half_ref.part_ref, f32[1280,128]{1,0:T(8,128)S(1)} %shard_map.52.outbox_ref, f32[1280,128]{1,0:T(8,128)S(1)} %collective-permute-done.10.inbox_ref, f32[512,512]{1,0:T(8,128)S(1)} %bitcast.5), custom_call_target="tpu_custom_call" | custom-call | tf_op jit(solution)/shard_map/pallas_call | solution.py:275
  (12 shorter events, 0.3 us)
Async XLA Ops:
  0.6 1.2 %copy-start = (f32[32,2,4096]{2,1,0:T(2,128)S(1)}, f32[32,2,4096]{2,1,0:T(2,128)}, u32[]{:S(2)}) copy-start(f32[32,2,4096]{2,1,0:T(2,128)} %tensor_ref.1) | copy-start | bytes 3145732
  3.2 32.8 %all-to-all-start = ((f32[16,32,512]{2,1,0:T(8,128)}), f32[16,32,512]{2,1,0:T(8,128)S(1)}, u32[]{:S(2)}, u32[]{:S(2)}) async-start(f32[16,32,512]{2,1,0:T(8,128)} %shard_map.49), calls=%async_computation | async-start | bytes 2097152 | tf_op jit(solution)/shard_map/all_to_all | solution.py:353
  37.3 1.7 %collective-permute-start = (f32[640,128]{1,0:T(8,128)S(1)}, f32[640,128]{1,0:T(8,128)S(1)}, u32[]{:S(2)}, u32[]{:S(2)}) collective-permute-start(f32[640,128]{1,0:T(8,128)S(1)} %shard_map.51), channel_id=1, source_target_pairs={{0,1},{1,0},{2,3},{3,2},{4,5},{5,4},{6,7},{7,6},{8,9},{9,8},{10,11... | collective-permute-start | bytes 983048 | tf_op jit(solution)/shard_map/ppermute | solution.py:36
  39.1 4.7 %collective-permute-start.1 = (f32[160,128]{1,0:T(8,128)S(1)}, f32[160,128]{1,0:T(8,128)S(1)}, u32[]{:S(2)}, u32[]{:S(2)}) collective-permute-start(f32[160,128]{1,0:T(8,128)S(1)} %get-tuple-element.5), channel_id=1, source_target_pairs={{0,2},{2,0},{4,6},{6,4},{8,10},{10,8},{12,14},{14,12},{16,18},{18,... | collective-permute-start | bytes 245768 | tf_op jit(solution)/shard_map/ppermute | solution.py:36
  39.7 7.3 %collective-permute-start.3 = (f32[160,128]{1,0:T(8,128)S(1)}, f32[160,128]{1,0:T(8,128)S(1)}, u32[]{:S(2)}, u32[]{:S(2)}) collective-permute-start(f32[160,128]{1,0:T(8,128)S(1)} %get-tuple-element.6), channel_id=1, source_target_pairs={{0,6},{2,4},{4,2},{6,0},{8,14},{10,12},{12,10},{14,8},{16,22},{18,... | collective-permute-start | bytes 245768 | tf_op jit(solution)/shard_map/ppermute | solution.py:36
  42.5 5.6 %collective-permute-start.2 = (f32[160,128]{1,0:T(8,128)S(1)}, f32[160,128]{1,0:T(8,128)S(1)}, u32[]{:S(2)}, u32[]{:S(2)}) collective-permute-start(f32[160,128]{1,0:T(8,128)S(1)} %get-tuple-element.7), channel_id=1, source_target_pairs={{0,4},{2,6},{4,0},{6,2},{8,12},{10,14},{12,8},{14,10},{16,20},{18,... | collective-permute-start | bytes 245768 | tf_op jit(solution)/shard_map/ppermute | solution.py:36
  48.2 4.8 %collective-permute-start.4 = (f32[160,128]{1,0:T(8,128)S(1)}, f32[160,128]{1,0:T(8,128)S(1)}, u32[]{:S(2)}, u32[]{:S(2)}) collective-permute-start(f32[160,128]{1,0:T(8,128)S(1)} %add_add_fusion), channel_id=1, source_target_pairs={{0,8},{2,10},{4,12},{6,14},{8,0},{10,2},{12,4},{14,6},{16,24},{18,... | collective-permute-start | bytes 245768 | tf_op jit(solution)/shard_map/ppermute | solution.py:36
  53.0 5.4 %collective-permute-start.5 = (f32[160,128]{1,0:T(8,128)S(1)}, f32[160,128]{1,0:T(8,128)S(1)}, u32[]{:S(2)}, u32[]{:S(2)}) collective-permute-start(f32[160,128]{1,0:T(8,128)S(1)} %add.60), channel_id=1, source_target_pairs={{0,16},{2,18},{4,20},{6,22},{8,24},{10,26},{12,28},{14,30},{16,0},... | collective-permute-start | bytes 245768 | tf_op jit(solution)/shard_map/ppermute | solution.py:36
  58.4 4.5 %collective-permute-start.6 = (f32[160,128]{1,0:T(8,128)S(1)}, f32[160,128]{1,0:T(8,128)S(1)}, u32[]{:S(2)}, u32[]{:S(2)}) collective-permute-start(f32[160,128]{1,0:T(8,128)S(1)} %get-tuple-element.4), channel_id=1, source_target_pairs={{0,2},{2,0},{4,6},{6,4},{8,10},{10,8},{12,14},{14,12},{16,18},{18,... | collective-permute-start | bytes 245768 | tf_op jit(solution)/shard_map/ppermute | solution.py:36
  59.2 4.4 %collective-permute-start.7 = (f32[160,128]{1,0:T(8,128)S(1)}, f32[160,128]{1,0:T(8,128)S(1)}, u32[]{:S(2)}, u32[]{:S(2)}) collective-permute-start(f32[160,128]{1,0:T(8,128)S(1)} %get-tuple-element.4), channel_id=1, source_target_pairs={{0,4},{2,6},{4,0},{6,2},{8,12},{10,14},{12,8},{14,10},{16,20},{18,... | collective-permute-start | bytes 245768 | tf_op jit(solution)/shard_map/ppermute | solution.py:36
  60.0 5.3 %collective-permute-start.8 = (f32[160,128]{1,0:T(8,128)S(1)}, f32[160,128]{1,0:T(8,128)S(1)}, u32[]{:S(2)}, u32[]{:S(2)}) collective-permute-start(f32[160,128]{1,0:T(8,128)S(1)} %get-tuple-element.4), channel_id=1, source_target_pairs={{0,6},{2,4},{4,2},{6,0},{8,14},{10,12},{12,10},{14,8},{16,22},{18,... | collective-permute-start | bytes 245768 | tf_op jit(solution)/shard_map/ppermute | solution.py:36
  65.4 1.7 %collective-permute-start.9 = (f32[640,128]{1,0:T(8,128)S(1)}, f32[640,128]{1,0:T(8,128)S(1)}, u32[]{:S(2)}, u32[]{:S(2)}) collective-permute-start(f32[640,128]{1,0:T(8,128)S(1)} %constant_dynamic-update-slice_fusion.2), channel_id=1, source_target_pairs={{0,1},{1,0},{2,3},{3,2},{4,5},{5,4},{6,7},{7,6},{8,9},{9,8},{10,11... | collective-permute-start | bytes 983048 | tf_op jit(solution)/shard_map/ppermute | solution.py:36
  65.6 1.5 %copy-start.1 = (f32[512,128]{1,0:T(8,128)S(1)}, f32[512,128]{1,0:T(8,128)}, u32[]{:S(2)}) copy-start(f32[512,128]{1,0:T(8,128)} %initial_ref.1) | copy-start | bytes 786436
  79.5 2.2 %collective-permute-start.10 = (f32[1280,128]{1,0:T(8,128)S(1)}, f32[1280,128]{1,0:T(8,128)S(1)}, u32[]{:S(2)}, u32[]{:S(2)}) collective-permute-start(f32[1280,128]{1,0:T(8,128)S(1)} %shard_map.52.outbox_ref), channel_id=1, source_target_pairs={{0,1},{1,0},{2,3},{3,2},{4,5},{5,4},{6,7},{7,6},{8,9},{9,8},{10,11... | collective-permute-start | bytes 1966088 | tf_op jit(solution)/shard_map/ppermute | solution.py:36

commit v7 on v6

--- a/solution.py
+++ b/solution.py
@@ -105,30 +105,53 @@
         if far:
             sent = jnp.concatenate([jnp.where(lane >= base + width + width, panel[h], 0.0) for h in members])
         kept, scale = list(panel), [None] * PANEL
-        for pivot in range(width):
+        for pivot in range(0, width, 2):
             own, place = divmod(pivot, SUB)
-            here = row == place
-            cleared = lane == base + pivot
-            reciprocal = pl.reciprocal(row_of(columns[pivot][own], place), approx=True)
-            scale[own] = jnp.where(here, reciprocal, scale[own]) if place else reciprocal
-            kept[own] = jnp.where(here, panel[own], kept[own]) if place else panel[own]
-            factor = [
-                (jnp.where(here, 0.0, columns[pivot][h]) if h == own else columns[pivot][h]) * reciprocal
-                for h in members
-            ]
-            for j in range(pivot + 1, width):
-                value = row_of(columns[j][own], place)
-                columns[j] = [columns[j][h] - factor[h] * value for h in members]
-            value = jnp.where(cleared, 1.0, row_of(panel[own], place))
-            panel = [
-                jnp.where(cleared, jnp.where(here, 1.0, 0.0) if h == own else 0.0, panel[h]) - factor[h] * value
-                for h in members
-            ]
+            reached = range(own, PANEL)
+            here, next_row = row == place, row == place + 1
+            at, next_at = lane == base + pivot, lane == base + pivot + 1
+            left, right = columns[pivot], columns[pivot + 1]
+            a, b = row_of(left[own], place), row_of(right[own], place)
+            c = row_of(right[own], place + 1)
+            over_a = pl.reciprocal(a, approx=True)
+            over_det = pl.reciprocal(a * c - b * b, approx=True)
+            left = {h: left[h] for h in reached}
+            right = {h: right[h] for h in reached}
+            left[own] = jnp.where(here, -1.0, jnp.where(next_row, 0.0, left[own]))
+            right[own] = jnp.where(here, 0.0, jnp.where(next_row, -1.0, right[own]))
+            factor = {h: (c * left[h] - b * right[h]) * over_det for h in reached}
+            next_factor = {h: (a * right[h] - b * left[h]) * over_det for h in reached}
+
+            def reduced_by(value, top, bottom, h):
+                return value - factor[h] * top - next_factor[h] * bottom
+
+            for j in range(pivot + 2, width):
+                top, bottom = row_of(columns[j][own], place), row_of(columns[j][own], place + 1)
+                for h in reached:
+                    value = jnp.where(here | next_row, 0.0, columns[j][h]) if h == own else columns[j][h]
+                    columns[j][h] = reduced_by(value, top, bottom, h)
+            top, bottom = row_of(panel[own], place), row_of(panel[own], place + 1)
+            following = jnp.where(at, 0.0, bottom) - (b * over_a) * jnp.where(at, 1.0, top)
+            kept[own] = jnp.where(here, panel[own], jnp.where(next_row, following, kept[own]))
+            scale[own] = jnp.where(here, over_a, jnp.where(next_row, a * over_det, scale[own] if place else 0.0))
+            top = jnp.where(at, 1.0, jnp.where(next_at, 0.0, top))
+            bottom = jnp.where(at, 0.0, jnp.where(next_at, 1.0, bottom))
+            for h in reached:
+                cleared = at | next_at
+                if h == own:
+                    cleared = cleared | here | next_row
+                panel[h] = reduced_by(jnp.where(cleared, 0.0, panel[h]), top, bottom, h)
+        for h in reversed(members):
+            for later in range(h + 1, PANEL):
+                start = base + SUB * later
+                panel[h] = jnp.where((lane >= start) & (lane < start + SUB), 0.0, panel[h])
+                for m in range(SUB):
+                    panel[h] = panel[h] - columns[SUB * later + m][h] * row_of(panel[later], m)
         for h in members:
             tiles[first + h] = kept[h]
             scales[first + h] = scale[h]
         if near:
-            reduced = [panel[h] * scale[h] for h in members]
+            reduced = panel
             rows = [row_of(reduced[m // SUB], m % SUB) for m in range(width)]
             for t in near:
                 even = jnp.where(inside, 0.0, tiles[t])

time: 83.9 us -> 83.3 us (level)
  no operation moved by 1% of the time
where the time goes in v7:
time: 83.3 us; the launch traced here: 83 us
  waiting for transfers between devices  43.6 us (52%)
  starting transfers between devices  19.4 us (23%)
  Pallas kernels  17.6 us (21%)
  local copies, waits for them, and re-layouts  1.4 us (2%)
  between operations  1.02 us (1%)
    all_to_all x1, waiting for transfers between devices, local(): lax.all_to_all(blocks_of(tensor, mode_size), 'mode', split_axis=0, concat...  24.4 us
    ppermute x11, waiting for transfers between devices, exchanged(): return lax.ppermute(value, axis, pairs)  19.2 us
    pallas_call x1, Pallas kernels, factors(): pl.pallas_call(functools.partial(factor_kernel, tiles), out_shape=jax.Sha...  11.7 us
    ppermute x11, starting transfers between devices, exchanged(): return lax.ppermute(value, axis, pairs)  11 us
    all_to_all x1, starting transfers between devices, local(): lax.all_to_all(blocks_of(tensor, mode_size), 'mode', split_axis=0, concat...  8.31 us
    pallas_call x2, Pallas kernels, gram_blocks(): pl.pallas_call(functools.partial(gram_kernel, parts, scale), out_shape=ja...  2.7 us
    pallas_call x1, Pallas kernels, finished(): pl.pallas_call(functools.partial(closing_kernel, rows // TILE), out_shape...  1.89 us
  transfers between devices with their start and end apart: 12, of which 12 were waited for; matrix products, arithmetic and copies ran while one was open for 0% of the time, Pallas kernels for 2%

profile of v7, /device:TPU:0, one launch (start us, length us, event | category | flops | bytes accessed | tf_op | source)
XLA Modules:
  0.0 83.0 jit_solution(14739029535182559759)
XLA Ops:
  0.6 0.0 copy-start
  0.6 1.2 %copy-done = f32[32,2,4096]{2,1,0:T(2,128)S(1)} copy-done((f32[32,2,4096]{2,1,0:T(2,128)S(1)}, f32[32,2,4096]{2,1,0:T(2,128)}, u32[]{:S(2)}) %copy-start) | copy-done | bytes 1048600
  1.9 1.3 %shard_map.49 = f32[16,32,512]{2,1,0:T(8,128)} custom-call(f32[32,2,4096]{2,1,0:T(2,128)S(1)} %copy-done), custom_call_target="tpu_custom_call" | custom-call | tf_op jit(solution)/shard_map/pallas_call | solution.py:329
  3.2 8.3 %all-to-all-start = ((f32[16,32,512]{2,1,0:T(8,128)}), f32[16,32,512]{2,1,0:T(8,128)S(1)}, u32[]{:S(2)}, u32[]{:S(2)}) async-start(f32[16,32,512]{2,1,0:T(8,128)} %shard_map.49), calls=%async_computation | async-start | bytes 2097152 | tf_op jit(solution)/shard_map/all_to_all | solution.py:376
  11.5 24.4 %all-to-all-done = f32[16,32,512]{2,1,0:T(8,128)S(1)} async-done(((f32[16,32,512]{2,1,0:T(8,128)}), f32[16,32,512]{2,1,0:T(8,128)S(1)}, u32[]{:S(2)}, u32[]{:S(2)}) %all-to-all-start) | async-done | bytes 1048608 | tf_op jit(solution)/shard_map/all_to_all | solution.py:376
  35.9 1.3 %shard_map.51 = f32[640,128]{1,0:T(8,128)S(1)} custom-call(s32[1]{0:T(128)} %bitcast.2.half_ref, f32[512,512]{1,0:T(8,128)S(1)} %bitcast.3), custom_call_target="tpu_custom_call" | custom-call | flops 83886080 | bytes 1048576 | tf_op jit(solution)/shard_map/pallas_call | solution.py:359
  37.3 0.1 collective-permute-start
  37.4 1.4 %shard_map.50 = f32[640,128]{1,0:T(8,128)S(1)} custom-call(s32[1]{0:T(128)} %bitcast.half_ref.part_ref, f32[512,512]{1,0:T(8,128)S(1)} %bitcast.4), custom_call_target="tpu_custom_call" | custom-call | flops 83886080 | bytes 1048576 | tf_op jit(solution)/shard_map/pallas_call | solution.py:359
  38.8 0.2 collective-permute-done
  39.1 0.6 collective-permute-start.1
  39.7 2.9 %collective-permute-start.3 = (f32[160,128]{1,0:T(8,128)S(1)}, f32[160,128]{1,0:T(8,128)S(1)}, u32[]{:S(2)}, u32[]{:S(2)}) collective-permute-start(f32[160,128]{1,0:T(8,128)S(1)} %get-tuple-element.6), channel_id=1, source_target_pairs={{0,6},{2,4},{4,2},{6,0},{8,14},{10,12},{12,10},{14,8},{16,22},{18,... | collective-permute-start | bytes 245768 | tf_op jit(solution)/shard_map/ppermute | solution.py:36
  42.5 0.1 collective-permute-start.2
  42.6 1.2 %collective-permute-done.1 = f32[160,128]{1,0:T(8,128)S(1)} collective-permute-done((f32[160,128]{1,0:T(8,128)S(1)}, f32[160,128]{1,0:T(8,128)S(1)}, u32[]{:S(2)}, u32[]{:S(2)}) %collective-permute-start.1) | collective-permute-done | bytes 81952 | tf_op jit(solution)/shard_map/ppermute | solution.py:36
  43.8 3.2 %collective-permute-done.3 = f32[160,128]{1,0:T(8,128)S(1)} collective-permute-done((f32[160,128]{1,0:T(8,128)S(1)}, f32[160,128]{1,0:T(8,128)S(1)}, u32[]{:S(2)}, u32[]{:S(2)}) %collective-permute-start.3) | collective-permute-done | bytes 81952 | tf_op jit(solution)/shard_map/ppermute | solution.py:36
  47.0 1.2 %collective-permute-done.2 = f32[160,128]{1,0:T(8,128)S(1)} collective-permute-done((f32[160,128]{1,0:T(8,128)S(1)}, f32[160,128]{1,0:T(8,128)S(1)}, u32[]{:S(2)}, u32[]{:S(2)}) %collective-permute-start.2) | collective-permute-done | bytes 81952 | tf_op jit(solution)/shard_map/ppermute | solution.py:36
  48.2 2.4 %collective-permute-start.4 = (f32[160,128]{1,0:T(8,128)S(1)}, f32[160,128]{1,0:T(8,128)S(1)}, u32[]{:S(2)}, u32[]{:S(2)}) collective-permute-start(f32[160,128]{1,0:T(8,128)S(1)} %add_add_fusion), channel_id=1, source_target_pairs={{0,8},{2,10},{4,12},{6,14},{8,0},{10,2},{12,4},{14,6},{16,24},{18,... | collective-permute-start | bytes 245768 | tf_op jit(solution)/shard_map/ppermute | solution.py:36
  50.5 2.4 %collective-permute-done.4 = f32[160,128]{1,0:T(8,128)S(1)} collective-permute-done((f32[160,128]{1,0:T(8,128)S(1)}, f32[160,128]{1,0:T(8,128)S(1)}, u32[]{:S(2)}, u32[]{:S(2)}) %collective-permute-start.4) | collective-permute-done | bytes 81952 | tf_op jit(solution)/shard_map/ppermute | solution.py:36
  53.0 1.3 %collective-permute-start.5 = (f32[160,128]{1,0:T(8,128)S(1)}, f32[160,128]{1,0:T(8,128)S(1)}, u32[]{:S(2)}, u32[]{:S(2)}) collective-permute-start(f32[160,128]{1,0:T(8,128)S(1)} %add.60), channel_id=1, source_target_pairs={{0,16},{2,18},{4,20},{6,22},{8,24},{10,26},{12,28},{14,30},{16,0},... | collective-permute-start | bytes 245768 | tf_op jit(solution)/shard_map/ppermute | solution.py:36
  54.3 4.1 %collective-permute-done.5 = f32[160,128]{1,0:T(8,128)S(1)} collective-permute-done((f32[160,128]{1,0:T(8,128)S(1)}, f32[160,128]{1,0:T(8,128)S(1)}, u32[]{:S(2)}, u32[]{:S(2)}) %collective-permute-start.5) | collective-permute-done | bytes 81952 | tf_op jit(solution)/shard_map/ppermute | solution.py:36
  58.4 0.8 collective-permute-start.6
  59.2 0.8 %collective-permute-start.7 = (f32[160,128]{1,0:T(8,128)S(1)}, f32[160,128]{1,0:T(8,128)S(1)}, u32[]{:S(2)}, u32[]{:S(2)}) collective-permute-start(f32[160,128]{1,0:T(8,128)S(1)} %get-tuple-element.4), channel_id=1, source_target_pairs={{0,4},{2,6},{4,0},{6,2},{8,12},{10,14},{12,8},{14,10},{16,20},{18,... | collective-permute-start | bytes 245768 | tf_op jit(solution)/shard_map/ppermute | solution.py:36
  60.0 2.0 %collective-permute-start.8 = (f32[160,128]{1,0:T(8,128)S(1)}, f32[160,128]{1,0:T(8,128)S(1)}, u32[]{:S(2)}, u32[]{:S(2)}) collective-permute-start(f32[160,128]{1,0:T(8,128)S(1)} %get-tuple-element.4), channel_id=1, source_target_pairs={{0,6},{2,4},{4,2},{6,0},{8,14},{10,12},{12,10},{14,8},{16,22},{18,... | collective-permute-start | bytes 245768 | tf_op jit(solution)/shard_map/ppermute | solution.py:36
  62.0 1.0 %collective-permute-done.6 = f32[160,128]{1,0:T(8,128)S(1)} collective-permute-done((f32[160,128]{1,0:T(8,128)S(1)}, f32[160,128]{1,0:T(8,128)S(1)}, u32[]{:S(2)}, u32[]{:S(2)}) %collective-permute-start.6) | collective-permute-done | bytes 81952 | tf_op jit(solution)/shard_map/ppermute | solution.py:36
  63.0 0.7 collective-permute-done.7
  63.6 1.7 %collective-permute-done.8 = f32[160,128]{1,0:T(8,128)S(1)} collective-permute-done((f32[160,128]{1,0:T(8,128)S(1)}, f32[160,128]{1,0:T(8,128)S(1)}, u32[]{:S(2)}, u32[]{:S(2)}) %collective-permute-start.8) | collective-permute-done | bytes 81952 | tf_op jit(solution)/shard_map/ppermute | solution.py:36
  65.4 0.1 collective-permute-start.9
  65.6 0.0 copy-start.1
  65.6 1.5 %collective-permute-done.9 = f32[640,128]{1,0:T(8,128)S(1)} collective-permute-done((f32[640,128]{1,0:T(8,128)S(1)}, f32[640,128]{1,0:T(8,128)S(1)}, u32[]{:S(2)}, u32[]{:S(2)}) %collective-permute-start.9) | collective-permute-done | bytes 327712 | tf_op jit(solution)/shard_map/ppermute | solution.py:36
  67.1 0.0 copy-done.1
  67.1 11.7 %shard_map.52.outbox_ref = f32[1280,128]{1,0:T(8,128)S(1)} custom-call(s32[1]{0:T(128)} %bitcast.half_ref.part_ref, f32[1280,128]{1,0:T(8,128)S(1)} %constant_dynamic-update-slice_fusion.packed_ref, f32[512,128]{1,0:T(8,128)S(1)} %copy-done.1), custom_call_target="tpu_custom_call" | custom-call | tf_op jit(solution)/shard_map/pallas_call | solution.py:277
  78.8 0.1 collective-permute-start.10
  78.9 2.1 %collective-permute-done.10.inbox_ref = f32[1280,128]{1,0:T(8,128)S(1)} collective-permute-done((f32[1280,128]{1,0:T(8,128)S(1)}, f32[1280,128]{1,0:T(8,128)S(1)}, u32[]{:S(2)}, u32[]{:S(2)}) %collective-permute-start.10) | collective-permute-done | bytes 655392 | tf_op jit(solution)/shard_map/ppermute | solution.py:36
  81.0 1.9 %shard_map.53 = (f32[128,2,256]{2,1,0:T(2,128)}, f32[512,128]{1,0:T(8,128)}, f32[512,512]{1,0:T(8,128)}) custom-call(s32[1]{0:T(128)} %bitcast.half_ref.part_ref, f32[1280,128]{1,0:T(8,128)S(1)} %shard_map.52.outbox_ref, f32[1280,128]{1,0:T(8,128)S(1)} %collective-permute-done.10.inbox_ref, f32[512,512]{1,0:T(8,128)S(1)} %bitcast.5), custom_call_target="tpu_custom_call" | custom-call | tf_op jit(solution)/shard_map/pallas_call | solution.py:298
  (12 shorter events, 0.3 us)
Async XLA Ops:
  0.6 1.2 %copy-start = (f32[32,2,4096]{2,1,0:T(2,128)S(1)}, f32[32,2,4096]{2,1,0:T(2,128)}, u32[]{:S(2)}) copy-start(f32[32,2,4096]{2,1,0:T(2,128)} %tensor_ref.1) | copy-start | bytes 3145732
  3.2 32.8 %all-to-all-start = ((f32[16,32,512]{2,1,0:T(8,128)}), f32[16,32,512]{2,1,0:T(8,128)S(1)}, u32[]{:S(2)}, u32[]{:S(2)}) async-start(f32[16,32,512]{2,1,0:T(8,128)} %shard_map.49), calls=%async_computation | async-start | bytes 2097152 | tf_op jit(solution)/shard_map/all_to_all | solution.py:376
  37.3 1.7 %collective-permute-start = (f32[640,128]{1,0:T(8,128)S(1)}, f32[640,128]{1,0:T(8,128)S(1)}, u32[]{:S(2)}, u32[]{:S(2)}) collective-permute-start(f32[640,128]{1,0:T(8,128)S(1)} %shard_map.51), channel_id=1, source_target_pairs={{0,1},{1,0},{2,3},{3,2},{4,5},{5,4},{6,7},{7,6},{8,9},{9,8},{10,11... | collective-permute-start | bytes 983048 | tf_op jit(solution)/shard_map/ppermute | solution.py:36
  39.1 4.7 %collective-permute-start.1 = (f32[160,128]{1,0:T(8,128)S(1)}, f32[160,128]{1,0:T(8,128)S(1)}, u32[]{:S(2)}, u32[]{:S(2)}) collective-permute-start(f32[160,128]{1,0:T(8,128)S(1)} %get-tuple-element.5), channel_id=1, source_target_pairs={{0,2},{2,0},{4,6},{6,4},{8,10},{10,8},{12,14},{14,12},{16,18},{18,... | collective-permute-start | bytes 245768 | tf_op jit(solution)/shard_map/ppermute | solution.py:36
  39.7 7.3 %collective-permute-start.3 = (f32[160,128]{1,0:T(8,128)S(1)}, f32[160,128]{1,0:T(8,128)S(1)}, u32[]{:S(2)}, u32[]{:S(2)}) collective-permute-start(f32[160,128]{1,0:T(8,128)S(1)} %get-tuple-element.6), channel_id=1, source_target_pairs={{0,6},{2,4},{4,2},{6,0},{8,14},{10,12},{12,10},{14,8},{16,22},{18,... | collective-permute-start | bytes 245768 | tf_op jit(solution)/shard_map/ppermute | solution.py:36
  42.5 5.6 %collective-permute-start.2 = (f32[160,128]{1,0:T(8,128)S(1)}, f32[160,128]{1,0:T(8,128)S(1)}, u32[]{:S(2)}, u32[]{:S(2)}) collective-permute-start(f32[160,128]{1,0:T(8,128)S(1)} %get-tuple-element.7), channel_id=1, source_target_pairs={{0,4},{2,6},{4,0},{6,2},{8,12},{10,14},{12,8},{14,10},{16,20},{18,... | collective-permute-start | bytes 245768 | tf_op jit(solution)/shard_map/ppermute | solution.py:36
  48.2 4.8 %collective-permute-start.4 = (f32[160,128]{1,0:T(8,128)S(1)}, f32[160,128]{1,0:T(8,128)S(1)}, u32[]{:S(2)}, u32[]{:S(2)}) collective-permute-start(f32[160,128]{1,0:T(8,128)S(1)} %add_add_fusion), channel_id=1, source_target_pairs={{0,8},{2,10},{4,12},{6,14},{8,0},{10,2},{12,4},{14,6},{16,24},{18,... | collective-permute-start | bytes 245768 | tf_op jit(solution)/shard_map/ppermute | solution.py:36
  53.0 5.4 %collective-permute-start.5 = (f32[160,128]{1,0:T(8,128)S(1)}, f32[160,128]{1,0:T(8,128)S(1)}, u32[]{:S(2)}, u32[]{:S(2)}) collective-permute-start(f32[160,128]{1,0:T(8,128)S(1)} %add.60), channel_id=1, source_target_pairs={{0,16},{2,18},{4,20},{6,22},{8,24},{10,26},{12,28},{14,30},{16,0},... | collective-permute-start | bytes 245768 | tf_op jit(solution)/shard_map/ppermute | solution.py:36
  58.4 4.5 %collective-permute-start.6 = (f32[160,128]{1,0:T(8,128)S(1)}, f32[160,128]{1,0:T(8,128)S(1)}, u32[]{:S(2)}, u32[]{:S(2)}) collective-permute-start(f32[160,128]{1,0:T(8,128)S(1)} %get-tuple-element.4), channel_id=1, source_target_pairs={{0,2},{2,0},{4,6},{6,4},{8,10},{10,8},{12,14},{14,12},{16,18},{18,... | collective-permute-start | bytes 245768 | tf_op jit(solution)/shard_map/ppermute | solution.py:36
  59.2 4.4 %collective-permute-start.7 = (f32[160,128]{1,0:T(8,128)S(1)}, f32[160,128]{1,0:T(8,128)S(1)}, u32[]{:S(2)}, u32[]{:S(2)}) collective-permute-start(f32[160,128]{1,0:T(8,128)S(1)} %get-tuple-element.4), channel_id=1, source_target_pairs={{0,4},{2,6},{4,0},{6,2},{8,12},{10,14},{12,8},{14,10},{16,20},{18,... | collective-permute-start | bytes 245768 | tf_op jit(solution)/shard_map/ppermute | solution.py:36
  60.0 5.3 %collective-permute-start.8 = (f32[160,128]{1,0:T(8,128)S(1)}, f32[160,128]{1,0:T(8,128)S(1)}, u32[]{:S(2)}, u32[]{:S(2)}) collective-permute-start(f32[160,128]{1,0:T(8,128)S(1)} %get-tuple-element.4), channel_id=1, source_target_pairs={{0,6},{2,4},{4,2},{6,0},{8,14},{10,12},{12,10},{14,8},{16,22},{18,... | collective-permute-start | bytes 245768 | tf_op jit(solution)/shard_map/ppermute | solution.py:36
  65.4 1.7 %collective-permute-start.9 = (f32[640,128]{1,0:T(8,128)S(1)}, f32[640,128]{1,0:T(8,128)S(1)}, u32[]{:S(2)}, u32[]{:S(2)}) collective-permute-start(f32[640,128]{1,0:T(8,128)S(1)} %constant_dynamic-update-slice_fusion.2), channel_id=1, source_target_pairs={{0,1},{1,0},{2,3},{3,2},{4,5},{5,4},{6,7},{7,6},{8,9},{9,8},{10,11... | collective-permute-start | bytes 983048 | tf_op jit(solution)/shard_map/ppermute | solution.py:36
  65.6 1.5 %copy-start.1 = (f32[512,128]{1,0:T(8,128)S(1)}, f32[512,128]{1,0:T(8,128)}, u32[]{:S(2)}) copy-start(f32[512,128]{1,0:T(8,128)} %initial_ref.1) | copy-start | bytes 786436
  78.8 2.2 %collective-permute-start.10 = (f32[1280,128]{1,0:T(8,128)S(1)}, f32[1280,128]{1,0:T(8,128)S(1)}, u32[]{:S(2)}, u32[]{:S(2)}) collective-permute-start(f32[1280,128]{1,0:T(8,128)S(1)} %shard_map.52.outbox_ref), channel_id=1, source_target_pairs={{0,1},{1,0},{2,3},{3,2},{4,5},{5,4},{6,7},{7,6},{8,9},{9,8},{10,11... | collective-permute-start | bytes 1966088 | tf_op jit(solution)/shard_map/ppermute | solution.py:36

commit v8 on v7

--- a/solution.py
+++ b/solution.py
@@ -10,6 +10,7 @@
 ITERS = 3
 TILE = 128
 SUB = 8
+SPARE = 32
 PANEL = 2
 
 precise = lax.Precision.HIGHEST
@@ -183,9 +184,42 @@
     }
 
 
+def packing(tiles):
+    above = [(i, j) for i in range(tiles) for j in range(i + 1, tiles)]
+    doubles = [(i, i + 1) for i in range(0, tiles, 2)]
+    cut = len(doubles) // 2
+    each = (len(above) + len(doubles)) // 2
+    length = each * TILE + SPARE
+    halves = []
+    for half in range(2):
+        base = half * length
+        pairs = doubles[cut:] if half else doubles[:cut]
+        blocks = above[each - cut :] if half else above[: each - cut]
+        places = {pair: (base + TILE * n, base + each * TILE + n) for n, pair in enumerate(pairs)}
+        offsets = {pair: base + TILE * (len(pairs) + n) for n, pair in enumerate(blocks)}
+        halves.append((offsets, places, base))
+    return halves, length
+
+
+def unpacked(packed_ref, tiles):
+    row = lax.broadcasted_iota(jnp.int32, (TILE, TILE), 0)
+    lane = lax.broadcasted_iota(jnp.int32, (TILE, TILE), 1)
+    blocks = {}
+    for offsets, doubles, _ in packing(tiles)[0]:
+        for pair, at in offsets.items():
+            blocks[pair] = packed_ref[at : at + TILE, :]
+        for (i, j), (at, line) in doubles.items():
+            both = packed_ref[at : at + TILE, :]
+            turned = both.T
+            diagonal = jnp.broadcast_to(packed_ref[line : line + 1, :], (TILE, TILE))
+            blocks[i, i] = jnp.where(lane >= row, both, turned)
+            blocks[j, j] = jnp.where(lane < row, both, jnp.where(lane > row, turned, diagonal))
+    return blocks
+
+
 def write_triangle(packed_ref, outbox_ref, tiles):
     places = block_places(tiles)
-    blocks = {pair: packed_ref[TILE * at : TILE * at + TILE, :] for pair, at in places.items()}
+    blocks = unpacked(packed_ref, tiles)
     for k in range(tiles):
         blocks[k, k], inverse = factored(blocks[k, k], True)
         for j in range(k + 1, tiles):
@@ -199,8 +233,7 @@
 
 
 def write_basis(packed_ref, initial_ref, outbox_ref, gram_ref, tiles):
-    for (i, j), at in block_places(tiles).items():
-        block = packed_ref[TILE * at : TILE * at + TILE, :]
+    for (i, j), block in unpacked(packed_ref, tiles).items():
         gram_ref[TILE * i : TILE * i + TILE, TILE * j : TILE * j + TILE] = block
         if i != j:
             gram_ref[TILE * j : TILE * j + TILE, TILE * i : TILE * i + TILE] = block.T
@@ -268,6 +301,7 @@
 
 
 VMEM_LIMIT = 32 * 2**20
+WHOLE_VMEM = 63 * 2**20
 
 
 def factors(packed, initial, part):
@@ -276,7 +310,7 @@
     vmem = pl.BlockSpec(memory_space=pltpu.VMEM)
     return pl.pallas_call(
         functools.partial(factor_kernel, tiles),
-        out_shape=jax.ShapeDtypeStruct((max(packed.shape[0], rows + tiles * keep), TILE), jnp.float32),
+        out_shape=jax.ShapeDtypeStruct((max(TILE * len(block_places(tiles)), rows + tiles * keep), TILE), jnp.float32),
         in_specs=[pl.BlockSpec(memory_space=pltpu.SMEM), vmem, vmem],
         out_specs=vmem,
         scratch_shapes=[pltpu.VMEM((rows, rows), jnp.float32)],
@@ -312,58 +346,96 @@
     )(part, outbox, inbox, unfold)
 
 
-def blocks_kernel(tensor_ref, blocks_ref):
-    count, _, columns = blocks_ref.shape
-    slab_count = tensor_ref.shape[1]
+def blocks_kernel(tensor_ref, blocks_ref, read_ref, written_ref, read_done, write_done):
+    chunks, rows, slab_count, _ = read_ref.shape
+    count, columns = blocks_ref.shape[0], blocks_ref.shape[2]
     cells = columns // slab_count
-    for part in range(count):
-        for slab in range(slab_count):
-            blocks_ref[part, :, slab * cells : slab * cells + cells] = tensor_ref[
-                :, slab, part * cells : part * cells + cells
-            ]
+    spans = [pl.ds(rows * n, rows) for n in range(chunks)]
+    reads = [
+        pltpu.make_async_copy(tensor_ref.at[span], read_ref.at[n], read_done.at[n]) for n, span in enumerate(spans)
+    ]
+    writes = [
+        pltpu.make_async_copy(written_ref.at[n], blocks_ref.at[:, span, :], write_done.at[n])
+        for n, span in enumerate(spans)
+    ]
+    for read in reads:
+        read.start()
+    for n in range(chunks):
+        reads[n].wait()
+        for part in range(count):
+            for slab in range(slab_count):
+                written_ref[n, part, :, slab * cells : slab * cells + cells] = read_ref[
+                    n, :, slab, part * cells : part * cells + cells
+                ]
+        writes[n].start()
+    for write in writes:
+        write.wait()
 
 
 def blocks_of(tensor, count):
     rows, slab_count, width = tensor.shape
+    columns = slab_count * width // count
+    chunk = SUB if rows % SUB == 0 else rows
+    chunks = rows // chunk
+    hbm = pl.BlockSpec(memory_space=pltpu.HBM)
+    return pl.pallas_call(
+        blocks_kernel,
+        out_shape=jax.ShapeDtypeStruct((count, rows, columns), jnp.float32),
+        in_specs=[hbm],
+        out_specs=hbm,
+        scratch_shapes=[
+            pltpu.VMEM((chunks, chunk, slab_count, width), jnp.float32),
+            pltpu.VMEM((chunks, count, chunk, columns), jnp.float32),
+            pltpu.SemaphoreType.DMA((chunks,)),
+            pltpu.SemaphoreType.DMA((chunks,)),
+        ],
+        compiler_params=pltpu.CompilerParams(vmem_limit_bytes=WHOLE_VMEM),
+    )(tensor)
+
+
+def gram_kernel(scale, half_ref, unfold_ref, packed_ref):
+    tiles = unfold_ref.shape[0] // TILE
+    row = lax.broadcasted_iota(jnp.int32, (TILE, TILE), 0)
+    lane = lax.broadcasted_iota(jnp.int32, (TILE, TILE), 1)
+
+    def make(offsets, doubles, base):
+        wanted = set(offsets) | {(i, i) for pair in doubles for i in pair}
+        blocks = {}
+        for i in sorted({i for i, _ in wanted}):
+            columns = sorted(j for first, j in wanted if first == i)
+            left = unfold_ref[TILE * i : TILE * i + TILE, :]
+            products = matmul_nt(left, unfold_ref[TILE * columns[0] : TILE * columns[-1] + TILE, :]) * scale
+            for j in columns:
+                start = TILE * (j - columns[0])
+                blocks[i, j] = products[:, start : start + TILE]
+        for pair, at in offsets.items():
+            packed_ref[at - base : at - base + TILE, :] = blocks[pair]
+        for (i, j), (at, line) in doubles.items():
+            packed_ref[at - base : at - base + TILE, :] = jnp.where(lane >= row, blocks[i, i], blocks[j, j])
+            diagonal = jnp.sum(jnp.where(lane == row, blocks[j, j], 0.0), axis=0, keepdims=True)
+            packed_ref[line - base : line - base + 1, :] = diagonal
+
+    for half, (offsets, doubles, base) in enumerate(packing(tiles)[0]):
+
+        @pl.when(half_ref[0] == half)
+        def _(offsets=offsets, doubles=doubles, base=base):
+            lines = packed_ref.shape[0] - SPARE
+            packed_ref[lines:, :] = jnp.zeros((SPARE, TILE), jnp.float32)
+            make(offsets, doubles, base)
+
+
+def gram_blocks(unfold, scale, half):
+    rows, columns = unfold.shape
+    _, length = packing(rows // TILE)
     vmem = pl.BlockSpec(memory_space=pltpu.VMEM)
     return pl.pallas_call(
-        blocks_kernel,
-        out_shape=jax.ShapeDtypeStruct((count, rows, slab_count * width // count), jnp.float32),
-        in_specs=[vmem],
-        out_specs=vmem,
-        compiler_params=pltpu.CompilerParams(vmem_limit_bytes=VMEM_LIMIT),
-    )(tensor)
-
-
-def gram_kernel(halves, scale, half_ref, unfold_ref, blocks_ref):
-    for half, pairs in enumerate(halves):
-
-        @pl.when(half_ref[0] == half)
-        def _(pairs=pairs):
-            at = 0
-            for i in sorted({i for i, _ in pairs}):
-                columns = [j for first, j in pairs if first == i]
-                left = unfold_ref[TILE * i : TILE * i + TILE, :]
-                products = matmul_nt(left, unfold_ref[TILE * columns[0] : TILE * columns[-1] + TILE, :]) * scale
-                for n in range(len(columns)):
-                    blocks_ref[TILE * at : TILE * at + TILE, :] = products[:, TILE * n : TILE * n + TILE]
-                    at += 1
-
-
-def gram_blocks(unfold, scale, half, halves):
-    rows, columns = unfold.shape
-    pairs = list(block_places(rows // TILE))
-    each = len(pairs) // halves
-    parts = [pairs[each * n : each * n + each] for n in range(halves)]
-    vmem = pl.BlockSpec(memory_space=pltpu.VMEM)
-    return pl.pallas_call(
-        functools.partial(gram_kernel, parts, scale),
-        out_shape=jax.ShapeDtypeStruct((each * TILE, TILE), jnp.float32),
+        functools.partial(gram_kernel, scale),
+        out_shape=jax.ShapeDtypeStruct((length, TILE), jnp.float32),
         in_specs=[pl.BlockSpec(memory_space=pltpu.SMEM), vmem],
         out_specs=vmem,
         compiler_params=pltpu.CompilerParams(vmem_limit_bytes=VMEM_LIMIT),
         cost_estimate=pl.CostEstimate(
-            flops=2 * each * TILE * TILE * columns, bytes_accessed=4 * rows * columns, transcendentals=0
+            flops=2 * length * TILE * columns, bytes_accessed=4 * rows * columns, transcendentals=0
         ),
     )(jnp.full((1,), half, jnp.int32), unfold)
 
@@ -376,12 +448,12 @@
     regrouped = lax.all_to_all(blocks_of(tensor, mode_size), "mode", split_axis=0, concat_axis=0, tiled=True)
     unfold = regrouped.reshape(row_count, slab_count * width // mode_size)
     scale = 1.0 / column_total
-    if lax.axis_size("col") % 2 or len(block_places(row_count // TILE)) % 2:
-        packed = summed(gram_blocks(unfold, scale, jnp.int32(0), 1))
+    if lax.axis_size("col") % 2:
+        packed = summed(jnp.concatenate([gram_blocks(unfold, scale, half) for half in range(2)]))
     else:
         half = lax.axis_index("col") % 2
-        other = gram_blocks(unfold, scale, 1 - half, 2)
-        packed = summed(gram_blocks(unfold, scale, half, 2), other)
+        other = gram_blocks(unfold, scale, 1 - half)
+        packed = summed(gram_blocks(unfold, scale, half), other)
     return finished(packed, initial, unfold, slab_count)
 
 

time: 83.3 us -> 81.9 us (0.983)
  local copies, waits for them, and re-layouts: 1.4 us -> 0.16 us
  waiting for transfers between devices: 43.6 us -> 42.6 us
    unnamed x4 -> x2, local copies, waits for them, and re-layouts: 1.22 us -> 0.01 us
    ppermute x11, waiting for transfers between devices: 19.2 us -> 18.2 us  [exchanged(): return lax.ppermute(value, axis, pairs)]
where the time goes in v8:
time: 81.9 us; the launch traced here: 81.7 us
  waiting for transfers between devices  42.6 us (52%)
  starting transfers between devices  19.4 us (24%)
  Pallas kernels  18.4 us (22%)
  between operations  1.01 us (1%)
    all_to_all x1, waiting for transfers between devices, local(): lax.all_to_all(blocks_of(tensor, mode_size), 'mode', split_axis=0, concat...  24.4 us
    ppermute x11, waiting for transfers between devices, exchanged(): return lax.ppermute(value, axis, pairs)  18.2 us
    pallas_call x1, Pallas kernels, factors(): pl.pallas_call(functools.partial(factor_kernel, tiles), out_shape=jax.Sha...  11.8 us
    ppermute x11, starting transfers between devices, exchanged(): return lax.ppermute(value, axis, pairs)  11.1 us
    all_to_all x1, starting transfers between devices, local(): lax.all_to_all(blocks_of(tensor, mode_size), 'mode', split_axis=0, concat...  8.32 us
    pallas_call x2, Pallas kernels, gram_blocks(): pl.pallas_call(functools.partial(gram_kernel, scale), out_shape=jax.Shape...  2.7 us
    pallas_call x1, Pallas kernels, blocks_of(): pl.pallas_call(blocks_kernel, out_shape=jax.ShapeDtypeStruct((count, rows...  2.07 us
    pallas_call x1, Pallas kernels, finished(): pl.pallas_call(functools.partial(closing_kernel, rows // TILE), out_shape...  1.89 us
  transfers between devices with their start and end apart: 12, of which 12 were waited for; matrix products, arithmetic and copies ran while one was open for 0% of the time, Pallas kernels for 2%

profile of v8, /device:TPU:0, one launch (start us, length us, event | category | flops | bytes accessed | tf_op | source)
XLA Modules:
  0.0 81.7 jit_solution(1116285823277812749)
XLA Ops:
  0.6 2.1 %shard_map.49 = f32[16,32,512]{2,1,0:T(8,128)} custom-call(f32[32,2,4096]{2,1,0:T(2,128)} %tensor_ref.1), custom_call_target="tpu_custom_call" | custom-call | tf_op jit(solution)/shard_map/pallas_call | solution.py:381
  2.7 8.3 %all-to-all-start = ((f32[16,32,512]{2,1,0:T(8,128)}), f32[16,32,512]{2,1,0:T(8,128)S(1)}, u32[]{:S(2)}, u32[]{:S(2)}) async-start(f32[16,32,512]{2,1,0:T(8,128)} %shard_map.49), calls=%async_computation | async-start | bytes 2097152 | tf_op jit(solution)/shard_map/all_to_all | solution.py:448
  11.1 24.4 %all-to-all-done = f32[16,32,512]{2,1,0:T(8,128)S(1)} async-done(((f32[16,32,512]{2,1,0:T(8,128)}), f32[16,32,512]{2,1,0:T(8,128)S(1)}, u32[]{:S(2)}, u32[]{:S(2)}) %all-to-all-start) | async-done | bytes 1048608 | tf_op jit(solution)/shard_map/all_to_all | solution.py:448
  35.5 1.3 %shard_map.51 = f32[544,128]{1,0:T(8,128)S(1)} custom-call(s32[1]{0:T(128)} %bitcast.2.half_ref, f32[512,512]{1,0:T(8,128)S(1)} %bitcast.3), custom_call_target="tpu_custom_call" | custom-call | flops 71303168 | bytes 1048576 | tf_op jit(solution)/shard_map/pallas_call | solution.py:431
  36.8 0.1 collective-permute-start
  36.9 1.4 %shard_map.50 = f32[544,128]{1,0:T(8,128)S(1)} custom-call(s32[1]{0:T(128)} %bitcast.half_ref.part_ref, f32[512,512]{1,0:T(8,128)S(1)} %bitcast.4), custom_call_target="tpu_custom_call" | custom-call | flops 71303168 | bytes 1048576 | tf_op jit(solution)/shard_map/pallas_call | solution.py:431
  38.3 0.1 collective-permute-done
  38.5 0.6 collective-permute-start.1
  39.1 2.9 %collective-permute-start.3 = (f32[136,128]{1,0:T(8,128)S(1)}, f32[136,128]{1,0:T(8,128)S(1)}, u32[]{:S(2)}, u32[]{:S(2)}) collective-permute-start(f32[136,128]{1,0:T(8,128)S(1)} %get-tuple-element.6), channel_id=1, source_target_pairs={{0,6},{2,4},{4,2},{6,0},{8,14},{10,12},{12,10},{14,8},{16,22},{18,... | collective-permute-start | bytes 208904 | tf_op jit(solution)/shard_map/ppermute | solution.py:37
  42.0 0.1 collective-permute-start.2
  42.1 0.9 %collective-permute-done.1 = f32[136,128]{1,0:T(8,128)S(1)} collective-permute-done((f32[136,128]{1,0:T(8,128)S(1)}, f32[136,128]{1,0:T(8,128)S(1)}, u32[]{:S(2)}, u32[]{:S(2)}) %collective-permute-start.1) | collective-permute-done | bytes 69664 | tf_op jit(solution)/shard_map/ppermute | solution.py:37
  43.0 3.0 %collective-permute-done.3 = f32[136,128]{1,0:T(8,128)S(1)} collective-permute-done((f32[136,128]{1,0:T(8,128)S(1)}, f32[136,128]{1,0:T(8,128)S(1)}, u32[]{:S(2)}, u32[]{:S(2)}) %collective-permute-start.3) | collective-permute-done | bytes 69664 | tf_op jit(solution)/shard_map/ppermute | solution.py:37
  46.0 1.1 %collective-permute-done.2 = f32[136,128]{1,0:T(8,128)S(1)} collective-permute-done((f32[136,128]{1,0:T(8,128)S(1)}, f32[136,128]{1,0:T(8,128)S(1)}, u32[]{:S(2)}, u32[]{:S(2)}) %collective-permute-start.2) | collective-permute-done | bytes 69664 | tf_op jit(solution)/shard_map/ppermute | solution.py:37
  47.1 2.4 %collective-permute-start.4 = (f32[136,128]{1,0:T(8,128)S(1)}, f32[136,128]{1,0:T(8,128)S(1)}, u32[]{:S(2)}, u32[]{:S(2)}) collective-permute-start(f32[136,128]{1,0:T(8,128)S(1)} %add_add_fusion), channel_id=1, source_target_pairs={{0,8},{2,10},{4,12},{6,14},{8,0},{10,2},{12,4},{14,6},{16,24},{18,... | collective-permute-start | bytes 208904 | tf_op jit(solution)/shard_map/ppermute | solution.py:37
  49.5 2.3 %collective-permute-done.4 = f32[136,128]{1,0:T(8,128)S(1)} collective-permute-done((f32[136,128]{1,0:T(8,128)S(1)}, f32[136,128]{1,0:T(8,128)S(1)}, u32[]{:S(2)}, u32[]{:S(2)}) %collective-permute-start.4) | collective-permute-done | bytes 69664 | tf_op jit(solution)/shard_map/ppermute | solution.py:37
  51.8 1.4 %collective-permute-start.5 = (f32[136,128]{1,0:T(8,128)S(1)}, f32[136,128]{1,0:T(8,128)S(1)}, u32[]{:S(2)}, u32[]{:S(2)}) collective-permute-start(f32[136,128]{1,0:T(8,128)S(1)} %add.60), channel_id=1, source_target_pairs={{0,16},{2,18},{4,20},{6,22},{8,24},{10,26},{12,28},{14,30},{16,0},... | collective-permute-start | bytes 208904 | tf_op jit(solution)/shard_map/ppermute | solution.py:37
  53.1 3.9 %collective-permute-done.5 = f32[136,128]{1,0:T(8,128)S(1)} collective-permute-done((f32[136,128]{1,0:T(8,128)S(1)}, f32[136,128]{1,0:T(8,128)S(1)}, u32[]{:S(2)}, u32[]{:S(2)}) %collective-permute-start.5) | collective-permute-done | bytes 69664 | tf_op jit(solution)/shard_map/ppermute | solution.py:37
  57.1 0.9 %collective-permute-start.6 = (f32[136,128]{1,0:T(8,128)S(1)}, f32[136,128]{1,0:T(8,128)S(1)}, u32[]{:S(2)}, u32[]{:S(2)}) collective-permute-start(f32[136,128]{1,0:T(8,128)S(1)} %get-tuple-element.4), channel_id=1, source_target_pairs={{0,2},{2,0},{4,6},{6,4},{8,10},{10,8},{12,14},{14,12},{16,18},{18,... | collective-permute-start | bytes 208904 | tf_op jit(solution)/shard_map/ppermute | solution.py:37
  57.9 0.8 %collective-permute-start.7 = (f32[136,128]{1,0:T(8,128)S(1)}, f32[136,128]{1,0:T(8,128)S(1)}, u32[]{:S(2)}, u32[]{:S(2)}) collective-permute-start(f32[136,128]{1,0:T(8,128)S(1)} %get-tuple-element.4), channel_id=1, source_target_pairs={{0,4},{2,6},{4,0},{6,2},{8,12},{10,14},{12,8},{14,10},{16,20},{18,... | collective-permute-start | bytes 208904 | tf_op jit(solution)/shard_map/ppermute | solution.py:37
  58.8 1.9 %collective-permute-start.8 = (f32[136,128]{1,0:T(8,128)S(1)}, f32[136,128]{1,0:T(8,128)S(1)}, u32[]{:S(2)}, u32[]{:S(2)}) collective-permute-start(f32[136,128]{1,0:T(8,128)S(1)} %get-tuple-element.4), channel_id=1, source_target_pairs={{0,6},{2,4},{4,2},{6,0},{8,14},{10,12},{12,10},{14,8},{16,22},{18,... | collective-permute-start | bytes 208904 | tf_op jit(solution)/shard_map/ppermute | solution.py:37
  60.6 0.8 %collective-permute-done.6 = f32[136,128]{1,0:T(8,128)S(1)} collective-permute-done((f32[136,128]{1,0:T(8,128)S(1)}, f32[136,128]{1,0:T(8,128)S(1)}, u32[]{:S(2)}, u32[]{:S(2)}) %collective-permute-start.6) | collective-permute-done | bytes 69664 | tf_op jit(solution)/shard_map/ppermute | solution.py:37
  61.5 0.8 collective-permute-done.7
  62.3 1.7 %collective-permute-done.8 = f32[136,128]{1,0:T(8,128)S(1)} collective-permute-done((f32[136,128]{1,0:T(8,128)S(1)}, f32[136,128]{1,0:T(8,128)S(1)}, u32[]{:S(2)}, u32[]{:S(2)}) %collective-permute-start.8) | collective-permute-done | bytes 69664 | tf_op jit(solution)/shard_map/ppermute | solution.py:37
  64.0 0.1 collective-permute-start.9
  64.2 0.0 copy-start
  64.2 1.4 %collective-permute-done.9 = f32[544,128]{1,0:T(8,128)S(1)} collective-permute-done((f32[544,128]{1,0:T(8,128)S(1)}, f32[544,128]{1,0:T(8,128)S(1)}, u32[]{:S(2)}, u32[]{:S(2)}) %collective-permute-start.9) | collective-permute-done | bytes 278560 | tf_op jit(solution)/shard_map/ppermute | solution.py:37
  65.6 0.0 copy-done
  65.6 11.8 %shard_map.52.outbox_ref = f32[1280,128]{1,0:T(8,128)S(1)} custom-call(s32[1]{0:T(128)} %bitcast.half_ref.part_ref, f32[1088,128]{1,0:T(8,128)S(1)} %constant_dynamic-update-slice_fusion.packed_ref, f32[512,128]{1,0:T(8,128)S(1)} %copy-done), custom_call_target="tpu_custom_call" | custom-call | tf_op jit(solution)/shard_map/pallas_call | solution.py:311
  77.4 0.1 collective-permute-start.10
  77.5 2.1 %collective-permute-done.10.inbox_ref = f32[1280,128]{1,0:T(8,128)S(1)} collective-permute-done((f32[1280,128]{1,0:T(8,128)S(1)}, f32[1280,128]{1,0:T(8,128)S(1)}, u32[]{:S(2)}, u32[]{:S(2)}) %collective-permute-start.10) | collective-permute-done | bytes 655392 | tf_op jit(solution)/shard_map/ppermute | solution.py:37
  79.6 1.9 %shard_map.53 = (f32[128,2,256]{2,1,0:T(2,128)}, f32[512,128]{1,0:T(8,128)}, f32[512,512]{1,0:T(8,128)}) custom-call(s32[1]{0:T(128)} %bitcast.half_ref.part_ref, f32[1280,128]{1,0:T(8,128)S(1)} %shard_map.52.outbox_ref, f32[1280,128]{1,0:T(8,128)S(1)} %collective-permute-done.10.inbox_ref, f32[512,512]{1,0:T(8,128)S(1)} %bitcast.5), custom_call_target="tpu_custom_call" | custom-call | tf_op jit(solution)/shard_map/pallas_call | solution.py:332
  (12 shorter events, 0.2 us)
Async XLA Ops:
  2.7 32.8 %all-to-all-start = ((f32[16,32,512]{2,1,0:T(8,128)}), f32[16,32,512]{2,1,0:T(8,128)S(1)}, u32[]{:S(2)}, u32[]{:S(2)}) async-start(f32[16,32,512]{2,1,0:T(8,128)} %shard_map.49), calls=%async_computation | async-start | bytes 2097152 | tf_op jit(solution)/shard_map/all_to_all | solution.py:448
  36.8 1.6 %collective-permute-start = (f32[544,128]{1,0:T(8,128)S(1)}, f32[544,128]{1,0:T(8,128)S(1)}, u32[]{:S(2)}, u32[]{:S(2)}) collective-permute-start(f32[544,128]{1,0:T(8,128)S(1)} %shard_map.51), channel_id=1, source_target_pairs={{0,1},{1,0},{2,3},{3,2},{4,5},{5,4},{6,7},{7,6},{8,9},{9,8},{10,11... | collective-permute-start | bytes 835592 | tf_op jit(solution)/shard_map/ppermute | solution.py:37
  38.5 4.5 %collective-permute-start.1 = (f32[136,128]{1,0:T(8,128)S(1)}, f32[136,128]{1,0:T(8,128)S(1)}, u32[]{:S(2)}, u32[]{:S(2)}) collective-permute-start(f32[136,128]{1,0:T(8,128)S(1)} %get-tuple-element.5), channel_id=1, source_target_pairs={{0,2},{2,0},{4,6},{6,4},{8,10},{10,8},{12,14},{14,12},{16,18},{18,... | collective-permute-start | bytes 208904 | tf_op jit(solution)/shard_map/ppermute | solution.py:37
  39.1 6.8 %collective-permute-start.3 = (f32[136,128]{1,0:T(8,128)S(1)}, f32[136,128]{1,0:T(8,128)S(1)}, u32[]{:S(2)}, u32[]{:S(2)}) collective-permute-start(f32[136,128]{1,0:T(8,128)S(1)} %get-tuple-element.6), channel_id=1, source_target_pairs={{0,6},{2,4},{4,2},{6,0},{8,14},{10,12},{12,10},{14,8},{16,22},{18,... | collective-permute-start | bytes 208904 | tf_op jit(solution)/shard_map/ppermute | solution.py:37
  42.0 5.0 %collective-permute-start.2 = (f32[136,128]{1,0:T(8,128)S(1)}, f32[136,128]{1,0:T(8,128)S(1)}, u32[]{:S(2)}, u32[]{:S(2)}) collective-permute-start(f32[136,128]{1,0:T(8,128)S(1)} %get-tuple-element.7), channel_id=1, source_target_pairs={{0,4},{2,6},{4,0},{6,2},{8,12},{10,14},{12,8},{14,10},{16,20},{18,... | collective-permute-start | bytes 208904 | tf_op jit(solution)/shard_map/ppermute | solution.py:37
  47.1 4.7 %collective-permute-start.4 = (f32[136,128]{1,0:T(8,128)S(1)}, f32[136,128]{1,0:T(8,128)S(1)}, u32[]{:S(2)}, u32[]{:S(2)}) collective-permute-start(f32[136,128]{1,0:T(8,128)S(1)} %add_add_fusion), channel_id=1, source_target_pairs={{0,8},{2,10},{4,12},{6,14},{8,0},{10,2},{12,4},{14,6},{16,24},{18,... | collective-permute-start | bytes 208904 | tf_op jit(solution)/shard_map/ppermute | solution.py:37
  51.8 5.3 %collective-permute-start.5 = (f32[136,128]{1,0:T(8,128)S(1)}, f32[136,128]{1,0:T(8,128)S(1)}, u32[]{:S(2)}, u32[]{:S(2)}) collective-permute-start(f32[136,128]{1,0:T(8,128)S(1)} %add.60), channel_id=1, source_target_pairs={{0,16},{2,18},{4,20},{6,22},{8,24},{10,26},{12,28},{14,30},{16,0},... | collective-permute-start | bytes 208904 | tf_op jit(solution)/shard_map/ppermute | solution.py:37
  57.1 4.4 %collective-permute-start.6 = (f32[136,128]{1,0:T(8,128)S(1)}, f32[136,128]{1,0:T(8,128)S(1)}, u32[]{:S(2)}, u32[]{:S(2)}) collective-permute-start(f32[136,128]{1,0:T(8,128)S(1)} %get-tuple-element.4), channel_id=1, source_target_pairs={{0,2},{2,0},{4,6},{6,4},{8,10},{10,8},{12,14},{14,12},{16,18},{18,... | collective-permute-start | bytes 208904 | tf_op jit(solution)/shard_map/ppermute | solution.py:37
  57.9 4.3 %collective-permute-start.7 = (f32[136,128]{1,0:T(8,128)S(1)}, f32[136,128]{1,0:T(8,128)S(1)}, u32[]{:S(2)}, u32[]{:S(2)}) collective-permute-start(f32[136,128]{1,0:T(8,128)S(1)} %get-tuple-element.4), channel_id=1, source_target_pairs={{0,4},{2,6},{4,0},{6,2},{8,12},{10,14},{12,8},{14,10},{16,20},{18,... | collective-permute-start | bytes 208904 | tf_op jit(solution)/shard_map/ppermute | solution.py:37
  58.8 5.2 %collective-permute-start.8 = (f32[136,128]{1,0:T(8,128)S(1)}, f32[136,128]{1,0:T(8,128)S(1)}, u32[]{:S(2)}, u32[]{:S(2)}) collective-permute-start(f32[136,128]{1,0:T(8,128)S(1)} %get-tuple-element.4), channel_id=1, source_target_pairs={{0,6},{2,4},{4,2},{6,0},{8,14},{10,12},{12,10},{14,8},{16,22},{18,... | collective-permute-start | bytes 208904 | tf_op jit(solution)/shard_map/ppermute | solution.py:37
  64.0 1.6 %collective-permute-start.9 = (f32[544,128]{1,0:T(8,128)S(1)}, f32[544,128]{1,0:T(8,128)S(1)}, u32[]{:S(2)}, u32[]{:S(2)}) collective-permute-start(f32[544,128]{1,0:T(8,128)S(1)} %constant_dynamic-update-slice_fusion.2), channel_id=1, source_target_pairs={{0,1},{1,0},{2,3},{3,2},{4,5},{5,4},{6,7},{7,6},{8,9},{9,8},{10,11... | collective-permute-start | bytes 835592 | tf_op jit(solution)/shard_map/ppermute | solution.py:37
  64.2 1.5 %copy-start = (f32[512,128]{1,0:T(8,128)S(1)}, f32[512,128]{1,0:T(8,128)}, u32[]{:S(2)}) copy-start(f32[512,128]{1,0:T(8,128)} %initial_ref.1) | copy-start | bytes 786436
  77.4 2.2 %collective-permute-start.10 = (f32[1280,128]{1,0:T(8,128)S(1)}, f32[1280,128]{1,0:T(8,128)S(1)}, u32[]{:S(2)}, u32[]{:S(2)}) collective-permute-start(f32[1280,128]{1,0:T(8,128)S(1)} %shard_map.52.outbox_ref), channel_id=1, source_target_pairs={{0,1},{1,0},{2,3},{3,2},{4,5},{5,4},{6,7},{7,6},{8,9},{9,8},{10,11... | collective-permute-start | bytes 1966088 | tf_op jit(solution)/shard_map/ppermute | solution.py:37

commit v9 on v8

--- a/solution.py
+++ b/solution.py
@@ -43,7 +43,7 @@
     total = lax.dynamic_slice_in_dim(value, place * rows, rows)
     parts = [
         exchanged(lax.dynamic_slice_in_dim(value, (place ^ distance) * rows, rows), axis, distance)
-        for distance in range(1, group)
+        for distance in reversed(range(1, group))
     ]
     for part in parts:
         total = total + part
@@ -55,7 +55,7 @@
     rows = value.shape[0]
     whole = jnp.zeros((group * rows,) + value.shape[1:], value.dtype)
     whole = lax.dynamic_update_slice_in_dim(whole, value, place * rows, 0)
-    for distance in range(1, group):
+    for distance in reversed(range(1, group)):
         part = exchanged(value, axis, distance)
         whole = lax.dynamic_update_slice_in_dim(whole, part, (place ^ distance) * rows, 0)
     return whole

time: 81.9 us -> 80.7 us (0.985)
  waiting for transfers between devices: 42.6 us -> 41.2 us
    ppermute x11, waiting for transfers between devices: 18.2 us -> 16.8 us  [exchanged(): return lax.ppermute(value, axis, pairs)]
where the time goes in v9:
time: 80.7 us; the launch traced here: 80.4 us
  waiting for transfers between devices  41.2 us (51%)
  starting transfers between devices  19.5 us (24%)
  Pallas kernels  18.4 us (23%)
  between operations  1.01 us (1%)
    all_to_all x1, waiting for transfers between devices, local(): lax.all_to_all(blocks_of(tensor, mode_size), 'mode', split_axis=0, concat...  24.4 us
    ppermute x11, waiting for transfers between devices, exchanged(): return lax.ppermute(value, axis, pairs)  16.8 us
    pallas_call x1, Pallas kernels, factors(): pl.pallas_call(functools.partial(factor_kernel, tiles), out_shape=jax.Sha...  11.8 us
    ppermute x11, starting transfers between devices, exchanged(): return lax.ppermute(value, axis, pairs)  11.2 us
    all_to_all x1, starting transfers between devices, local(): lax.all_to_all(blocks_of(tensor, mode_size), 'mode', split_axis=0, concat...  8.32 us
    pallas_call x2, Pallas kernels, gram_blocks(): pl.pallas_call(functools.partial(gram_kernel, scale), out_shape=jax.Shape...  2.7 us
    pallas_call x1, Pallas kernels, blocks_of(): pl.pallas_call(blocks_kernel, out_shape=jax.ShapeDtypeStruct((count, rows...  2.07 us
    pallas_call x1, Pallas kernels, finished(): pl.pallas_call(functools.partial(closing_kernel, rows // TILE), out_shape...  1.89 us
  transfers between devices with their start and end apart: 12, of which 12 were waited for; matrix products, arithmetic and copies ran while one was open for 0% of the time, Pallas kernels for 2%

profile of v9, /device:TPU:0, one launch (start us, length us, event | category | flops | bytes accessed | tf_op | source)
XLA Modules:
  0.0 80.4 jit_solution(13276502043074361090)
XLA Ops:
  0.6 2.1 %shard_map.49 = f32[16,32,512]{2,1,0:T(8,128)} custom-call(f32[32,2,4096]{2,1,0:T(2,128)} %tensor_ref.1), custom_call_target="tpu_custom_call" | custom-call | tf_op jit(solution)/shard_map/pallas_call | solution.py:381
  2.7 8.3 %all-to-all-start = ((f32[16,32,512]{2,1,0:T(8,128)}), f32[16,32,512]{2,1,0:T(8,128)S(1)}, u32[]{:S(2)}, u32[]{:S(2)}) async-start(f32[16,32,512]{2,1,0:T(8,128)} %shard_map.49), calls=%async_computation | async-start | bytes 2097152 | tf_op jit(solution)/shard_map/all_to_all | solution.py:448
  11.1 24.4 %all-to-all-done = f32[16,32,512]{2,1,0:T(8,128)S(1)} async-done(((f32[16,32,512]{2,1,0:T(8,128)}), f32[16,32,512]{2,1,0:T(8,128)S(1)}, u32[]{:S(2)}, u32[]{:S(2)}) %all-to-all-start) | async-done | bytes 1048608 | tf_op jit(solution)/shard_map/all_to_all | solution.py:448
  35.5 1.3 %shard_map.51 = f32[544,128]{1,0:T(8,128)S(1)} custom-call(s32[1]{0:T(128)} %bitcast.2.half_ref, f32[512,512]{1,0:T(8,128)S(1)} %bitcast.3), custom_call_target="tpu_custom_call" | custom-call | flops 71303168 | bytes 1048576 | tf_op jit(solution)/shard_map/pallas_call | solution.py:431
  36.8 0.1 collective-permute-start
  36.9 1.4 %shard_map.50 = f32[544,128]{1,0:T(8,128)S(1)} custom-call(s32[1]{0:T(128)} %bitcast.half_ref.part_ref, f32[512,512]{1,0:T(8,128)S(1)} %bitcast.4), custom_call_target="tpu_custom_call" | custom-call | flops 71303168 | bytes 1048576 | tf_op jit(solution)/shard_map/pallas_call | solution.py:431
  38.3 0.1 collective-permute-done
  38.5 2.0 %collective-permute-start.1 = (f32[136,128]{1,0:T(8,128)S(1)}, f32[136,128]{1,0:T(8,128)S(1)}, u32[]{:S(2)}, u32[]{:S(2)}) collective-permute-start(f32[136,128]{1,0:T(8,128)S(1)} %get-tuple-element.5), channel_id=1, source_target_pairs={{0,6},{2,4},{4,2},{6,0},{8,14},{10,12},{12,10},{14,8},{16,22},{18,... | collective-permute-start | bytes 208904 | tf_op jit(solution)/shard_map/ppermute | solution.py:37
  40.5 1.5 %collective-permute-start.3 = (f32[136,128]{1,0:T(8,128)S(1)}, f32[136,128]{1,0:T(8,128)S(1)}, u32[]{:S(2)}, u32[]{:S(2)}) collective-permute-start(f32[136,128]{1,0:T(8,128)S(1)} %get-tuple-element.6), channel_id=1, source_target_pairs={{0,2},{2,0},{4,6},{6,4},{8,10},{10,8},{12,14},{14,12},{16,18},{18,... | collective-permute-start | bytes 208904 | tf_op jit(solution)/shard_map/ppermute | solution.py:37
  42.0 0.1 collective-permute-start.2
  42.1 2.4 %collective-permute-done.1 = f32[136,128]{1,0:T(8,128)S(1)} collective-permute-done((f32[136,128]{1,0:T(8,128)S(1)}, f32[136,128]{1,0:T(8,128)S(1)}, u32[]{:S(2)}, u32[]{:S(2)}) %collective-permute-start.1) | collective-permute-done | bytes 69664 | tf_op jit(solution)/shard_map/ppermute | solution.py:37
  44.5 1.4 %collective-permute-done.3 = f32[136,128]{1,0:T(8,128)S(1)} collective-permute-done((f32[136,128]{1,0:T(8,128)S(1)}, f32[136,128]{1,0:T(8,128)S(1)}, u32[]{:S(2)}, u32[]{:S(2)}) %collective-permute-start.3) | collective-permute-done | bytes 69664 | tf_op jit(solution)/shard_map/ppermute | solution.py:37
  45.9 0.4 collective-permute-done.2
  46.3 2.4 %collective-permute-start.4 = (f32[136,128]{1,0:T(8,128)S(1)}, f32[136,128]{1,0:T(8,128)S(1)}, u32[]{:S(2)}, u32[]{:S(2)}) collective-permute-start(f32[136,128]{1,0:T(8,128)S(1)} %add_add_fusion), channel_id=1, source_target_pairs={{0,8},{2,10},{4,12},{6,14},{8,0},{10,2},{12,4},{14,6},{16,24},{18,... | collective-permute-start | bytes 208904 | tf_op jit(solution)/shard_map/ppermute | solution.py:37
  48.7 2.3 %collective-permute-done.4 = f32[136,128]{1,0:T(8,128)S(1)} collective-permute-done((f32[136,128]{1,0:T(8,128)S(1)}, f32[136,128]{1,0:T(8,128)S(1)}, u32[]{:S(2)}, u32[]{:S(2)}) %collective-permute-start.4) | collective-permute-done | bytes 69664 | tf_op jit(solution)/shard_map/ppermute | solution.py:37
  51.0 1.5 %collective-permute-start.5 = (f32[136,128]{1,0:T(8,128)S(1)}, f32[136,128]{1,0:T(8,128)S(1)}, u32[]{:S(2)}, u32[]{:S(2)}) collective-permute-start(f32[136,128]{1,0:T(8,128)S(1)} %add.60), channel_id=1, source_target_pairs={{0,16},{2,18},{4,20},{6,22},{8,24},{10,26},{12,28},{14,30},{16,0},... | collective-permute-start | bytes 208904 | tf_op jit(solution)/shard_map/ppermute | solution.py:37
  52.5 3.8 %collective-permute-done.5 = f32[136,128]{1,0:T(8,128)S(1)} collective-permute-done((f32[136,128]{1,0:T(8,128)S(1)}, f32[136,128]{1,0:T(8,128)S(1)}, u32[]{:S(2)}, u32[]{:S(2)}) %collective-permute-start.5) | collective-permute-done | bytes 69664 | tf_op jit(solution)/shard_map/ppermute | solution.py:37
  56.4 1.1 %collective-permute-start.6 = (f32[136,128]{1,0:T(8,128)S(1)}, f32[136,128]{1,0:T(8,128)S(1)}, u32[]{:S(2)}, u32[]{:S(2)}) collective-permute-start(f32[136,128]{1,0:T(8,128)S(1)} %get-tuple-element.4), channel_id=1, source_target_pairs={{0,6},{2,4},{4,2},{6,0},{8,14},{10,12},{12,10},{14,8},{16,22},{18,... | collective-permute-start | bytes 208904 | tf_op jit(solution)/shard_map/ppermute | solution.py:37
  57.4 1.0 %collective-permute-start.7 = (f32[136,128]{1,0:T(8,128)S(1)}, f32[136,128]{1,0:T(8,128)S(1)}, u32[]{:S(2)}, u32[]{:S(2)}) collective-permute-start(f32[136,128]{1,0:T(8,128)S(1)} %get-tuple-element.4), channel_id=1, source_target_pairs={{0,4},{2,6},{4,0},{6,2},{8,12},{10,14},{12,8},{14,10},{16,20},{18,... | collective-permute-start | bytes 208904 | tf_op jit(solution)/shard_map/ppermute | solution.py:37
  58.4 1.5 %collective-permute-start.8 = (f32[136,128]{1,0:T(8,128)S(1)}, f32[136,128]{1,0:T(8,128)S(1)}, u32[]{:S(2)}, u32[]{:S(2)}) collective-permute-start(f32[136,128]{1,0:T(8,128)S(1)} %get-tuple-element.4), channel_id=1, source_target_pairs={{0,2},{2,0},{4,6},{6,4},{8,10},{10,8},{12,14},{14,12},{16,18},{18,... | collective-permute-start | bytes 208904 | tf_op jit(solution)/shard_map/ppermute | solution.py:37
  59.9 1.8 %collective-permute-done.6 = f32[136,128]{1,0:T(8,128)S(1)} collective-permute-done((f32[136,128]{1,0:T(8,128)S(1)}, f32[136,128]{1,0:T(8,128)S(1)}, u32[]{:S(2)}, u32[]{:S(2)}) %collective-permute-start.6) | collective-permute-done | bytes 69664 | tf_op jit(solution)/shard_map/ppermute | solution.py:37
  61.7 0.7 collective-permute-done.7
  62.4 0.4 collective-permute-done.8
  62.8 0.1 collective-permute-start.9
  62.9 0.0 copy-start
  62.9 1.4 %collective-permute-done.9 = f32[544,128]{1,0:T(8,128)S(1)} collective-permute-done((f32[544,128]{1,0:T(8,128)S(1)}, f32[544,128]{1,0:T(8,128)S(1)}, u32[]{:S(2)}, u32[]{:S(2)}) %collective-permute-start.9) | collective-permute-done | bytes 278560 | tf_op jit(solution)/shard_map/ppermute | solution.py:37
  64.4 0.0 copy-done
  64.4 11.8 %shard_map.52.outbox_ref = f32[1280,128]{1,0:T(8,128)S(1)} custom-call(s32[1]{0:T(128)} %bitcast.half_ref.part_ref, f32[1088,128]{1,0:T(8,128)S(1)} %constant_dynamic-update-slice_fusion.packed_ref, f32[512,128]{1,0:T(8,128)S(1)} %copy-done), custom_call_target="tpu_custom_call" | custom-call | tf_op jit(solution)/shard_map/pallas_call | solution.py:311
  76.2 0.1 collective-permute-start.10
  76.3 2.1 %collective-permute-done.10.inbox_ref = f32[1280,128]{1,0:T(8,128)S(1)} collective-permute-done((f32[1280,128]{1,0:T(8,128)S(1)}, f32[1280,128]{1,0:T(8,128)S(1)}, u32[]{:S(2)}, u32[]{:S(2)}) %collective-permute-start.10) | collective-permute-done | bytes 655392 | tf_op jit(solution)/shard_map/ppermute | solution.py:37
  78.4 1.9 %shard_map.53 = (f32[128,2,256]{2,1,0:T(2,128)}, f32[512,128]{1,0:T(8,128)}, f32[512,512]{1,0:T(8,128)}) custom-call(s32[1]{0:T(128)} %bitcast.half_ref.part_ref, f32[1280,128]{1,0:T(8,128)S(1)} %shard_map.52.outbox_ref, f32[1280,128]{1,0:T(8,128)S(1)} %collective-permute-done.10.inbox_ref, f32[512,512]{1,0:T(8,128)S(1)} %bitcast.5), custom_call_target="tpu_custom_call" | custom-call | tf_op jit(solution)/shard_map/pallas_call | solution.py:332
  (12 shorter events, 0.2 us)
Async XLA Ops:
  2.7 32.8 %all-to-all-start = ((f32[16,32,512]{2,1,0:T(8,128)}), f32[16,32,512]{2,1,0:T(8,128)S(1)}, u32[]{:S(2)}, u32[]{:S(2)}) async-start(f32[16,32,512]{2,1,0:T(8,128)} %shard_map.49), calls=%async_computation | async-start | bytes 2097152 | tf_op jit(solution)/shard_map/all_to_all | solution.py:448
  36.8 1.6 %collective-permute-start = (f32[544,128]{1,0:T(8,128)S(1)}, f32[544,128]{1,0:T(8,128)S(1)}, u32[]{:S(2)}, u32[]{:S(2)}) collective-permute-start(f32[544,128]{1,0:T(8,128)S(1)} %shard_map.51), channel_id=1, source_target_pairs={{0,1},{1,0},{2,3},{3,2},{4,5},{5,4},{6,7},{7,6},{8,9},{9,8},{10,11... | collective-permute-start | bytes 835592 | tf_op jit(solution)/shard_map/ppermute | solution.py:37
  38.5 6.0 %collective-permute-start.1 = (f32[136,128]{1,0:T(8,128)S(1)}, f32[136,128]{1,0:T(8,128)S(1)}, u32[]{:S(2)}, u32[]{:S(2)}) collective-permute-start(f32[136,128]{1,0:T(8,128)S(1)} %get-tuple-element.5), channel_id=1, source_target_pairs={{0,6},{2,4},{4,2},{6,0},{8,14},{10,12},{12,10},{14,8},{16,22},{18,... | collective-permute-start | bytes 208904 | tf_op jit(solution)/shard_map/ppermute | solution.py:37
  40.5 5.3 %collective-permute-start.3 = (f32[136,128]{1,0:T(8,128)S(1)}, f32[136,128]{1,0:T(8,128)S(1)}, u32[]{:S(2)}, u32[]{:S(2)}) collective-permute-start(f32[136,128]{1,0:T(8,128)S(1)} %get-tuple-element.6), channel_id=1, source_target_pairs={{0,2},{2,0},{4,6},{6,4},{8,10},{10,8},{12,14},{14,12},{16,18},{18,... | collective-permute-start | bytes 208904 | tf_op jit(solution)/shard_map/ppermute | solution.py:37
  42.0 4.3 %collective-permute-start.2 = (f32[136,128]{1,0:T(8,128)S(1)}, f32[136,128]{1,0:T(8,128)S(1)}, u32[]{:S(2)}, u32[]{:S(2)}) collective-permute-start(f32[136,128]{1,0:T(8,128)S(1)} %get-tuple-element.7), channel_id=1, source_target_pairs={{0,4},{2,6},{4,0},{6,2},{8,12},{10,14},{12,8},{14,10},{16,20},{18,... | collective-permute-start | bytes 208904 | tf_op jit(solution)/shard_map/ppermute | solution.py:37
  46.3 4.7 %collective-permute-start.4 = (f32[136,128]{1,0:T(8,128)S(1)}, f32[136,128]{1,0:T(8,128)S(1)}, u32[]{:S(2)}, u32[]{:S(2)}) collective-permute-start(f32[136,128]{1,0:T(8,128)S(1)} %add_add_fusion), channel_id=1, source_target_pairs={{0,8},{2,10},{4,12},{6,14},{8,0},{10,2},{12,4},{14,6},{16,24},{18,... | collective-permute-start | bytes 208904 | tf_op jit(solution)/shard_map/ppermute | solution.py:37
  51.0 5.3 %collective-permute-start.5 = (f32[136,128]{1,0:T(8,128)S(1)}, f32[136,128]{1,0:T(8,128)S(1)}, u32[]{:S(2)}, u32[]{:S(2)}) collective-permute-start(f32[136,128]{1,0:T(8,128)S(1)} %add.60), channel_id=1, source_target_pairs={{0,16},{2,18},{4,20},{6,22},{8,24},{10,26},{12,28},{14,30},{16,0},... | collective-permute-start | bytes 208904 | tf_op jit(solution)/shard_map/ppermute | solution.py:37
  56.4 5.3 %collective-permute-start.6 = (f32[136,128]{1,0:T(8,128)S(1)}, f32[136,128]{1,0:T(8,128)S(1)}, u32[]{:S(2)}, u32[]{:S(2)}) collective-permute-start(f32[136,128]{1,0:T(8,128)S(1)} %get-tuple-element.4), channel_id=1, source_target_pairs={{0,6},{2,4},{4,2},{6,0},{8,14},{10,12},{12,10},{14,8},{16,22},{18,... | collective-permute-start | bytes 208904 | tf_op jit(solution)/shard_map/ppermute | solution.py:37
  57.4 4.9 %collective-permute-start.7 = (f32[136,128]{1,0:T(8,128)S(1)}, f32[136,128]{1,0:T(8,128)S(1)}, u32[]{:S(2)}, u32[]{:S(2)}) collective-permute-start(f32[136,128]{1,0:T(8,128)S(1)} %get-tuple-element.4), channel_id=1, source_target_pairs={{0,4},{2,6},{4,0},{6,2},{8,12},{10,14},{12,8},{14,10},{16,20},{18,... | collective-permute-start | bytes 208904 | tf_op jit(solution)/shard_map/ppermute | solution.py:37
  58.4 4.3 %collective-permute-start.8 = (f32[136,128]{1,0:T(8,128)S(1)}, f32[136,128]{1,0:T(8,128)S(1)}, u32[]{:S(2)}, u32[]{:S(2)}) collective-permute-start(f32[136,128]{1,0:T(8,128)S(1)} %get-tuple-element.4), channel_id=1, source_target_pairs={{0,2},{2,0},{4,6},{6,4},{8,10},{10,8},{12,14},{14,12},{16,18},{18,... | collective-permute-start | bytes 208904 | tf_op jit(solution)/shard_map/ppermute | solution.py:37
  62.8 1.6 %collective-permute-start.9 = (f32[544,128]{1,0:T(8,128)S(1)}, f32[544,128]{1,0:T(8,128)S(1)}, u32[]{:S(2)}, u32[]{:S(2)}) collective-permute-start(f32[544,128]{1,0:T(8,128)S(1)} %constant_dynamic-update-slice_fusion.2), channel_id=1, source_target_pairs={{0,1},{1,0},{2,3},{3,2},{4,5},{5,4},{6,7},{7,6},{8,9},{9,8},{10,11... | collective-permute-start | bytes 835592 | tf_op jit(solution)/shard_map/ppermute | solution.py:37
  62.9 1.5 %copy-start = (f32[512,128]{1,0:T(8,128)S(1)}, f32[512,128]{1,0:T(8,128)}, u32[]{:S(2)}) copy-start(f32[512,128]{1,0:T(8,128)} %initial_ref.1) | copy-start | bytes 786436
  76.2 2.2 %collective-permute-start.10 = (f32[1280,128]{1,0:T(8,128)S(1)}, f32[1280,128]{1,0:T(8,128)S(1)}, u32[]{:S(2)}, u32[]{:S(2)}) collective-permute-start(f32[1280,128]{1,0:T(8,128)S(1)} %shard_map.52.outbox_ref), channel_id=1, source_target_pairs={{0,1},{1,0},{2,3},{3,2},{4,5},{5,4},{6,7},{7,6},{8,9},{9,8},{10,11... | collective-permute-start | bytes 1966088 | tf_op jit(solution)/shard_map/ppermute | solution.py:37
